TPU v7x, 32 devices: a whole 2x2x4 slice. The times are simulated.
32 devices in a mesh: gx: 8 (over z, core), gy: 4 (over y, x).
Axes of the slice: x: 2, y: 2, z: 4, core: 2. Of those that a mesh axis runs over, the one named last changes fastest.
Arguments:
- positions: float32 [3, 16, 32, 128], P(None, 'gx', 'gy'), may hold values from 0 to 1
- embed: bfloat16 [16, 32, 128, 256], P('gx', 'gy'), may hold values from -0.75 to 0.75
- counts: int32 [16, 32], P('gx', 'gy'), may hold values from 0 to 128, as said below
- neighbours: int32 [16, 32, 9], P('gx', 'gy'), may hold values from 0 to 40, as said below
- w_one: bfloat16 [256, 256], replicated, may hold values from -0.375 to 0.375
- bias_one: float32 [256], replicated, may hold values from -4 to 4
- w_two: bfloat16 [256, 256], replicated, may hold values from -0.375 to 0.375
- w_out: float32 [256], replicated, may hold values from -0.375 to 0.375
Outputs:
- forces: float32 [3, 16, 32, 128], P(None, 'gx', 'gy')
- energies: float32 [16, 32, 128], P('gx', 'gy')
Inputs may be any that keep to these rules, and one draw needn't show every extreme that they name: `counts`: each device's block of 2 x 8 bins has at most 16 non-empty bins, and some devices have exactly 16. The number of non-empty bins of every device's block is a multiple of the size of gy. The blocks of all devices that share a gx index hold together at most 10 times the size of gy non-empty bins, and some such row holds exactly that many. `neighbours`: entry k of a bin at (x, y) of its device's block is 40 or (x + k // 3) * 10 + y + k % 3, the bin offset by (k // 3 - 1, k % 3 - 1) in the block extended by one ghost bin on every side; entry 4 is always present.
All inputs are finite; a program needn't handle non-finite values.
Results may differ from a plain program's by a relative error of at most 0.014.
Values may be sent and summed in bfloat16 or wider, within the bound.
No kernel may reach another device: no remote copies, remote signals or barrier semaphores. Data moves between devices by JAX's collectives and lax.ppermute only.
A program may use at most 64 MiB of HBM per device.

v0:
```python
import jax
import jax.numpy as jnp
from jax import lax
from jax.sharding import PartitionSpec as P

radius = 0.4


def padded(value, sides, width):
    for axis, dim in sides:
        count, length = (lax.axis_size(axis), value.shape[dim])
        up = [(i, (i + 1) % count) for i in range(count)]
        down = [(j, i) for i, j in up]
        last = lax.slice_in_dim(value, length - width, length, axis=dim)
        leading = lax.slice_in_dim(value, 0, width, axis=dim)
        before = lax.ppermute(last, axis, up)
        after = lax.ppermute(leading, axis, down)
        value = jnp.concatenate([before, value, after], axis=dim)
    return value


def shifted(block, axis, distance):
    devices = range(lax.axis_size(axis))
    route = [((i - distance) % len(devices), i) for i in devices]
    return lax.ppermute(block, axis, route)


def network(features, w_one, bias_one, w_two, w_out):
    flat_rows = features.reshape(-1, features.shape[-1])
    act_one = jnp.tanh(jnp.dot(flat_rows, w_one, preferred_element_type=jnp.float32) + bias_one)
    act_two = jnp.tanh(
        jnp.dot(act_one.astype(jnp.bfloat16), w_two, preferred_element_type=jnp.float32)
    )
    energy = jnp.sum(act_two * w_out, axis=-1)
    back_two = (w_out * (1.0 - act_two * act_two)).astype(jnp.bfloat16)
    back_one = (
        jnp.dot(back_two, w_two.T, preferred_element_type=jnp.float32) * (1.0 - act_one * act_one)
    ).astype(jnp.bfloat16)
    gradients = jnp.dot(back_one, w_one.T, preferred_element_type=jnp.float32).astype(jnp.bfloat16)
    return (gradients.reshape(features.shape), energy.reshape(features.shape[:-1]))


def pair_weights(own_pos, own_mask, remote_pos, remote_mask, shift_x, shift_y):
    delta_x = shift_x[:, None, None] + remote_pos[0][:, None, :] - own_pos[0][:, :, None]
    delta_y = shift_y[:, None, None] + remote_pos[1][:, None, :] - own_pos[1][:, :, None]
    delta_z = remote_pos[2][:, None, :] - own_pos[2][:, :, None]
    square = delta_x * delta_x + delta_y * delta_y + delta_z * delta_z
    weight = (
        jnp.exp(-square / (2.0 * radius * radius)) * own_mask[:, :, None] * remote_mask[:, None, :]
    )
    return (weight, delta_x, delta_y, delta_z)


def body(positions, embed, counts, neighbours, w_one, bias_one, w_two, w_out):
    per_bin = positions.shape[-1]
    rows_x, rows_y = counts.shape
    bin_count = rows_x * rows_y
    feat_width = embed.shape[-1]
    atom_index = jnp.arange(per_bin, dtype=jnp.int32)
    occupied = (atom_index[None, None, :] < counts[:, :, None]).astype(jnp.float32)
    coords = jnp.concatenate([positions, occupied[None]], axis=0)
    ext_coords = padded(coords.astype(jnp.bfloat16), (("gx", 1), ("gy", 2)), 1).astype(coords.dtype)
    ext_embed = padded(embed, (("gx", 0), ("gy", 1)), 1)
    ext_cols = rows_y + 2
    extent = (rows_x + 2) * ext_cols
    flat_coords = jnp.concatenate(
        [ext_coords.reshape(4, extent, per_bin), jnp.zeros((4, 1, per_bin), jnp.float32)], axis=1
    )
    flat_embed = jnp.concatenate(
        [
            ext_embed.reshape(extent, per_bin, feat_width),
            jnp.zeros((1, per_bin, feat_width), embed.dtype),
        ],
        axis=0,
    )
    own_pos = positions.reshape(3, bin_count, per_bin)
    own_mask = occupied.reshape(bin_count, per_bin)
    bin_index = jnp.arange(bin_count, dtype=jnp.int32)
    home_x = bin_index // rows_y
    home_y = bin_index % rows_y
    own_slot = (home_x + 1) * ext_cols + home_y + 1
    links = neighbours.reshape(bin_count, 9)

    def gather_bin(neighbour):
        linked = links[:, neighbour]
        shift_x = (linked // ext_cols - home_x - 1).astype(jnp.float32)
        shift_y = (linked % ext_cols - home_y - 1).astype(jnp.float32)
        remote = flat_coords[:, linked]
        return (remote[:3], remote[3], flat_embed[linked], shift_x, shift_y, linked)

    summed = jnp.zeros((bin_count, per_bin, feat_width), jnp.float32)
    for neighbour in range(9):
        remote_pos, remote_mask, remote_embed, shift_x, shift_y, linked = gather_bin(neighbour)
        weight, delta_x, delta_y, delta_z = pair_weights(
            own_pos, own_mask, remote_pos, remote_mask, shift_x, shift_y
        )
        summed = summed + jnp.einsum(
            "bij,bjf->bif",
            weight.astype(jnp.bfloat16),
            remote_embed,
            preferred_element_type=jnp.float32,
        )
    features = summed.astype(jnp.bfloat16)
    gradients, energy = network(features, w_one, bias_one, w_two, w_out)
    ghost_force = jnp.zeros((3, extent + 1, per_bin), jnp.float32)
    own_force = jnp.zeros((3, bin_count, per_bin), jnp.float32)
    for neighbour in range(9):
        remote_pos, remote_mask, remote_embed, shift_x, shift_y, linked = gather_bin(neighbour)
        weight, delta_x, delta_y, delta_z = pair_weights(
            own_pos, own_mask, remote_pos, remote_mask, shift_x, shift_y
        )
        projected = jnp.einsum(
            "bif,bjf->bij", gradients, remote_embed, preferred_element_type=jnp.float32
        )
        strength = projected * weight / (radius * radius)
        moved = [strength * delta_x, strength * delta_y, strength * delta_z]
        own_force = own_force - jnp.stack([jnp.sum(part, axis=2) for part in moved])
        pushed = jnp.stack([jnp.sum(part, axis=1) for part in moved])
        ghost_force = ghost_force.at[:, linked].add(pushed)
    ghost_force = ghost_force.at[:, own_slot].add(own_force)
    grid = ghost_force[:, :extent].reshape(3, rows_x + 2, ext_cols, per_bin)
    from_below = shifted(grid[:, rows_x + 1], "gx", 1)
    from_above = shifted(grid[:, 0], "gx", -1)
    middle = grid[:, 1 : rows_x + 1]
    middle = middle.at[:, 0].add(from_below).at[:, rows_x - 1].add(from_above)
    col_below = shifted(middle[:, :, ext_cols - 1], "gy", 1)
    col_above = shifted(middle[:, :, 0], "gy", -1)
    forces = middle[:, :, 1 : rows_y + 1]
    forces = forces.at[:, :, 0].add(col_below).at[:, :, rows_y - 1].add(col_above)
    return (forces, energy.reshape(rows_x, rows_y, per_bin) * occupied)


def solution(mesh):
    in_specs = (
        P(None, "gx", "gy", None),
        P("gx", "gy", None, None),
        P("gx", "gy"),
        P("gx", "gy", None),
        P(),
        P(),
        P(),
        P(),
    )
    out_specs = (P(None, "gx", "gy", None), P("gx", "gy", None))
    return jax.shard_map(body, mesh=mesh, in_specs=in_specs, out_specs=out_specs, check_vma=False)
```

profile of v0, /device:TPU:0, one launch (start us, length us, event | category | flops | bytes accessed | tf_op | source)
XLA Modules:
  0.0 155.6 jit_solution(4873265454893415354)
XLA Ops:
  2.7 4.1 %collective-permute-start.1 = (bf16[4,1,8,128]{3,2,1,0:T(8,128)(2,1)S(1)}, bf16[4,1,8,128]{3,2,1,0:T(8,128)(2,1)S(1)}, u32[]{:S(2)}, u32[]{:S(2)}) collective-permute-start(bf16[4,1,8,128]{3,2,1,0:T(8,128)(2,1)S(1)} %get-tuple-element.226), channel_id=1, source_target_pairs={{4,0},{8,4},{12,8},{16,12},{20,16},{24,20},{28,24},{0,28},{5,1},{9... | collective-permute-start | bytes 24584 | tf_op jit(solution)/shard_map/ppermute | solution.py:17
  6.8 1.3 fusion.296
  14.2 1.8 %collective-permute-start.2 = (bf16[4,4,1,128]{3,2,1,0:T(2,128)(2,1)S(1)}, bf16[4,4,1,128]{3,2,1,0:T(2,128)(2,1)S(1)}, u32[]{:S(2)}, u32[]{:S(2)}) collective-permute-start(bf16[4,4,1,128]{3,2,1,0:T(2,128)(2,1)S(1)} %get-tuple-element.218), channel_id=1, source_target_pairs={{0,1},{1,2},{2,3},{3,0},{4,5},{5,6},{6,7},{7,4},{8,9},{9,10},{10,1... | collective-permute-start | bytes 12296 | tf_op jit(solution)/shard_map/ppermute | solution.py:16
  16.0 1.2 collective-permute-start.3
  36.2 1.4 broadcast_add_fusion.13
  37.6 1.3 broadcast_add_fusion.12
  42.4 1.3 broadcast_add_fusion.5
  43.9 2.4 %collective-permute-start.6 = (bf16[4,1,128,256]{3,2,1,0:T(8,128)(2,1)S(1)}, bf16[4,1,128,256]{3,2,1,0:T(8,128)(2,1)S(1)}, u32[]{:S(2)}, u32[]{:S(2)}) collective-permute-start(bf16[4,1,128,256]{3,2,1,0:T(8,128)(2,1)S(1)} %get-tuple-element.176), channel_id=1, source_target_pairs={{0,1},{1,2},{2,3},{3,0},{4,5},{5,6},{6,7},{7,4},{8,9},{9,10},{10,1... | collective-permute-start | bytes 786440 | tf_op jit(solution)/shard_map/ppermute | solution.py:16
  47.1 7.1 %collective-permute-done.6 = bf16[4,1,128,256]{3,2,1,0:T(8,128)(2,1)S(1)} collective-permute-done((bf16[4,1,128,256]{3,2,1,0:T(8,128)(2,1)S(1)}, bf16[4,1,128,256]{3,2,1,0:T(8,128)(2,1)S(1)}, u32[]{:S(2)}, u32[]{:S(2)}) %collective-permute-start.6) | collective-permute-done | bytes 262176 | tf_op jit(solution)/shard_map/ppermute | solution.py:16
  54.1 3.5 %collective-permute-done.7 = bf16[4,1,128,256]{3,2,1,0:T(8,128)(2,1)S(1)} collective-permute-done((bf16[4,1,128,256]{3,2,1,0:T(8,128)(2,1)S(1)}, bf16[4,1,128,256]{3,2,1,0:T(8,128)(2,1)S(1)}, u32[]{:S(2)}, u32[]{:S(2)}) %collective-permute-start.7) | collective-permute-done | bytes 262176 | tf_op jit(solution)/shard_map/ppermute | solution.py:17
  58.3 1.7 %gather_fusion.17 = bf16[16,128,256]{2,1,0:T(8,128)(2,1)} fusion(bf16[41,128,256]{2,1,0:T(8,128)(2,1)S(1)} %concatenate.39, s32[1024]{0:T(1024)} %copy-done.71), kind=kCustom, calls=%fused_computation.17 | custom fusion | bytes 2097216 | tf_op jit(solution)/shard_map/gather | solution.py:89
  60.0 1.7 %gather_fusion.15 = bf16[16,128,256]{2,1,0:T(8,128)(2,1)} fusion(bf16[41,128,256]{2,1,0:T(8,128)(2,1)S(1)} %concatenate.39, s32[1024]{0:T(1024)} %pad_clamp_fusion.1), kind=kCustom, calls=%fused_computation.15 | custom fusion | bytes 2097216 | tf_op jit(solution)/shard_map/gather | solution.py:89
  61.7 1.7 %gather_fusion.13 = bf16[16,128,256]{2,1,0:T(8,128)(2,1)} fusion(bf16[41,128,256]{2,1,0:T(8,128)(2,1)S(1)} %concatenate.39, s32[1024]{0:T(1024)} %pad_clamp_fusion.2), kind=kCustom, calls=%fused_computation.13 | custom fusion | bytes 2097216 | tf_op jit(solution)/shard_map/gather | solution.py:89
  63.4 1.7 %gather_fusion.11 = bf16[16,128,256]{2,1,0:T(8,128)(2,1)} fusion(bf16[41,128,256]{2,1,0:T(8,128)(2,1)S(1)} %concatenate.39, s32[1024]{0:T(1024)} %copy-done.70), kind=kCustom, calls=%fused_computation.11 | custom fusion | bytes 2097216 | tf_op jit(solution)/shard_map/gather | solution.py:89
  65.2 1.8 %gather_fusion.9 = bf16[16,128,256]{2,1,0:T(8,128)(2,1)} fusion(bf16[41,128,256]{2,1,0:T(8,128)(2,1)S(1)} %concatenate.39, s32[1024]{0:T(1024)} %copy-done.67), kind=kCustom, calls=%fused_computation.9 | custom fusion | bytes 2097216 | tf_op jit(solution)/shard_map/gather | solution.py:89
  67.0 1.7 %gather_fusion.7 = bf16[16,128,256]{2,1,0:T(8,128)(2,1)} fusion(bf16[41,128,256]{2,1,0:T(8,128)(2,1)S(1)} %concatenate.39, s32[1024]{0:T(1024)} %copy-done.69), kind=kCustom, calls=%fused_computation.7 | custom fusion | bytes 2097216 | tf_op jit(solution)/shard_map/gather | solution.py:89
  68.7 1.7 %gather_fusion.5 = bf16[16,128,256]{2,1,0:T(8,128)(2,1)} fusion(bf16[41,128,256]{2,1,0:T(8,128)(2,1)S(1)} %concatenate.39, s32[1024]{0:T(1024)} %copy-done.66), kind=kCustom, calls=%fused_computation.5 | custom fusion | bytes 2097216 | tf_op jit(solution)/shard_map/gather | solution.py:89
  70.4 1.9 %gather_fusion.3 = bf16[16,128,256]{2,1,0:T(8,128)(2,1)} fusion(bf16[41,128,256]{2,1,0:T(8,128)(2,1)S(1)} %concatenate.39, s32[1024]{0:T(1024)} %copy-done.68), kind=kCustom, calls=%fused_computation.3 | custom fusion | bytes 2097216 | tf_op jit(solution)/shard_map/gather | solution.py:89
  72.3 1.6 %gather_fusion.1 = bf16[16,128,256]{2,1,0:T(8,128)(2,1)} fusion(bf16[41,128,256]{2,1,0:T(8,128)(2,1)S(1)} %concatenate.39, s32[1024]{0:T(1024)S(1)} %pad_clamp_fusion.8), kind=kCustom, calls=%fused_computation.1 | custom fusion | bytes 2097216 | tf_op jit(solution)/shard_map/gather | solution.py:89
  73.9 2.9 %fusion.142 = f32[16,128,256]{2,1,0:T(8,128)S(1)} fusion(bf16[16,128,256]{2,1,0:T(8,128)(2,1)} %gather_fusion.1, f32[16,128]{1,0:T(8,128)S(1)} %bitcast.479, f32[16,128]{1,0:T(8,128)S(1)} %fusion.251, f32[16,128]{1,0:T(8,128)S(1)} %get-tuple-element.223, f32[16,128]{1,0:T(8,128)S(1)} %bitcast.471, f32[16,128]{1,0:T(8,128)S(1)} %get-tuple-element.224, ...), kind=kOutput, calls=%fused_computation.239 | convolution fusion | flops 137625600 | bytes 3211264 | tf_op jit(solution)/shard_map/bij,bjf->bif/dot_general | solution.py:97
  76.9 2.7 %fusion.144 = f32[16,128,256]{2,1,0:T(8,128)S(1)} fusion(bf16[16,128,256]{2,1,0:T(8,128)(2,1)S(1)} %copy-done.6, f32[16,128]{1,0:T(8,128)S(1)} %bitcast.477, f32[16,128]{1,0:T(8,128)S(1)} %bitcast.468, f32[16,128]{1,0:T(8,128)S(1)} %broadcast_add_fusion.14, f32[16,128]{1,0:T(8,128)S(1)} %broadcast_add_fusion.15, f32[16,128]{1,0:T(8,128)S(1)} %fusion.251, ...), kind=kOutput, calls=%fused_computation.240 | convolution fusion | flops 137625600 | bytes 3211264 | tf_op jit(solution)/shard_map/bij,bjf->bif/dot_general | solution.py:97
  79.7 2.7 %fusion.146 = f32[16,128,256]{2,1,0:T(8,128)S(1)} fusion(bf16[16,128,256]{2,1,0:T(8,128)(2,1)S(1)} %copy-done.8, f32[16,128]{1,0:T(8,128)S(1)} %bitcast.483, f32[16,128]{1,0:T(8,128)S(1)} %bitcast.474, f32[16,128]{1,0:T(8,128)S(1)} %copy-done.32, f32[16,128]{1,0:T(8,128)S(1)} %copy-done.30, f32[16,128]{1,0:T(8,128)S(1)} %fusion.251, ...), kind=kOutput, calls=%fused_computation.241 | convolution fusion | flops 137625600 | bytes 3211264 | tf_op jit(solution)/shard_map/bij,bjf->bif/dot_general | solution.py:97
  82.5 2.7 %fusion.148 = f32[16,128,256]{2,1,0:T(8,128)S(1)} fusion(bf16[16,128,256]{2,1,0:T(8,128)(2,1)S(1)} %copy-done.10, f32[16,128]{1,0:T(8,128)S(1)} %bitcast.481, f32[16,128]{1,0:T(8,128)S(1)} %bitcast.455, f32[16,128]{1,0:T(8,128)S(1)} %broadcast_add_fusion.10, f32[16,128]{1,0:T(8,128)S(1)} %broadcast_add_fusion.11, f32[16,128]{1,0:T(8,128)S(1)} %fusion.251, ...), kind=kOutput, calls=%fused_computation.242 | convolution fusion | flops 137625600 | bytes 3211264 | tf_op jit(solution)/shard_map/bij,bjf->bif/dot_general | solution.py:97
  85.2 2.7 %fusion.150 = f32[16,128,256]{2,1,0:T(8,128)S(1)} fusion(bf16[16,128,256]{2,1,0:T(8,128)(2,1)S(1)} %copy-done.12, f32[16,128]{1,0:T(8,128)S(1)} %bitcast.487, f32[16,128]{1,0:T(8,128)S(1)} %bitcast.461, f32[16,128]{1,0:T(8,128)S(1)} %broadcast_add_fusion.8, f32[16,128]{1,0:T(8,128)S(1)} %broadcast_add_fusion.9, f32[16,128]{1,0:T(8,128)S(1)} %fusion.251, ...), kind=kOutput, calls=%fused_computation.243 | convolution fusion | flops 137625600 | bytes 3211264 | tf_op jit(solution)/shard_map/bij,bjf->bif/dot_general | solution.py:97
  88.0 2.7 %fusion.152 = f32[16,128,256]{2,1,0:T(8,128)S(1)} fusion(bf16[16,128,256]{2,1,0:T(8,128)(2,1)S(1)} %copy-done.14, f32[16,128]{1,0:T(8,128)S(1)} %bitcast.485, f32[16,128]{1,0:T(8,128)S(1)} %bitcast.458, f32[16,128]{1,0:T(8,128)S(1)} %broadcast_add_fusion.6, f32[16,128]{1,0:T(8,128)S(1)} %broadcast_add_fusion.7, f32[16,128]{1,0:T(8,128)S(1)} %fusion.251, ...), kind=kOutput, calls=%fused_computation.244 | convolution fusion | flops 137625600 | bytes 3211264 | tf_op jit(solution)/shard_map/bij,bjf->bif/dot_general | solution.py:97
  90.8 2.7 %fusion.154 = f32[16,128,256]{2,1,0:T(8,128)S(1)} fusion(bf16[16,128,256]{2,1,0:T(8,128)(2,1)S(1)} %copy-done.16, f32[16,128]{1,0:T(8,128)S(1)} %bitcast.492, f32[16,128]{1,0:T(8,128)S(1)} %bitcast.490, f32[16,128]{1,0:T(8,128)S(1)} %broadcast_add_fusion.4, f32[16,128]{1,0:T(8,128)S(1)} %copy-done.34, f32[16,128]{1,0:T(8,128)S(1)} %fusion.251, ...), kind=kOutput, calls=%fused_computation.245 | convolution fusion | flops 137625600 | bytes 3211264 | tf_op jit(solution)/shard_map/bij,bjf->bif/dot_general | solution.py:97
  93.6 2.7 %fusion.156 = f32[16,128,256]{2,1,0:T(8,128)S(1)} fusion(bf16[16,128,256]{2,1,0:T(8,128)(2,1)S(1)} %copy-done.3, f32[16,128]{1,0:T(8,128)S(1)} %bitcast.466, f32[16,128]{1,0:T(8,128)S(1)} %bitcast.464, f32[16,128]{1,0:T(8,128)S(1)} %broadcast_add_fusion.2, f32[16,128]{1,0:T(8,128)S(1)} %broadcast_add_fusion.3, f32[16,128]{1,0:T(8,128)S(1)} %fusion.251, ...), kind=kOutput, calls=%fused_computation.246 | convolution fusion | flops 137625600 | bytes 3211264 | tf_op jit(solution)/shard_map/bij,bjf->bif/dot_general | solution.py:97
  96.3 2.0 %add_convert_fusion = bf16[16,128,256]{2,1,0:T(8,128)(2,1)S(1)} fusion(f32[16,128,256]{2,1,0:T(8,128)S(1)} %fusion.156, f32[16,128,256]{2,1,0:T(8,128)S(1)} %fusion.154, f32[16,128,256]{2,1,0:T(8,128)S(1)} %fusion.152, f32[16,128,256]{2,1,0:T(8,128)S(1)} %fusion.150, f32[16,128,256]{2,1,0:T(8,128)S(1)} %fusion.148, f32[16,128,256]{2,1,0:T(8,128)S(1)} %fusion.146, ...), kind=kOutput, calls=%fused_computation.37 | convolution fusion | flops 142344192 | bytes 18939904 | tf_op jit(solution)/shard_map/bij,bjf->bif/dot_general | solution.py:97
  99.0 1.8 %multiply_reduce_fusion = (f32[2048]{0:T(1024)S(1)}, f32[2048,256]{1,0:T(8,128)}) fusion(f32[256]{0:T(256)S(1)} %copy-done.88, bf16[256,256]{1,0:T(8,128)(2,1)S(1)} %copy-done, f32[2048,256]{1,0:T(8,128)S(1)} %fusion), kind=kOutput, calls=%fused_computation.35 | convolution fusion | flops 270006272 | bytes 4334592 | tf_op jit(solution)/shard_map/dot_general | solution.py:32
  100.8 3.4 %convolution_convert_fusion = bf16[2048,256]{1,0:T(8,128)(2,1)} fusion(bf16[256,256]{1,0:T(8,128)(2,1)S(1)} %copy-done.19, bf16[256,256]{1,0:T(8,128)(2,1)S(1)} %copy-done, f32[2048,256]{1,0:T(8,128)S(1)} %fusion, f32[2048,256]{1,0:T(8,128)} %get-tuple-element.255, f32[256]{0:T(256)S(1)} %copy-done.88), kind=kOutput, calls=%fused_computation.34 | convolution fusion | flops 541589504 | bytes 5506048 | tf_op jit(solution)/shard_map/dot_general | solution.py:39
  104.2 3.7 %fusion.115 = (f32[16,128]{1,0:T(8,128)S(1)}, f32[16,128]{1,0:T(8,128)S(1)}, f32[16,128]{1,0:T(8,128)S(1)}, f32[16,128]{1,0:T(8,128)S(1)}, f32[16,128]{1,0:T(8,128)S(1)}, /*index=5*/f32[16,128]{1,0:T(8,128)S(1)}) fusion(f32[16,128]{1,0:T(8,128)} %broadcast_add_fusion.5, f32[16,128]{1,0:T(8,128)S(1)} %get-tuple-element.222, ...), kind=kOutput, calls=%fused_computation.212 | convolution fusion | flops 140234752 | bytes 2211840 | tf_op jit(solution)/shard_map/bif,bjf->bij/dot_general | solution.py:112
  108.0 2.1 %fusion.5 = f32[16,128,128]{2,1,0:T(8,128)} fusion(bf16[16,128,256]{2,1,0:T(8,128)(2,1)S(1)} %bitcast.357, bf16[16,128,256]{2,1,0:T(8,128)(2,1)S(1)} %copy-done.15, f32[16,128]{1,0:T(8,128)S(1)} %bitcast.486, f32[16,128]{1,0:T(8,128)S(1)} %bitcast.459, f32[16,128]{1,0:T(8,128)S(1)} %broadcast_add_fusion.6, f32[16,128]{1,0:T(8,128)S(1)} %broadcast_add_fusion.7, ...), kind=kOutput, calls=%fused_computation.99 | convolution fusion | flops 137887744 | bytes 3211264 | tf_op jit(solution)/shard_map/bif,bjf->bij/dot_general | solution.py:112
  110.2 2.1 %fusion.6 = f32[16,128,128]{2,1,0:T(8,128)} fusion(bf16[16,128,256]{2,1,0:T(8,128)(2,1)S(1)} %bitcast.358, bf16[16,128,256]{2,1,0:T(8,128)(2,1)S(1)} %copy-done.13, f32[16,128]{1,0:T(8,128)S(1)} %bitcast.488, f32[16,128]{1,0:T(8,128)S(1)} %bitcast.462, f32[16,128]{1,0:T(8,128)S(1)} %broadcast_add_fusion.8, f32[16,128]{1,0:T(8,128)S(1)} %broadcast_add_fusion.9, ...), kind=kOutput, calls=%fused_computation.101 | convolution fusion | flops 137887744 | bytes 3211264 | tf_op jit(solution)/shard_map/bif,bjf->bij/dot_general | solution.py:112
  112.4 2.1 %fusion.7 = f32[16,128,128]{2,1,0:T(8,128)} fusion(bf16[16,128,256]{2,1,0:T(8,128)(2,1)S(1)} %bitcast.359, bf16[16,128,256]{2,1,0:T(8,128)(2,1)S(1)} %copy-done.11, f32[16,128]{1,0:T(8,128)S(1)} %bitcast.482, f32[16,128]{1,0:T(8,128)S(1)} %bitcast.456, f32[16,128]{1,0:T(8,128)S(1)} %broadcast_add_fusion.10, f32[16,128]{1,0:T(8,128)S(1)} %broadcast_add_fusion.11, ...), kind=kOutput, calls=%fused_computation.103 | convolution fusion | flops 137887744 | bytes 3211264 | tf_op jit(solution)/shard_map/bif,bjf->bij/dot_general | solution.py:112
  114.6 1.9 %fusion.8 = f32[16,128,128]{2,1,0:T(8,128)S(1)} fusion(bf16[16,128,256]{2,1,0:T(8,128)(2,1)S(1)} %bitcast.360, bf16[16,128,256]{2,1,0:T(8,128)(2,1)S(1)} %copy-done.9, f32[16,128]{1,0:T(8,128)S(1)} %bitcast.484, f32[16,128]{1,0:T(8,128)S(1)} %bitcast.475, f32[16,128]{1,0:T(8,128)S(1)} %copy-done.33, f32[16,128]{1,0:T(8,128)S(1)} %copy-done.31, ...), kind=kOutput, calls=%fused_computation.105 | convolution fusion | flops 137887744 | bytes 3211264 | tf_op jit(solution)/shard_map/bif,bjf->bij/dot_general | solution.py:112
  116.6 1.9 %fusion.9 = f32[16,128,128]{2,1,0:T(8,128)S(1)} fusion(bf16[16,128,256]{2,1,0:T(8,128)(2,1)S(1)} %bitcast.361, bf16[16,128,256]{2,1,0:T(8,128)(2,1)S(1)} %copy-done.7, f32[16,128]{1,0:T(8,128)S(1)} %bitcast.478, f32[16,128]{1,0:T(8,128)S(1)} %bitcast.469, f32[16,128]{1,0:T(8,128)S(1)} %copy-done.25, f32[16,128]{1,0:T(8,128)S(1)} %copy-done.23, ...), kind=kOutput, calls=%fused_computation.107 | convolution fusion | flops 137887744 | bytes 3211264 | tf_op jit(solution)/shard_map/bif,bjf->bij/dot_general | solution.py:112
  118.6 1.9 %fusion.10 = f32[16,128,128]{2,1,0:T(8,128)S(1)} fusion(bf16[16,128,256]{2,1,0:T(8,128)(2,1)S(1)} %bitcast.362, bf16[16,128,256]{2,1,0:T(8,128)(2,1)S(1)} %copy-done.5, f32[16,128]{1,0:T(8,128)S(1)} %bitcast.480, f32[16,128]{1,0:T(8,128)S(1)} %fusion.251, f32[16,128]{1,0:T(8,128)S(1)} %get-tuple-element.223, f32[16,128]{1,0:T(8,128)S(1)} %bitcast.472, ...), kind=kOutput, calls=%fused_computation.109 | convolution fusion | flops 137887744 | bytes 3211264 | tf_op jit(solution)/shard_map/bif,bjf->bij/dot_general | solution.py:112
  120.5 5.1 %fusion.127 = (f32[16,128]{1,0:T(8,128)S(1)}, f32[16,128]{1,0:T(8,128)S(1)}, f32[16,128]{1,0:T(8,128)S(1)}, f32[16,128]{1,0:T(8,128)S(1)}, f32[16,128]{1,0:T(8,1...) fusion(f32[16,128]{1,0:T(8,128)S(1)} %broadcast_add_fusion.1, ...), kind=kOutput, calls=%fused_computation.224 | convolution fusion | flops 149635072 | bytes 5578752 | tf_op jit(solution)/shard_map/bif,bjf->bij/dot_general | solution.py:112
  125.7 1.1 scatter_fusion
  128.0 1.3 scatter_fusion.2
  129.4 6.4 %fusion.121 = (f32[16,128]{1,0:T(8,128)S(1)}, f32[16,128]{1,0:T(8,128)S(1)}, f32[16,128]{1,0:T(8,128)S(1)}, f32[16,128]{1,0:T(8,128)S(1)}, f32[16,128]{1,0:T(8,1...) fusion(f32[16,128]{1,0:T(8,128)S(1)} %broadcast_add_fusion.3, ...), kind=kOutput, calls=%fused_computation.218 | convolution fusion | flops 149635072 | bytes 5578752 | tf_op jit(solution)/shard_map/bif,bjf->bij/dot_general | solution.py:112
  138.1 1.1 scatter_fusion.5
  139.3 1.1 scatter_fusion.6
  141.6 1.1 scatter_fusion.8
  144.1 3.6 %collective-permute-start.9 = (f32[3,10,128]{2,0,1:T(4,128)S(1)}, f32[3,10,128]{2,0,1:T(4,128)S(1)}, u32[]{:S(2)}, u32[]{:S(2)}) collective-permute-start(f32[3,10,128]{2,0,1:T(4,128)S(1)} %get-tuple-element.180), channel_id=1, source_target_pairs={{4,0},{8,4},{12,8},{16,12},{20,16},{24,20},{28,24},{0,28},{5,1},{9... | collective-permute-start | bytes 46088 | tf_op jit(solution)/shard_map/ppermute | solution.py:25
  147.7 1.4 collective-permute-done.8
  149.3 1.3 collective-permute-start.10
  151.4 1.6 %collective-permute-start.11 = (f32[3,2,128]{2,1,0:T(2,128)S(1)}, f32[3,2,128]{2,1,0:T(2,128)S(1)}, u32[]{:S(2)}, u32[]{:S(2)}) collective-permute-start(f32[3,2,128]{2,1,0:T(2,128)S(1)} %get-tuple-element.220), channel_id=1, source_target_pairs={{1,0},{2,1},{3,2},{0,3},{5,4},{6,5},{7,6},{4,7},{9,8},{10,9},{11,1... | collective-permute-start | bytes 9224 | tf_op jit(solution)/shard_map/ppermute | solution.py:25
  (320 shorter events, 42.4 us)
Async XLA Ops:
  0.6 98.1 %copy-start = (bf16[256,256]{1,0:T(8,128)(2,1)S(1)}, bf16[256,256]{1,0:T(8,128)(2,1)}, u32[]{:S(2)}) copy-start(bf16[256,256]{1,0:T(8,128)(2,1)} %param.22) | copy-start | bytes 393220
  0.6 8.2 %copy-start.89 = (s32[2,8]{1,0:T(2,128)S(1)}, s32[2,8]{1,0:T(2,128)}, u32[]{:S(2)}) copy-start(s32[2,8]{1,0:T(2,128)} %param.18) | copy-start | bytes 196
  0.7 8.3 %copy-start.20 = (f32[3,2,8,128]{3,2,1,0:T(8,128)S(1)}, f32[3,2,8,128]{3,2,1,0:T(8,128)}, u32[]{:S(2)}) copy-start(f32[3,2,8,128]{3,2,1,0:T(8,128)} %param.16) | copy-start | bytes 73732
  0.7 8.3 %copy-start.18 = (s32[2,8,9]{2,1,0:T(8,128)S(1)}, s32[2,8,9]{2,1,0:T(8,128)}, u32[]{:S(2)}) copy-start(s32[2,8,9]{2,1,0:T(8,128)} %param.19) | copy-start | bytes 1732
  2.2 11.9 %collective-permute-start = (bf16[4,1,8,128]{3,2,1,0:T(8,128)(2,1)S(1)}, bf16[4,1,8,128]{3,2,1,0:T(8,128)(2,1)S(1)}, u32[]{:S(2)}, u32[]{:S(2)}) collective-permute-start(bf16[4,1,8,128]{3,2,1,0:T(8,128)(2,1)S(1)} %get-tuple-element.225), channel_id=1, source_target_pairs={{0,4},{4,8},{8,12},{12,16},{16,20},{20,24},{24,28},{28,0},{1,5},{5... | collective-permute-start | bytes 24584 | tf_op jit(solution)/shard_map/ppermute | solution.py:16
  2.7 11.5 %collective-permute-start.1 = (bf16[4,1,8,128]{3,2,1,0:T(8,128)(2,1)S(1)}, bf16[4,1,8,128]{3,2,1,0:T(8,128)(2,1)S(1)}, u32[]{:S(2)}, u32[]{:S(2)}) collective-permute-start(bf16[4,1,8,128]{3,2,1,0:T(8,128)(2,1)S(1)} %get-tuple-element.226), channel_id=1, source_target_pairs={{4,0},{8,4},{12,8},{16,12},{20,16},{24,20},{28,24},{0,28},{5,1},{9... | collective-permute-start | bytes 24584 | tf_op jit(solution)/shard_map/ppermute | solution.py:17
  8.1 35.6 %copy-start.2 = (bf16[2,8,128,256]{3,2,1,0:T(8,128)(2,1)S(1)}, bf16[2,8,128,256]{3,2,1,0:T(8,128)(2,1)}, u32[]{:S(2)}) copy-start(bf16[2,8,128,256]{3,2,1,0:T(8,128)(2,1)} %param.17) | copy-start | bytes 3145732
  8.1 35.7 %collective-permute-start.5 = (bf16[1,8,128,256]{3,2,1,0:T(8,128)(2,1)S(1)}, bf16[1,8,128,256]{3,2,1,0:T(8,128)(2,1)S(1)}, u32[]{:S(2)}, u32[]{:S(2)}) collective-permute-start(bf16[1,8,128,256]{3,2,1,0:T(8,128)(2,1)S(1)} %get-tuple-element.178), channel_id=1, source_target_pairs={{4,0},{8,4},{12,8},{16,12},{20,16},{24,20},{28,24},{0,28},{5,1},{9... | collective-permute-start | bytes 1572872 | tf_op jit(solution)/shard_map/ppermute | solution.py:17
  8.9 34.8 %collective-permute-start.4 = (bf16[1,8,128,256]{3,2,1,0:T(8,128)(2,1)S(1)}, bf16[1,8,128,256]{3,2,1,0:T(8,128)(2,1)S(1)}, u32[]{:S(2)}, u32[]{:S(2)}) collective-permute-start(bf16[1,8,128,256]{3,2,1,0:T(8,128)(2,1)S(1)} %get-tuple-element.179), channel_id=1, source_target_pairs={{0,4},{4,8},{8,12},{12,16},{16,20},{20,24},{24,28},{28,0},{1,5},{5... | collective-permute-start | bytes 1572872 | tf_op jit(solution)/shard_map/ppermute | solution.py:16
  9.1 6.9 %copy-start.91 = (s32[16]{0:T(128)}, s32[16]{0:T(128)S(1)}, u32[]{:S(2)}) copy-start(s32[16]{0:T(128)S(1)} %fusion.282) | copy-start | bytes 196
  10.3 3.8 %copy-start.86 = (s32[16]{0:T(128)}, s32[16]{0:T(128)S(1)}, u32[]{:S(2)}) copy-start(s32[16]{0:T(128)S(1)} %get-tuple-element.256) | copy-start | bytes 196
  10.3 3.9 %copy-start.82 = (s32[16]{0:T(128)}, s32[16]{0:T(128)S(1)}, u32[]{:S(2)}) copy-start(s32[16]{0:T(128)S(1)} %get-tuple-element.257) | copy-start | bytes 196
  11.0 10.1 %copy-start.78 = (s32[16]{0:T(128)}, s32[16]{0:T(128)S(1)}, u32[]{:S(2)}) copy-start(s32[16]{0:T(128)S(1)} %get-tuple-element.259) | copy-start | bytes 196
  11.5 9.5 %copy-start.80 = (s32[16]{0:T(128)}, s32[16]{0:T(128)S(1)}, u32[]{:S(2)}) copy-start(s32[16]{0:T(128)S(1)} %get-tuple-element.260) | copy-start | bytes 196
  12.1 7.7 %copy-start.72 = (s32[16]{0:T(128)}, s32[16]{0:T(128)S(1)}, u32[]{:S(2)}) copy-start(s32[16]{0:T(128)S(1)} %get-tuple-element.263) | copy-start | bytes 196
  14.0 13.1 %copy-start.67 = (s32[1024]{0:T(1024)}, s32[1024]{0:T(1024)S(1)}, u32[]{:S(2)}) copy-start(s32[1024]{0:T(1024)S(1)} %pad_clamp_fusion.4) | copy-start | bytes 12292
  14.0 11.9 %copy-start.70 = (s32[1024]{0:T(1024)}, s32[1024]{0:T(1024)S(1)}, u32[]{:S(2)}) copy-start(s32[1024]{0:T(1024)S(1)} %pad_clamp_fusion.3) | copy-start | bytes 12292
  14.1 10.6 %copy-start.66 = (s32[1024]{0:T(1024)}, s32[1024]{0:T(1024)S(1)}, u32[]{:S(2)}) copy-start(s32[1024]{0:T(1024)S(1)} %pad_clamp_fusion.6) | copy-start | bytes 12292
  14.1 10.6 %copy-start.69 = (s32[1024]{0:T(1024)}, s32[1024]{0:T(1024)S(1)}, u32[]{:S(2)}) copy-start(s32[1024]{0:T(1024)S(1)} %pad_clamp_fusion.5) | copy-start | bytes 12292
  14.1 13.0 %copy-start.68 = (s32[1024]{0:T(1024)}, s32[1024]{0:T(1024)S(1)}, u32[]{:S(2)}) copy-start(s32[1024]{0:T(1024)S(1)} %pad_clamp_fusion.7) | copy-start | bytes 12292
  14.2 11.8 %copy-start.71 = (s32[1024]{0:T(1024)}, s32[1024]{0:T(1024)S(1)}, u32[]{:S(2)}) copy-start(s32[1024]{0:T(1024)S(1)} %pad_clamp_fusion) | copy-start | bytes 12292
  14.2 4.6 %collective-permute-start.2 = (bf16[4,4,1,128]{3,2,1,0:T(2,128)(2,1)S(1)}, bf16[4,4,1,128]{3,2,1,0:T(2,128)(2,1)S(1)}, u32[]{:S(2)}, u32[]{:S(2)}) collective-permute-start(bf16[4,4,1,128]{3,2,1,0:T(2,128)(2,1)S(1)} %get-tuple-element.218), channel_id=1, source_target_pairs={{0,1},{1,2},{2,3},{3,0},{4,5},{5,6},{6,7},{7,4},{8,9},{9,10},{10,1... | collective-permute-start | bytes 12296 | tf_op jit(solution)/shard_map/ppermute | solution.py:16
  16.0 3.7 %collective-permute-start.3 = (bf16[4,4,1,128]{3,2,1,0:T(2,128)(2,1)S(1)}, bf16[4,4,1,128]{3,2,1,0:T(2,128)(2,1)S(1)}, u32[]{:S(2)}, u32[]{:S(2)}) collective-permute-start(bf16[4,4,1,128]{3,2,1,0:T(2,128)(2,1)S(1)} %get-tuple-element.219), channel_id=1, source_target_pairs={{1,0},{2,1},{3,2},{0,3},{5,4},{6,5},{7,6},{4,7},{9,8},{10,9},{11,1... | collective-permute-start | bytes 12296 | tf_op jit(solution)/shard_map/ppermute | solution.py:17
  32.5 44.2 %copy-start.22 = (f32[16,128]{1,0:T(8,128)}, f32[16,128]{1,0:T(8,128)S(1)}, u32[]{:S(2)}) copy-start(f32[16,128]{1,0:T(8,128)S(1)} %broadcast_add_fusion.15) | copy-start | bytes 24580
  33.3 43.5 %copy-start.24 = (f32[16,128]{1,0:T(8,128)}, f32[16,128]{1,0:T(8,128)S(1)}, u32[]{:S(2)}) copy-start(f32[16,128]{1,0:T(8,128)S(1)} %broadcast_add_fusion.14) | copy-start | bytes 24580
  34.1 39.8 %copy-start.26 = (f32[16,128]{1,0:T(8,128)}, f32[16,128]{1,0:T(8,128)S(1)}, u32[]{:S(2)}) copy-start(f32[16,128]{1,0:T(8,128)S(1)} %broadcast_add_fusion.17) | copy-start | bytes 24580
  34.7 39.1 %copy-start.28 = (f32[16,128]{1,0:T(8,128)}, f32[16,128]{1,0:T(8,128)S(1)}, u32[]{:S(2)}) copy-start(f32[16,128]{1,0:T(8,128)S(1)} %broadcast_add_fusion.16) | copy-start | bytes 24580
  43.9 10.2 %collective-permute-start.6 = (bf16[4,1,128,256]{3,2,1,0:T(8,128)(2,1)S(1)}, bf16[4,1,128,256]{3,2,1,0:T(8,128)(2,1)S(1)}, u32[]{:S(2)}, u32[]{:S(2)}) collective-permute-start(bf16[4,1,128,256]{3,2,1,0:T(8,128)(2,1)S(1)} %get-tuple-element.176), channel_id=1, source_target_pairs={{0,1},{1,2},{2,3},{3,0},{4,5},{5,6},{6,7},{7,4},{8,9},{9,10},{10,1... | collective-permute-start | bytes 786440 | tf_op jit(solution)/shard_map/ppermute | solution.py:16
  46.4 11.3 %collective-permute-start.7 = (bf16[4,1,128,256]{3,2,1,0:T(8,128)(2,1)S(1)}, bf16[4,1,128,256]{3,2,1,0:T(8,128)(2,1)S(1)}, u32[]{:S(2)}, u32[]{:S(2)}) collective-permute-start(bf16[4,1,128,256]{3,2,1,0:T(8,128)(2,1)S(1)} %get-tuple-element.177), channel_id=1, source_target_pairs={{1,0},{2,1},{3,2},{0,3},{5,4},{6,5},{7,6},{4,7},{9,8},{10,9},{11,1... | collective-permute-start | bytes 786440 | tf_op jit(solution)/shard_map/ppermute | solution.py:17
  47.0 43.7 %copy-start.35 = (f32[16,128]{1,0:T(8,128)}, f32[16,128]{1,0:T(8,128)S(1)}, u32[]{:S(2)}) copy-start(f32[16,128]{1,0:T(8,128)S(1)} %broadcast_add_fusion.4) | copy-start | bytes 24580
  120.5 5.2 %copy-start.87 = (s32[16]{0:T(128)S(1)}, s32[16]{0:T(128)}, u32[]{:S(2)}) copy-start(s32[16]{0:T(128)} %copy-done.86) | copy-start | bytes 196
  120.5 6.4 %copy-start.83 = (s32[16]{0:T(128)S(1)}, s32[16]{0:T(128)}, u32[]{:S(2)}) copy-start(s32[16]{0:T(128)} %copy-done.82) | copy-start | bytes 196
  120.5 7.5 %copy-start.85 = (s32[16]{0:T(128)S(1)}, s32[16]{0:T(128)}, u32[]{:S(2)}) copy-start(s32[16]{0:T(128)} %copy-done.84) | copy-start | bytes 196
  120.5 8.8 %copy-start.4 = (bf16[16,128,256]{2,1,0:T(8,128)(2,1)S(1)}, bf16[16,128,256]{2,1,0:T(8,128)(2,1)}, u32[]{:S(2)}) copy-start(bf16[16,128,256]{2,1,0:T(8,128)(2,1)} %gather_fusion.15) | copy-start | bytes 3145732
  120.5 8.8 %copy-start.43 = (f32[1,16,128]{2,0,1:T(1,128)S(1)}, f32[1,16,128]{2,0,1:T(1,128)}, u32[]{:S(2)}) copy-start(f32[1,16,128]{2,0,1:T(1,128)} %get-tuple-element.215) | copy-start | bytes 24580
  120.5 8.8 %copy-start.45 = (f32[1,16,128]{2,0,1:T(1,128)S(1)}, f32[1,16,128]{2,0,1:T(1,128)}, u32[]{:S(2)}) copy-start(f32[1,16,128]{2,0,1:T(1,128)} %get-tuple-element.217) | copy-start | bytes 24580
  129.3 6.5 %copy-start.79 = (s32[16]{0:T(128)S(1)}, s32[16]{0:T(128)}, u32[]{:S(2)}) copy-start(s32[16]{0:T(128)} %copy-done.78) | copy-start | bytes 196
  129.4 7.6 %copy-start.81 = (s32[16]{0:T(128)S(1)}, s32[16]{0:T(128)}, u32[]{:S(2)}) copy-start(s32[16]{0:T(128)} %copy-done.80) | copy-start | bytes 196
  129.4 8.8 %copy-start.75 = (s32[16]{0:T(128)S(1)}, s32[16]{0:T(128)}, u32[]{:S(2)}) copy-start(s32[16]{0:T(128)} %copy-done.74) | copy-start | bytes 196
  129.4 9.9 %copy-start.77 = (s32[16]{0:T(128)S(1)}, s32[16]{0:T(128)}, u32[]{:S(2)}) copy-start(s32[16]{0:T(128)} %copy-done.76) | copy-start | bytes 196
  129.4 11.1 %copy-start.73 = (s32[16]{0:T(128)S(1)}, s32[16]{0:T(128)}, u32[]{:S(2)}) copy-start(s32[16]{0:T(128)} %copy-done.72) | copy-start | bytes 196
  129.4 12.2 %copy-start.92 = (s32[16]{0:T(128)S(1)}, s32[16]{0:T(128)}, u32[]{:S(2)}) copy-start(s32[16]{0:T(128)} %copy-done.91) | copy-start | bytes 196
  129.4 13.5 %copy-start.96 = (s32[16]{0:T(128)S(1)}, s32[16]{0:T(128)}, u32[]{:S(2)}) copy-start(s32[16]{0:T(128)} %fusion.283) | copy-start | bytes 196
  129.4 21.3 %copy-start.90 = (s32[2,8]{1,0:T(2,128)S(1)}, s32[2,8]{1,0:T(2,128)}, u32[]{:S(2)}) copy-start(s32[2,8]{1,0:T(2,128)} %param.18) | copy-start | bytes 196
  144.1 5.1 %collective-permute-start.8 = (f32[3,10,128]{2,0,1:T(4,128)S(1)}, f32[3,10,128]{2,0,1:T(4,128)S(1)}, u32[]{:S(2)}, u32[]{:S(2)}) collective-permute-start(f32[3,10,128]{2,0,1:T(4,128)S(1)} %get-tuple-element.181), channel_id=1, source_target_pairs={{28,0},{0,4},{4,8},{8,12},{12,16},{16,20},{20,24},{24,28},{29,1},{... | collective-permute-start | bytes 46088 | tf_op jit(solution)/shard_map/ppermute | solution.py:25
  144.1 5.1 %collective-permute-start.9 = (f32[3,10,128]{2,0,1:T(4,128)S(1)}, f32[3,10,128]{2,0,1:T(4,128)S(1)}, u32[]{:S(2)}, u32[]{:S(2)}) collective-permute-start(f32[3,10,128]{2,0,1:T(4,128)S(1)} %get-tuple-element.180), channel_id=1, source_target_pairs={{4,0},{8,4},{12,8},{16,12},{20,16},{24,20},{28,24},{0,28},{5,1},{9... | collective-permute-start | bytes 46088 | tf_op jit(solution)/shard_map/ppermute | solution.py:25
  149.3 4.5 %collective-permute-start.10 = (f32[3,2,128]{2,1,0:T(2,128)S(1)}, f32[3,2,128]{2,1,0:T(2,128)S(1)}, u32[]{:S(2)}, u32[]{:S(2)}) collective-permute-start(f32[3,2,128]{2,1,0:T(2,128)S(1)} %get-tuple-element.221), channel_id=1, source_target_pairs={{3,0},{0,1},{1,2},{2,3},{7,4},{4,5},{5,6},{6,7},{11,8},{8,9},{9,10... | collective-permute-start | bytes 9224 | tf_op jit(solution)/shard_map/ppermute | solution.py:25
  151.4 3.6 %collective-permute-start.11 = (f32[3,2,128]{2,1,0:T(2,128)S(1)}, f32[3,2,128]{2,1,0:T(2,128)S(1)}, u32[]{:S(2)}, u32[]{:S(2)}) collective-permute-start(f32[3,2,128]{2,1,0:T(2,128)S(1)} %get-tuple-element.220), channel_id=1, source_target_pairs={{1,0},{2,1},{3,2},{0,3},{5,4},{6,5},{7,6},{4,7},{9,8},{10,9},{11,1... | collective-permute-start | bytes 9224 | tf_op jit(solution)/shard_map/ppermute | solution.py:25
  (61 other events, 154.2 us)
where the time goes:
time: 156 us
  matrix products  56.7 us (36%)
  other arithmetic  32.5 us (21%)
  local copies, waits for them, and re-layouts  30.2 us (19%)
  starting transfers between devices  17.9 us (11%)
  waiting for transfers between devices  15.9 us (10%)
  between operations  2.42 us (2%)
    dot_general x9, matrix products, body(): jnp.einsum('bif,bjf->bij', gradients, remote_embed, preferred_element_typ...  27.3 us
    dot_general x9, matrix products, body(): jnp.einsum('bij,bjf->bif', weight.astype(jnp.bfloat16), remote_embed, pre...  23.8 us
    gather x9, local copies, waits for them, and re-layouts, gather_bin(): return (remote[:3], remote[3], flat_embed[linked], shift_x, shift_y, linked)  15.6 us
    scatter-add x9, other arithmetic, body(): ghost_force = ghost_force.at[:, linked].add(pushed)  10.1 us
    ppermute x4, waiting for transfers between devices, padded(): before = lax.ppermute(last, axis, up)  8.11 us
    add x9, other arithmetic, pair_weights(): shift_x[:, None, None] + remote_pos[0][:, None, :] - own_pos[0][:, :, None]  7.83 us
    ppermute x4, starting transfers between devices, shifted(): return lax.ppermute(block, axis, route)  6.61 us
    ppermute x4, starting transfers between devices, padded(): after = lax.ppermute(leading, axis, down)  6.53 us
  transfers between devices with their start and end apart: 12, of which 7 were waited for; matrix products, arithmetic and copies ran while one was open for 20% of the time, Pallas kernels for 0%

commit v1 on v0

v1 whole, which is shorter than its diff:
```python
import functools
import math

import jax
import jax.numpy as jnp
from jax import lax
from jax.experimental import pallas as pl
from jax.experimental.pallas import tpu as pltpu
from jax.sharding import PartitionSpec as P

radius = 0.4
coord_scale = math.sqrt(math.log2(math.e) / (2.0 * radius * radius))
far = 1e18
f32 = jnp.float32
bf16 = jnp.bfloat16
across = (((1,), (1,)), ((), ()))


def pair_exchange(value, axis, offset):
    count = lax.axis_size(axis)
    pairs = []
    for a in range(offset, count + offset, 2):
        pairs += [(a % count, (a + 1) % count), ((a + 1) % count, a % count)]
    return lax.ppermute(value, axis, pairs)


def split(value):
    high = value.astype(bf16)
    return high, (value - high.astype(f32)).astype(bf16)


def row_sums(value):
    high, low = split(value)
    ones = jnp.ones((8, value.shape[1]), bf16)
    total = lax.dot_general(ones, high, across, preferred_element_type=f32)
    return (total + lax.dot_general(ones, low, across, preferred_element_type=f32))[0:1]


def kernel(
    sizes, info, links, coords, embed, row_a, row_b, col_a, col_b, w_one, bias_one, w_two, w_out,
    grid_out, energy_out, ext, tails, weights, features, gradients, table, pushed, sems
):
    rows_y, atoms, width = sizes
    cols = rows_y + 2
    odd_x, odd_y = info[0], info[1]
    sign = jnp.where(odd_x == 1, 1.0, -1.0).astype(f32)
    side_a = jnp.where(odd_y == 1, 0, cols - 1)
    side_b = cols - 1 - side_a
    block = rows_y * atoms
    copies = []

    def fetch(src, dst):
        copy = pltpu.make_async_copy(src, dst, sems.at[len(copies)])
        copy.start()
        copies.append(copy)

    def rows_at(slot, count):
        return ext.at[pl.ds(pl.multiple_of(slot * atoms, atoms), count)]

    fetch(embed.at[1 - odd_x], rows_at(cols + 1, block))
    fetch(embed.at[odd_x], rows_at(2 * cols + 1, block))
    fetch(row_a.at[pl.ds(0, block)], rows_at(1, block))
    fetch(row_b.at[pl.ds(0, block)], rows_at(3 * cols + 1, block))
    for lx in range(4):
        fetch(col_a.at[pl.ds(lx * atoms, atoms)], rows_at(lx * cols + side_a, atoms))
        fetch(col_b.at[pl.ds(lx * atoms, atoms)], rows_at(lx * cols + side_b, atoms))
    fetch(row_a.at[pl.ds(block, 4 * rows_y)], tails.at[0])
    fetch(row_b.at[pl.ds(block, 4 * rows_y)], tails.at[1])
    fetch(col_a.at[pl.ds(4 * atoms, 16)], tails.at[2, pl.ds(0, 16)])
    fetch(col_b.at[pl.ds(4 * atoms, 16)], tails.at[3, pl.ds(0, 16)])

    def place(slot_x, slot_y, value):
        slot = slot_x * cols + slot_y
        there = value[3:4] > 0.5
        z = value[2:3] * coord_scale
        table[slot, 0:1] = (value[0:1] * sign + float(slot_x)) * coord_scale
        at_y = slot_y if isinstance(slot_y, int) else slot_y.astype(f32)
        table[slot, 1:2] = (value[1:2] + at_y) * coord_scale
        table[slot, 2:3] = jnp.where(there, z, -far)
        table[slot, 3:4] = jnp.where(there, z, far)
        table[slot, 4:5] = value[3:4]

    for lx in (1, 2):
        at = 1 - odd_x if lx == 1 else odd_x
        for y in range(rows_y):
            place(lx, y + 1, coords[at, y])
    pushed[...] = jnp.zeros_like(pushed)
    for copy in copies:
        copy.wait()

    def unpack(part, rows):
        both = tails[part, pl.ds(0, rows)].astype(f32)
        return both[:, :atoms] + both[:, atoms:]

    for part, lx in ((0, 0), (1, 3)):
        value = unpack(part, 4 * rows_y)
        for y in range(rows_y):
            place(lx, y + 1, value[4 * y : 4 * y + 4])
    for part, side in ((2, side_a), (3, side_b)):
        value = unpack(part, 16)
        for lx in range(4):
            place(lx, side, value[4 * lx : 4 * lx + 4])

    def columns(slot):
        spread = [jnp.broadcast_to(table[slot, c : c + 1], (atoms, atoms)).T for c in (0, 1, 3)]
        return spread

    def describe(lx, y):
        at = (lx - 1) * rows_y + y
        home_x = 1 - odd_x if lx == 1 else odd_x
        xi, yi, zi = columns(lx * cols + y + 1)
        total = jnp.zeros((atoms, width), f32)
        for kx in range(3):
            first = (lx + kx - 1) * cols + y
            list_x = jnp.where(odd_x == 1, kx, 2 - kx)
            parts = []
            for ky in range(3):
                slot = first + ky
                link = links[(home_x * rows_y + y) * 9 + list_x * 3 + ky]
                zj = jnp.where(link < 4 * cols, table[slot, 2:3], -far)
                dx = table[slot, 0:1] - xi
                dy = table[slot, 1:2] - yi
                dz = zj - zi
                parts.append(jnp.exp2(-(dx * dx + dy * dy + dz * dz)).astype(bf16))
            group = jnp.concatenate(parts, axis=1)
            weights[at, :, 3 * atoms * kx : 3 * atoms * (kx + 1)] = group
            near = ext[pl.ds(pl.multiple_of(first * atoms, atoms), 3 * atoms)]
            total = total + jnp.dot(group, near, preferred_element_type=f32)
        features[pl.ds(pl.multiple_of(at * atoms, atoms), atoms)] = total.astype(bf16)

    for lx in (1, 2):
        @pl.loop(0, rows_y)
        def _(y):
            describe(lx, y)

    bins = 2

    @pl.loop(0, 2 * rows_y // bins)
    def _(chunk):
        rows = pl.ds(pl.multiple_of(chunk * bins * atoms, bins * atoms), bins * atoms)
        act_one = jnp.tanh(jnp.dot(features[rows], w_one[...], preferred_element_type=f32) + bias_one[...])
        act_two = jnp.tanh(jnp.dot(act_one.astype(bf16), w_two[...], preferred_element_type=f32))
        out = w_out[...]
        scaled = act_two * out
        half = scaled[:, :128]
        for start in range(128, scaled.shape[1], 128):
            half = half + scaled[:, start : start + 128]
        energy = row_sums(half)
        for b in range(bins):
            at = chunk * bins + b
            slot = cols + 1 + at + jnp.where(at >= rows_y, 2, 0)
            energy_out[pl.ds(at, 1)] = energy[:, b * atoms : (b + 1) * atoms] * table[slot, 4:5]
        back_two = (out - scaled * act_two).astype(bf16)
        back_one = lax.dot_general(back_two, w_two[...], across, preferred_element_type=f32)
        back_one = (back_one * (1.0 - act_one * act_one)).astype(bf16)
        gradients[rows] = lax.dot_general(back_one, w_one[...], across, preferred_element_type=f32).astype(bf16)

    def push(lx, y):
        at = (lx - 1) * rows_y + y
        home = lx * cols + y + 1
        xi, yi, zi = columns(home)
        own = [jnp.zeros((atoms, atoms), f32) for _ in range(3)]
        grad = gradients[pl.ds(pl.multiple_of(at * atoms, atoms), atoms)]
        for kx in range(3):
            first = (lx + kx - 1) * cols + y
            near = ext[pl.ds(pl.multiple_of(first * atoms, atoms), 3 * atoms)]
            strength = lax.dot_general(grad, near, across, preferred_element_type=f32)
            strength = strength * weights[at, :, 3 * atoms * kx : 3 * atoms * (kx + 1)].astype(f32)
            for ky in range(3):
                slot = first + ky
                part = strength[:, ky * atoms : (ky + 1) * atoms]
                moved = [
                    part * (table[slot, 0:1] - xi),
                    part * (table[slot, 1:2] - yi),
                    part * (table[slot, 2:3] - zi),
                ]
                for c in range(3):
                    own[c] = own[c] + moved[c]
                    pushed[c, slot] += jnp.sum(moved[c].reshape(atoms // 8, 8, atoms), axis=0)
        for c in range(3):
            pushed[c, home, 0:1] -= row_sums(own[c])

    for lx in (1, 2):
        @pl.loop(0, rows_y)
        def _(y):
            push(lx, y)

    unit = 1.0 / (coord_scale * radius * radius)
    for c in range(3):
        total = jnp.sum(pushed[c], axis=1)
        grid_out[c] = total * (unit * sign if c == 0 else unit)


def body(positions, embed, counts, neighbours, w_one, bias_one, w_two, w_out):
    atoms = positions.shape[-1]
    rows_x, rows_y = counts.shape
    width, hidden = w_one.shape
    cols = rows_y + 2
    assert rows_x == 2 and atoms == 128
    block = rows_y * atoms
    odd_x = lax.axis_index("gx") % 2
    odd_y = lax.axis_index("gy") % 2
    occupied = (jnp.arange(atoms, dtype=jnp.int32) < counts[:, :, None]).astype(f32)
    coords = jnp.concatenate([positions.transpose(1, 2, 0, 3), occupied[:, :, None]], axis=2)
    packed = jnp.concatenate(split(coords), axis=-1)

    def row_message(x):
        main = lax.dynamic_index_in_dim(embed, x, 0, False).reshape(block, width)
        tail = lax.dynamic_index_in_dim(packed, x, 0, False).reshape(4 * rows_y, width)
        return jnp.concatenate([main, tail], axis=0)

    mine_a, mine_b = row_message(1 - odd_x), row_message(odd_x)
    row_b = pair_exchange(mine_b, "gx", 1)
    row_a = pair_exchange(mine_a, "gx", 0)

    def col_message(y):
        lines = [row_a, mine_a, mine_b, row_b]
        mains = [lax.dynamic_slice_in_dim(line, y * atoms, atoms, 0) for line in lines]
        ends = [lax.dynamic_slice_in_dim(line, block + 4 * y, 4, 0) for line in lines]
        return jnp.concatenate(mains + ends, axis=0)

    col_b = pair_exchange(col_message(odd_y * (rows_y - 1)), "gy", 1)
    col_a = pair_exchange(col_message((1 - odd_y) * (rows_y - 1)), "gy", 0)
    info = jnp.stack([odd_x, odd_y]).astype(jnp.int32)
    vmem = pl.BlockSpec(memory_space=pltpu.VMEM)
    smem = pl.BlockSpec(memory_space=pltpu.SMEM)
    anywhere = pl.BlockSpec(memory_space=pl.ANY)
    slots = 4 * cols
    own_rows = 2 * block
    grid, energy = pl.pallas_call(
        functools.partial(kernel, (rows_y, atoms, width)),
        out_shape=(
            jax.ShapeDtypeStruct((3, slots, atoms), f32),
            jax.ShapeDtypeStruct((2 * rows_y, atoms), f32),
        ),
        in_specs=[smem, smem, vmem] + [anywhere] * 5 + [vmem] * 4,
        out_specs=(vmem, vmem),
        scratch_shapes=[
            pltpu.VMEM((slots * atoms, width), bf16),
            pltpu.VMEM((4, 4 * rows_y, width), bf16),
            pltpu.VMEM((2 * rows_y, atoms, 9 * atoms), bf16),
            pltpu.VMEM((own_rows, width), bf16),
            pltpu.VMEM((own_rows, width), bf16),
            pltpu.VMEM((slots, 8, atoms), f32),
            pltpu.VMEM((3, slots, 8, atoms), f32),
            pltpu.SemaphoreType.DMA((16,)),
        ],
        compiler_params=pltpu.CompilerParams(vmem_limit_bytes=48 * 2**20),
    )(
        info, neighbours.reshape(-1), coords, embed.reshape(2, block, width), row_a, row_b, col_a, col_b,
        w_one, bias_one.reshape(1, hidden), w_two, w_out.reshape(1, hidden),
    )
    grid = grid.reshape(3, 4, cols, atoms)
    from_a = pair_exchange(grid[:, 0], "gx", 0)
    from_b = pair_exchange(grid[:, 3], "gx", 1)
    middle = jnp.stack([grid[:, 1] + from_a, grid[:, 2] + from_b], axis=1)
    first, last = middle[:, :, 0], middle[:, :, cols - 1]
    side_a = pair_exchange(jnp.where(odd_y == 1, first, last), "gy", 0)
    side_b = pair_exchange(jnp.where(odd_y == 1, last, first), "gy", 1)
    forces = middle[:, :, 1 : rows_y + 1]
    forces = forces.at[:, :, 0].add(jnp.where(odd_y == 1, side_a, side_b))
    forces = forces.at[:, :, rows_y - 1].add(jnp.where(odd_y == 1, side_b, side_a))
    energy = energy.reshape(2, rows_y, atoms)
    forces = jnp.where(odd_x == 1, forces, forces[:, ::-1])
    energy = jnp.where(odd_x == 1, energy, energy[::-1])
    return forces, energy


def solution(mesh):
    in_specs = (
        P(None, "gx", "gy", None),
        P("gx", "gy", None, None),
        P("gx", "gy"),
        P("gx", "gy", None),
        P(),
        P(),
        P(),
        P(),
    )
    out_specs = (P(None, "gx", "gy", None), P("gx", "gy", None))
    return jax.shard_map(body, mesh=mesh, in_specs=in_specs, out_specs=out_specs, check_vma=False)
```

time: 156 us -> 72.6 us (0.47)
  matrix products: 56.7 us -> 0 us
  other arithmetic: 32.5 us -> 3.47 us
  local copies, waits for them, and re-layouts: 30.2 us -> 3.09 us
  Pallas kernels: 0 us -> 24.4 us
  waiting for transfers between devices: 15.9 us -> 25.1 us
  starting transfers between devices: 17.9 us -> 15.4 us
    dot_general x21 -> x0, matrix products: 56.7 us -> none  [the longest x9 27.3 us: body(): jnp.einsum('bif,bjf->bij', gradients, remote_embed, preferred_element_typ...]
    pallas_call x0 -> x1, Pallas kernels: none -> 24.4 us  [body(): pl.pallas_call(functools.partial(kernel, (rows_y, atoms, width)), out_sha...]
    gather x18 -> x0, local copies, waits for them, and re-layouts: 21.1 us -> none  [the longest x9 15.6 us: gather_bin(): return (remote[:3], remote[3], flat_embed[linked], shift_x, shift_y, linked)]
    add x20 -> x2, other arithmetic: 13.4 us -> 0.02 us  [the longest x1 0.01 us: body(): forces = forces.at[:, :, 0].add(jnp.where(odd_y == 1, side_a, side_b))]
    scatter-add x12 -> x0, other arithmetic: 11.2 us -> none  [the longest x9 10.1 us: body(): ghost_force = ghost_force.at[:, linked].add(pushed)]
    ppermute x12 -> x8, waiting for transfers between devices: 15.9 us -> 25.1 us  [pair_exchange(): return lax.ppermute(value, axis, pairs)]
    slice x15 -> x0, local copies, waits for them, and re-layouts: 6.45 us -> none  [the longest x9 5.02 us: pair_weights(): remote_pos[0][:, None, :]]
    ppermute x12 -> x8, starting transfers between devices: 17.9 us -> 15.4 us  [pair_exchange(): return lax.ppermute(value, axis, pairs)]
  transfers between devices with their start and end apart: 12 -> 8, of which waited for: 7 -> 6; matrix products, arithmetic and copies ran while one was open for 20% -> 3% of each run, Pallas kernels for 0% -> 0%
where the time goes in v1:
time: 72.6 us; the launch traced here: 72.4 us
  waiting for transfers between devices  25.1 us (35%)
  Pallas kernels  24.4 us (34%)
  starting transfers between devices  15.4 us (21%)
  other arithmetic  3.47 us (5%)
  local copies, waits for them, and re-layouts  3.09 us (4%)
  between operations  0.91 us (1%)
    ppermute x8, waiting for transfers between devices, pair_exchange(): return lax.ppermute(value, axis, pairs)  25.1 us
    pallas_call x1, Pallas kernels, body(): pl.pallas_call(functools.partial(kernel, (rows_y, atoms, width)), out_sha...  24.4 us
    ppermute x8, starting transfers between devices, pair_exchange(): return lax.ppermute(value, axis, pairs)  15.4 us
    concatenate x4, other arithmetic, row_message(): return jnp.concatenate([main, tail], axis=0)  1.92 us
  transfers between devices with their start and end apart: 8, of which 6 were waited for; matrix products, arithmetic and copies ran while one was open for 3% of the time, Pallas kernels for 0%

profile of v1, /device:TPU:0, one launch (start us, length us, event | category | flops | bytes accessed | tf_op | source)
XLA Modules:
  0.0 72.4 jit_solution(16017388255008873247)
XLA Ops:
  0.6 0.8 %copy.76 = f32[3,2,8,128]{3,0,2,1:T(4,128)S(1)} copy(f32[3,2,8,128]{3,2,1,0:T(8,128)} %param.12) | data formatting | bytes 49152 | tf_op args[0]
  1.4 0.8 %compare_convert_fusion = f32[2,8,1,128]{3,2,1,0:T(1,128)S(1)} fusion(s32[2,8]{1,0:T(2,128)} %param.14), kind=kLoop, calls=%fused_computation.36 | loop fusion | flops 4096 | bytes 8256 | tf_op jit(solution)/shard_map/convert_element_type | solution.py:203
  2.2 1.3 %constant_dynamic-slice_fusion.8 = (bf16[1,8,128,256]{3,2,1,0:T(8,128)(2,1)S(1)}, bf16[1,8,128,256]{3,2,1,0:T(8,128)(2,1)S(1)}) fusion(bf16[2,8,128,256]{3,2,1,0:T(8,128)(2,1)} %param.13, s32[]{:T(128)S(6)} %select_n.93, s32[]{:T(128)S(6)} %select_n.92), kind=kLoop, calls=%fused_computation.57 | loop fusion | bytes 2097160 | tf_op jit(solution)/shard_map/jit(dynamic_index_in_dim)/dynamic_slice | solution.py:208
  3.5 0.9 %pad_maximum_fusion.1 = bf16[1056,256]{1,0:T(8,128)(2,1)} fusion(bf16[32,256]{1,0:T(8,128)(2,1)S(1)} %reshape.129, bf16[1024,256]{1,0:T(8,128)(2,1)S(1)} %bitcast.51), kind=kLoop, calls=%fused_computation.9 | loop fusion | flops 1081344 | bytes 1081344 | tf_op jit(solution)/shard_map/concatenate | solution.py:210
  4.4 4.5 %collective-permute-start.1 = (bf16[1056,256]{1,0:T(8,128)(2,1)}, bf16[1056,256]{1,0:T(8,128)(2,1)S(1)}, u32[]{:S(2)}, u32[]{:S(2)}) collective-permute-start(bf16[1056,256]{1,0:T(8,128)(2,1)} %pad_maximum_fusion.1), channel_id=1, source_target_pairs={{4,8},{8,4},{12,16},{16,12},{20,24},{24,20},{28,0},{0,28},{5,9},{9... | collective-permute-start | bytes 1622024 | tf_op jit(solution)/shard_map/ppermute | solution.py:24
  8.9 0.8 %pad_maximum_fusion = bf16[1056,256]{1,0:T(8,128)(2,1)} fusion(bf16[32,256]{1,0:T(8,128)(2,1)S(1)} %reshape.127, bf16[1024,256]{1,0:T(8,128)(2,1)S(1)} %bitcast.54), kind=kLoop, calls=%fused_computation.4 | loop fusion | flops 1081344 | bytes 1081344 | tf_op jit(solution)/shard_map/concatenate | solution.py:210
  9.7 0.0 collective-permute-start
  9.8 0.2 fusion.1
  10.0 0.0 copy-start.5
  10.0 0.0 copy-start
  10.0 0.0 copy-start.1
  10.0 0.0 copy-start.2
  10.0 0.0 copy-start.3
  10.0 0.0 copy-start.4
  10.1 11.0 %collective-permute-done.1.row_b = bf16[1056,256]{1,0:T(8,128)(2,1)S(1)} collective-permute-done((bf16[1056,256]{1,0:T(8,128)(2,1)}, bf16[1056,256]{1,0:T(8,128)(2,1)S(1)}, u32[]{:S(2)}, u32[]{:S(2)}) %collective-permute-start.1) | collective-permute-done | bytes 540704 | tf_op jit(solution)/shard_map/ppermute | solution.py:24
  21.1 0.0 collective-permute-done.row_a
  21.2 0.1 concatenate.27
  21.3 3.6 %collective-permute-start.3 = (bf16[528,256]{1,0:T(8,128)(2,1)S(1)}, bf16[528,256]{1,0:T(8,128)(2,1)S(1)}, u32[]{:S(2)}, u32[]{:S(2)}) collective-permute-start(bf16[528,256]{1,0:T(8,128)(2,1)S(1)} %concatenate.27), channel_id=1, source_target_pairs={{1,2},{2,1},{3,0},{0,3},{5,6},{6,5},{7,4},{4,7},{9,10},{10,9},{11,... | collective-permute-start | bytes 811016 | tf_op jit(solution)/shard_map/ppermute | solution.py:24
  24.8 0.1 concatenate.26
  24.9 0.6 collective-permute-start.2
  25.5 0.0 copy-done.5
  25.5 0.1 reshape.124.links
  25.6 0.1 pad_add_fusion.info
  25.6 6.6 %collective-permute-done.3.col_b = bf16[528,256]{1,0:T(8,128)(2,1)S(1)} collective-permute-done((bf16[528,256]{1,0:T(8,128)(2,1)S(1)}, bf16[528,256]{1,0:T(8,128)(2,1)S(1)}, u32[]{:S(2)}, u32[]{:S(2)}) %collective-permute-start.3) | collective-permute-done | bytes 270368 | tf_op jit(solution)/shard_map/ppermute | solution.py:24
  32.2 2.6 %collective-permute-done.2.col_a = bf16[528,256]{1,0:T(8,128)(2,1)S(1)} collective-permute-done((bf16[528,256]{1,0:T(8,128)(2,1)S(1)}, bf16[528,256]{1,0:T(8,128)(2,1)S(1)}, u32[]{:S(2)}, u32[]{:S(2)}) %collective-permute-start.2) | collective-permute-done | bytes 270368 | tf_op jit(solution)/shard_map/ppermute | solution.py:24
  34.8 0.0 copy-done
  34.8 0.0 copy-done.1
  34.8 0.0 copy-done.2
  34.8 0.0 copy-done.3
  34.8 0.0 copy-done.4
  34.8 24.4 %shard_map.95 = (f32[3,40,128]{2,1,0:T(8,128)S(1)}, f32[16,128]{1,0:T(8,128)S(1)}) custom-call(s32[2]{0:T(128)S(1)} %pad_add_fusion.info, s32[144]{0:T(256)S(1)} %reshape.124.links, f32[2,8,4,128]{3,2,1,0:T(4,128)S(1)} %get-tuple-element.45.coords, bf16[2,1024,256]{2,1,0:T(8,128)(2,1)S(1)} %bitcast.47, bf16[1056,256]{1,0:T(8,128)(2,1)S(1)} %collective-permute-done.row_a, ...), custom_call_target="tpu_custom_call" | custom-call | tf_op jit(solution)/shard_map/pallas_call | solution.py:230
  59.3 0.1 collective-permute-start.4
  59.3 4.6 %collective-permute-start.5 = (f32[3,10,128]{2,1,0:T(8,128)S(1)}, f32[3,10,128]{2,1,0:T(8,128)S(1)}, u32[]{:S(2)}, u32[]{:S(2)}) collective-permute-start(f32[3,10,128]{2,1,0:T(8,128)S(1)} %get-tuple-element.66), channel_id=1, source_target_pairs={{4,8},{8,4},{12,16},{16,12},{20,24},{24,20},{28,0},{0,28},{5,9},{9... | collective-permute-start | bytes 46088 | tf_op jit(solution)/shard_map/ppermute | solution.py:24
  64.0 0.6 reverse_select_fusion.1
  64.6 0.0 collective-permute-done.4
  64.6 0.9 %collective-permute-done.5 = f32[3,10,128]{2,1,0:T(8,128)S(1)} collective-permute-done((f32[3,10,128]{2,1,0:T(8,128)S(1)}, f32[3,10,128]{2,1,0:T(8,128)S(1)}, u32[]{:S(2)}, u32[]{:S(2)}) %collective-permute-start.5) | collective-permute-done | bytes 15392 | tf_op jit(solution)/shard_map/ppermute | solution.py:24
  65.5 1.6 %collective-permute-start.6 = (f32[3,2,128]{2,1,0:T(2,128)S(1)}, f32[3,2,128]{2,1,0:T(2,128)S(1)}, u32[]{:S(2)}, u32[]{:S(2)}) collective-permute-start(f32[3,2,128]{2,1,0:T(2,128)S(1)} %bitcast.58), channel_id=1, source_target_pairs={{0,1},{1,0},{2,3},{3,2},{4,5},{5,4},{6,7},{7,6},{8,9},{9,8},{10,11... | collective-permute-start | bytes 9224 | tf_op jit(solution)/shard_map/ppermute | solution.py:24
  67.1 0.5 collective-permute-start.7
  67.6 1.6 %collective-permute-done.6 = f32[3,2,128]{2,1,0:T(2,128)S(1)} collective-permute-done((f32[3,2,128]{2,1,0:T(2,128)S(1)}, f32[3,2,128]{2,1,0:T(2,128)S(1)}, u32[]{:S(2)}, u32[]{:S(2)}) %collective-permute-start.6) | collective-permute-done | bytes 3104 | tf_op jit(solution)/shard_map/ppermute | solution.py:24
  69.2 2.4 %collective-permute-done.7 = f32[3,2,128]{2,1,0:T(2,128)S(1)} collective-permute-done((f32[3,2,128]{2,1,0:T(2,128)S(1)}, f32[3,2,128]{2,1,0:T(2,128)S(1)}, u32[]{:S(2)}, u32[]{:S(2)}) %collective-permute-start.7) | collective-permute-done | bytes 3104 | tf_op jit(solution)/shard_map/ppermute | solution.py:24
  71.8 0.6 copy.67
  (23 shorter events, 0.3 us)
Async XLA Ops:
  4.4 16.7 %collective-permute-start.1 = (bf16[1056,256]{1,0:T(8,128)(2,1)}, bf16[1056,256]{1,0:T(8,128)(2,1)S(1)}, u32[]{:S(2)}, u32[]{:S(2)}) collective-permute-start(bf16[1056,256]{1,0:T(8,128)(2,1)} %pad_maximum_fusion.1), channel_id=1, source_target_pairs={{4,8},{8,4},{12,16},{16,12},{20,24},{24,20},{28,0},{0,28},{5,9},{9... | collective-permute-start | bytes 1622024 | tf_op jit(solution)/shard_map/ppermute | solution.py:24
  9.7 11.4 %collective-permute-start = (bf16[1056,256]{1,0:T(8,128)(2,1)}, bf16[1056,256]{1,0:T(8,128)(2,1)S(1)}, u32[]{:S(2)}, u32[]{:S(2)}) collective-permute-start(bf16[1056,256]{1,0:T(8,128)(2,1)} %pad_maximum_fusion), channel_id=1, source_target_pairs={{0,4},{4,0},{8,12},{12,8},{16,20},{20,16},{24,28},{28,24},{1,5},{5... | collective-permute-start | bytes 1622024 | tf_op jit(solution)/shard_map/ppermute | solution.py:24
  10.0 15.5 %copy-start.5 = (s32[2,8,9]{2,1,0:T(8,128)S(1)}, s32[2,8,9]{2,1,0:T(8,128)}, u32[]{:S(2)}) copy-start(s32[2,8,9]{2,1,0:T(8,128)} %param.15) | copy-start | bytes 1732
  10.0 24.8 %copy-start = (bf16[2,8,128,256]{3,2,1,0:T(8,128)(2,1)S(1)}, bf16[2,8,128,256]{3,2,1,0:T(8,128)(2,1)}, u32[]{:S(2)}) copy-start(bf16[2,8,128,256]{3,2,1,0:T(8,128)(2,1)} %param.13) | copy-start | bytes 3145732
  10.0 24.8 %copy-start.1 = (bf16[256,256]{1,0:T(8,128)(2,1)S(1)}, bf16[256,256]{1,0:T(8,128)(2,1)}, u32[]{:S(2)}) copy-start(bf16[256,256]{1,0:T(8,128)(2,1)} %w_one.1) | copy-start | bytes 393220
  10.0 24.8 %copy-start.2 = (bf16[256,256]{1,0:T(8,128)(2,1)S(1)}, bf16[256,256]{1,0:T(8,128)(2,1)}, u32[]{:S(2)}) copy-start(bf16[256,256]{1,0:T(8,128)(2,1)} %w_two.1) | copy-start | bytes 393220
  10.0 24.8 %copy-start.3 = (f32[256]{0:T(256)S(1)}, f32[256]{0:T(256)}, u32[]{:S(2)}) copy-start(f32[256]{0:T(256)} %param.17) | copy-start | bytes 3076
  10.0 24.8 %copy-start.4 = (f32[256]{0:T(256)S(1)}, f32[256]{0:T(256)}, u32[]{:S(2)}) copy-start(f32[256]{0:T(256)} %param.19) | copy-start | bytes 3076
  21.3 11.0 %collective-permute-start.3 = (bf16[528,256]{1,0:T(8,128)(2,1)S(1)}, bf16[528,256]{1,0:T(8,128)(2,1)S(1)}, u32[]{:S(2)}, u32[]{:S(2)}) collective-permute-start(bf16[528,256]{1,0:T(8,128)(2,1)S(1)} %concatenate.27), channel_id=1, source_target_pairs={{1,2},{2,1},{3,0},{0,3},{5,6},{6,5},{7,4},{4,7},{9,10},{10,9},{11,... | collective-permute-start | bytes 811016 | tf_op jit(solution)/shard_map/ppermute | solution.py:24
  24.9 9.9 %collective-permute-start.2 = (bf16[528,256]{1,0:T(8,128)(2,1)S(1)}, bf16[528,256]{1,0:T(8,128)(2,1)S(1)}, u32[]{:S(2)}, u32[]{:S(2)}) collective-permute-start(bf16[528,256]{1,0:T(8,128)(2,1)S(1)} %concatenate.26), channel_id=1, source_target_pairs={{0,1},{1,0},{2,3},{3,2},{4,5},{5,4},{6,7},{7,6},{8,9},{9,8},{10,11... | collective-permute-start | bytes 811016 | tf_op jit(solution)/shard_map/ppermute | solution.py:24
  59.3 5.3 %collective-permute-start.4 = (f32[3,10,128]{2,1,0:T(8,128)S(1)}, f32[3,10,128]{2,1,0:T(8,128)S(1)}, u32[]{:S(2)}, u32[]{:S(2)}) collective-permute-start(f32[3,10,128]{2,1,0:T(8,128)S(1)} %get-tuple-element.67), channel_id=1, source_target_pairs={{0,4},{4,0},{8,12},{12,8},{16,20},{20,16},{24,28},{28,24},{1,5},{5... | collective-permute-start | bytes 46088 | tf_op jit(solution)/shard_map/ppermute | solution.py:24
  59.3 6.2 %collective-permute-start.5 = (f32[3,10,128]{2,1,0:T(8,128)S(1)}, f32[3,10,128]{2,1,0:T(8,128)S(1)}, u32[]{:S(2)}, u32[]{:S(2)}) collective-permute-start(f32[3,10,128]{2,1,0:T(8,128)S(1)} %get-tuple-element.66), channel_id=1, source_target_pairs={{4,8},{8,4},{12,16},{16,12},{20,24},{24,20},{28,0},{0,28},{5,9},{9... | collective-permute-start | bytes 46088 | tf_op jit(solution)/shard_map/ppermute | solution.py:24
  65.5 3.7 %collective-permute-start.6 = (f32[3,2,128]{2,1,0:T(2,128)S(1)}, f32[3,2,128]{2,1,0:T(2,128)S(1)}, u32[]{:S(2)}, u32[]{:S(2)}) collective-permute-start(f32[3,2,128]{2,1,0:T(2,128)S(1)} %bitcast.58), channel_id=1, source_target_pairs={{0,1},{1,0},{2,3},{3,2},{4,5},{5,4},{6,7},{7,6},{8,9},{9,8},{10,11... | collective-permute-start | bytes 9224 | tf_op jit(solution)/shard_map/ppermute | solution.py:24
  67.1 4.5 %collective-permute-start.7 = (f32[3,2,128]{2,1,0:T(2,128)S(1)}, f32[3,2,128]{2,1,0:T(2,128)S(1)}, u32[]{:S(2)}, u32[]{:S(2)}) collective-permute-start(f32[3,2,128]{2,1,0:T(2,128)S(1)} %bitcast.59), channel_id=1, source_target_pairs={{1,2},{2,1},{3,0},{0,3},{5,6},{6,5},{7,4},{4,7},{9,10},{10,9},{11,... | collective-permute-start | bytes 9224 | tf_op jit(solution)/shard_map/ppermute | solution.py:24

commit v2 on v0

v2 whole, which is shorter than its diff:
```python
import functools
import math

import jax
import jax.numpy as jnp
from jax import lax
from jax.experimental import pallas as pl
from jax.experimental.pallas import tpu as pltpu
from jax.sharding import PartitionSpec as P

radius = 0.4
coord_scale = math.sqrt(math.log2(math.e) / (2.0 * radius * radius))
far = 1e18
f32 = jnp.float32
bf16 = jnp.bfloat16
across = (((1,), (1,)), ((), ()))
lead = 7
lines = 32


def pair_exchange(value, axis, offset):
    count = lax.axis_size(axis)
    pairs = []
    for a in range(offset, count + offset, 2):
        pairs += [(a % count, (a + 1) % count), ((a + 1) % count, a % count)]
    return lax.ppermute(value, axis, pairs)


def split(value):
    high = value.astype(bf16)
    return high, (value - high.astype(f32)).astype(bf16)


def packed(value):
    return jnp.concatenate(split(value), axis=-1)


def row_sums(value):
    high, low = split(value)
    ones = jnp.ones((8, value.shape[1]), bf16)
    total = lax.dot_general(ones, high, across, preferred_element_type=f32)
    return (total + lax.dot_general(ones, low, across, preferred_element_type=f32))[0:1]


class Block:
    def __init__(self, sizes, info, links, ext, tab, sems):
        self.rows_y, self.atoms, self.width = sizes
        self.cols = self.rows_y + 2
        self.odd_x, self.odd_y = info[0], info[1]
        self.sign = jnp.where(self.odd_x == 1, 1.0, -1.0).astype(f32)
        self.side_a = jnp.where(self.odd_y == 1, 0, self.cols - 1)
        self.side_b = self.cols - 1 - self.side_a
        self.links, self.ext, self.tab, self.sems = links, ext, tab, sems
        self.copies = []

    def home(self, lx):
        return 1 - self.odd_x if lx == 1 else self.odd_x

    def fetch(self, src, dst):
        copy = pltpu.make_async_copy(src, dst, self.sems.at[len(self.copies)])
        copy.start()
        self.copies.append(copy)

    def wait(self, start=0, end=None):
        for copy in self.copies[start:end]:
            copy.wait()

    def bins_at(self, slot, count):
        at = pl.multiple_of(slot * self.atoms, self.atoms)
        return self.ext.at[pl.ds(at, count * self.atoms)]

    def fetch_row(self, lx, src):
        self.fetch(src, self.bins_at(lx * self.cols + 1, self.rows_y))

    def fetch_side(self, lx, side, src):
        self.fetch(src, self.bins_at(lx * self.cols + side, 1))

    def fetch_own(self, embed):
        for lx in (1, 2):
            self.fetch_row(lx, embed.at[self.home(lx)])

    def fetch_cols(self, col_a, col_b):
        for lx in (1, 2):
            rows = pl.ds((lx - 1) * self.atoms, self.atoms)
            self.fetch_side(lx, self.side_a, col_a.at[rows])
            self.fetch_side(lx, self.side_b, col_b.at[rows])

    def store(self, lx, rows, y, value):
        there = value[3] > 0.5
        z = value[2] * coord_scale
        self.tab[0, lx, rows] = (value[0] * self.sign + float(lx)) * coord_scale
        self.tab[1, lx, rows] = (value[1] + y) * coord_scale
        self.tab[2, lx, rows] = jnp.where(there, z, -far)
        self.tab[3, lx, rows] = jnp.where(there, z, far)

    def place_row(self, lx, value):
        y = lax.broadcasted_iota(jnp.int32, (self.rows_y, self.atoms), 0).astype(f32) + 1.0
        self.store(lx, pl.ds(lead + 1, self.rows_y), y, value)

    def place_side(self, lx, side, value):
        self.store(lx, pl.ds(lead + side, 1), side.astype(f32), value)

    def place_own(self, positions, occupied):
        for lx in (1, 2):
            at = self.home(lx)
            self.place_row(lx, [positions[0, at], positions[1, at], positions[2, at], occupied[at]])

    def unpacked(self, value):
        both = value.astype(f32)
        return both[:, : self.atoms] + both[:, self.atoms :]

    def place_cols(self, tail_a, tail_b):
        for tail, side in ((tail_a, self.side_a), (tail_b, self.side_b)):
            value = self.unpacked(tail)
            for lx in (1, 2):
                self.place_side(lx, side, [value[4 * c + lx - 1 : 4 * c + lx] for c in range(4)])

    def spread(self, upright):
        parts = [self.tab[part, lx, lead + 1 : lead + 1 + self.rows_y] for lx in (1, 2) for part in (0, 1, 3)]
        rest = jnp.zeros((self.atoms - 6 * self.rows_y, self.atoms), f32)
        upright[...] = jnp.concatenate(parts + [rest], axis=0).T
        self.upright = upright

    def mine(self, lx, y, some):
        first = 3 * (lx - 1) * self.rows_y + y
        columns = [first + c * self.rows_y for c in range(3)]
        return [jnp.broadcast_to(self.upright[some, c : c + 1], (lines, self.atoms)) for c in columns]

    def rows_of(self, lx, y, to, ky):
        kx = to - lx + 1
        list_x = jnp.where(self.odd_x == 1, kx, 2 - kx)
        link = self.links[(self.home(lx) * self.rows_y + y) * 9 + list_x * 3 + ky]
        at = pl.ds(lead + y + ky, 1)
        z = jnp.where(link < 4 * self.cols, self.tab[2, to, at], -far)
        return self.tab[0, to, at], self.tab[1, to, at], z

    def near(self, to, y, ky, count):
        return self.bins_at(to * self.cols + y + ky, count)[...]

    def describe(self, group, lx, y, targets):
        atoms = self.atoms
        for start in range(0, atoms, lines):
            some = slice(start, start + lines)
            mine = self.mine(lx, y, some)
            at = 0
            for to, ky, count in targets:
                for k in range(ky, ky + count):
                    row = self.rows_of(lx, y, to, k)
                    dx, dy, dz = (row[c] - mine[c] for c in range(3))
                    weight = jnp.exp2(-(dx * dx + dy * dy + dz * dz))
                    group[some, at : at + atoms] = weight.astype(bf16)
                    at += atoms
        total, at = None, 0
        for to, ky, count in targets:
            part = group[:, at : at + count * atoms]
            part = jnp.dot(part, self.near(to, y, ky, count), preferred_element_type=f32)
            total = part if total is None else total + part
            at += count * atoms
        return total

    def push(self, dots, sums, pushed, lx, y, grad, targets):
        atoms, at = self.atoms, 0
        for to, ky, count in targets:
            dots[:, at : at + count * atoms] = lax.dot_general(
                grad, self.near(to, y, ky, count), across, preferred_element_type=f32
            )
            at += count * atoms
        for start in range(0, atoms, lines):
            some = slice(start, start + lines)
            own = [None] * 3
            mine = self.mine(lx, y, some)
            at = 0
            for to, first, count in targets:
                for ky in range(first, first + count):
                    row = self.rows_of(lx, y, to, ky)
                    delta = [row[c] - mine[c] for c in range(3)]
                    square = delta[0] * delta[0] + delta[1] * delta[1] + delta[2] * delta[2]
                    strength = dots[some, at : at + atoms] * jnp.exp2(-square)
                    at += atoms
                    for c in range(3):
                        moved = strength * delta[c]
                        own[c] = moved if own[c] is None else own[c] + moved
                        pushed[c, to, y + ky] += jnp.sum(moved.reshape(lines // 8, 8, atoms), axis=0)
            for c in range(3):
                sums[c, y * atoms + start : y * atoms + start + lines] = own[c]

    def inside(self, y, rows):
        first, last = (1 if y == 0 else 0), (1 if y == self.rows_y - 1 else 2)
        return tuple((to, first, last + 1 - first) for to in rows)

    def outside(self, y, lx, other, ghost):
        targets = ((ghost, 0, 3),)
        for edge, ky in ((0, 0), (self.rows_y - 1, 2)):
            if y == edge:
                targets = targets + ((lx, ky, 1), (other, ky, 1))
        return targets

    def gathered(self, sums, c):
        total = row_sums(sums[c])
        return [total[:, y * self.atoms : (y + 1) * self.atoms] for y in range(self.rows_y)]

    def unit(self, c):
        unit = 1.0 / (coord_scale * radius * radius)
        return unit * self.sign if c == 0 else unit


def first_kernel(sizes, info, links, positions, occupied, embed, tail, sums_a, sums_b, tail_out, ext, tab, upright, group, sems):
    block = Block(sizes, info, links, ext, tab, sems)
    rows_y, atoms = block.rows_y, block.atoms
    block.fetch_own(embed)
    block.place_own(positions, occupied)
    block.spread(upright)
    tail_out[...] = tail[...]
    block.wait()
    for lx, out in ((1, sums_a), (2, sums_b)):
        for y in range(rows_y):
            total = block.describe(group.at[lx - 1, y], lx, y, block.inside(y, (1, 2)))
            out[y * atoms : (y + 1) * atoms] = total


def corner_kernel(atoms, tail, col_a, col_b, corner_a, corner_b):
    held = tail.shape[0] // 2
    for n, out in ((0, corner_a), (1, corner_b)):
        bins = slice(n * atoms, (n + 1) * atoms)
        out[0:atoms] = col_a[bins]
        out[atoms : 2 * atoms] = col_b[bins]
        at = 2 * atoms + held
        out[2 * atoms : at] = tail[n * held : (n + 1) * held]
        out[at : at + 16] = col_a[2 * atoms :]
        out[at + 16 : at + 32] = col_b[2 * atoms :]


def side_kernel(
    sizes, lx, other, ghost, info, links, positions, occupied, row, corner, col_a, col_b, sums_in,
    w_one_in, w_two_in, bias_one, w_out, pushed_out, edges_out, own_out, gradients, energy_out,
    ext, tab, upright, features, group, dots, own_sums, pushed, tails, sums, w_one, w_two, sems
):
    block = Block(sizes, info, links, ext, tab, sems)
    rows_y, atoms, cols = block.rows_y, block.atoms, block.cols
    block.fetch_row(ghost, row)
    block.fetch_cols(col_a, col_b)
    block.fetch_side(ghost, block.side_a, corner.at[pl.ds(0, atoms)])
    block.fetch_side(ghost, block.side_b, corner.at[pl.ds(atoms, atoms)])
    tail = 4 * rows_y
    block.fetch(corner.at[pl.ds(2 * atoms, tail + 32)], tails.at[pl.ds(0, tail + 32)])
    block.fetch(col_a.at[pl.ds(2 * atoms, 16)], tails.at[pl.ds(tail + 32, 16)])
    block.fetch(col_b.at[pl.ds(2 * atoms, 16)], tails.at[pl.ds(tail + 48, 16)])
    held = len(block.copies)
    for src, dst in ((sums_in, sums), (w_one_in, w_one), (w_two_in, w_two)):
        block.fetch(src, dst)
    block.place_own(positions, occupied)
    pushed[...] = jnp.zeros_like(pushed)
    block.wait(0, held)
    value = block.unpacked(tails[pl.ds(0, tail)])
    block.place_row(ghost, [value[rows_y * c : rows_y * (c + 1)] for c in range(4)])
    for n, side in enumerate((block.side_a, block.side_b)):
        value = block.unpacked(tails[pl.ds(tail + 16 * n, 16)])
        block.place_side(ghost, side, [value[4 * c + lx - 1 : 4 * c + lx] for c in range(4)])
    block.place_cols(tails[pl.ds(tail + 32, 16)], tails[pl.ds(tail + 48, 16)])
    block.spread(upright)

    block.wait(held)
    for y in range(rows_y):
        targets = block.outside(y, lx, other, ghost)
        rows = slice(y * atoms, (y + 1) * atoms)
        features[rows] = (sums[rows] + block.describe(group.at[y], lx, y, targets)).astype(bf16)

    bins = 4

    @pl.loop(0, rows_y // bins)
    def _(chunk):
        rows = pl.ds(pl.multiple_of(chunk * bins * atoms, bins * atoms), bins * atoms)
        inner = jnp.dot(features[rows], w_one[...], preferred_element_type=f32)
        act_one = jnp.tanh(inner + bias_one[...])
        act_two = jnp.tanh(jnp.dot(act_one.astype(bf16), w_two[...], preferred_element_type=f32))
        out = w_out[...]
        scaled = act_two * out
        half = scaled[:, :128]
        for start in range(128, scaled.shape[1], 128):
            half = half + scaled[:, start : start + 128]
        energy = row_sums(half)
        for b in range(bins):
            at = pl.ds(chunk * bins + b, 1)
            energy_out[at] = energy[:, b * atoms : (b + 1) * atoms] * occupied[block.home(lx), at]
        back_two = (out - scaled * act_two).astype(bf16)
        back_one = lax.dot_general(back_two, w_two[...], across, preferred_element_type=f32)
        back_one = (back_one * (1.0 - act_one * act_one)).astype(bf16)
        gradients[rows] = lax.dot_general(back_one, w_one[...], across, preferred_element_type=f32).astype(bf16)

    for y in range(rows_y):
        grad = gradients[y * atoms : (y + 1) * atoms]
        block.push(dots.at[y], own_sums, pushed, lx, y, grad, block.outside(y, lx, other, ghost))
    for c in range(3):
        for y, total in enumerate(block.gathered(own_sums, c)):
            own_out[c, y : y + 1] = total * -block.unit(c)

    for c in range(3):
        pushed_out[c] = jnp.sum(pushed[c, ghost], axis=1) * block.unit(c)
        for to in (1, 2):
            for n, at in enumerate((0, cols - 1)):
                total = jnp.sum(pushed[c, to, at], axis=0, keepdims=True)
                edges_out[c, 2 * n + to - 1 : 2 * n + to] = total * block.unit(c)


def last_kernel(sizes, lx, info, links, positions, occupied, embed, gradients, own_in, *refs):
    *refs, ext, tab, upright, dots, own_sums, pushed, sems = refs
    *before, grid_out, edges_out = refs if lx == 1 else refs + [None]
    block = Block(sizes, info, links, ext, tab, sems)
    rows_y, atoms = block.rows_y, block.atoms
    block.fetch_own(embed)
    block.place_own(positions, occupied)
    block.spread(upright)
    pushed[...] = jnp.zeros_like(pushed)
    block.wait()
    for y in range(rows_y):
        grad = gradients[y * atoms : (y + 1) * atoms]
        block.push(dots.at[y], own_sums, pushed, lx, y, grad, block.inside(y, (1, 2)))
    for c in range(3):
        for y, total in enumerate(block.gathered(own_sums, c)):
            pushed[c, lx, y + 1, 0:1] -= total
        for to in (1, 2):
            total = jnp.sum(pushed[c, to, 1 : rows_y + 1], axis=1) * block.unit(c)
            total = total + own_in[c] if to == lx else total
            if len(before) == 3:
                grid, from_a, from_b = before
                ghost = from_a if to == 1 else from_b
                grid_out[c, block.home(to)] = total + grid[c, to - 1] + ghost[c, pl.ds(1, rows_y)]
            else:
                grid_out[c, to - 1] = total
    if len(before) == 2:
        edges_out[...] = before[0][...] + before[1][...]


def body(positions, embed, counts, neighbours, w_one, bias_one, w_two, w_out):
    atoms = positions.shape[-1]
    rows_x, rows_y = counts.shape
    width, hidden = w_one.shape
    cols = rows_y + 2
    assert rows_x == 2 and atoms == 128
    rows = rows_y * atoms
    odd_x = lax.axis_index("gx") % 2
    odd_y = lax.axis_index("gy") % 2
    lines_of = embed.reshape(2, rows, width)
    row_b = pair_exchange(lax.dynamic_slice_in_dim(embed, odd_x, 1, 0), "gx", 1)
    occupied = (jnp.arange(atoms, dtype=jnp.int32) < counts[:, :, None]).astype(f32)
    coords = packed(jnp.concatenate([positions, occupied[None]], axis=0))
    order = jnp.where(odd_x == 1, coords, coords[:, ::-1])

    again, order = lax.optimization_barrier((embed, order))
    row_a = pair_exchange(lax.dynamic_slice_in_dim(again, 1 - odd_x, 1, 0), "gx", 0)
    later, row_a = lax.optimization_barrier((embed, row_a))
    later = later.reshape(2, rows, width)
    row_a, row_b = row_a.reshape(rows, width), row_b.reshape(rows, width)

    def col_message(y):
        low = [lax.dynamic_slice(later, (x, y * atoms, 0), (1, atoms, width))[0] for x in (1 - odd_x, odd_x)]
        tail = lax.dynamic_index_in_dim(order, y, 2, False)
        tail = jnp.concatenate([tail, tail], axis=1).reshape(16, width)
        return jnp.concatenate(low + [tail], axis=0)

    col_b = pair_exchange(col_message(odd_y * (rows_y - 1)), "gy", 1)
    col_a = pair_exchange(col_message((1 - odd_y) * (rows_y - 1)), "gy", 0)

    links = neighbours.reshape(-1)
    info = jnp.stack([odd_x, odd_y]).astype(jnp.int32)
    bias, out = bias_one.reshape(1, hidden), w_out.reshape(1, hidden)
    vmem = pl.BlockSpec(memory_space=pltpu.VMEM)
    smem = pl.BlockSpec(memory_space=pltpu.SMEM)
    hbm = pl.BlockSpec(memory_space=pl.ANY)
    sizes = (rows_y, atoms, width)
    params = pltpu.CompilerParams(vmem_limit_bytes=13 * 2**20)
    ext = pltpu.VMEM((4 * cols * atoms, width), bf16)
    tab = pltpu.VMEM((4, 4, 24, atoms), f32)
    upright = pltpu.VMEM((atoms, atoms), f32)
    own_sums = pltpu.VMEM((3, rows, atoms), f32)
    pushed = pltpu.VMEM((3, 4, cols, 8, atoms), f32)
    sems = pltpu.SemaphoreType.DMA((16,))
    sums = jax.ShapeDtypeStruct((rows, width), f32)
    tail = order.transpose(1, 0, 2, 3).reshape(8 * rows_y, width)
    sums_a, sums_b, tail = pl.pallas_call(
        functools.partial(first_kernel, sizes),
        out_shape=(sums, sums, jax.ShapeDtypeStruct(tail.shape, bf16)),
        in_specs=[smem, smem, vmem, vmem, hbm, vmem],
        out_specs=(vmem, vmem, vmem),
        scratch_shapes=[ext, tab, upright, pltpu.VMEM((2, rows_y, atoms, 6 * atoms), bf16), sems],
        compiler_params=params,
    )(info, links, positions, occupied, later, tail)


    corner = jax.ShapeDtypeStruct((2 * atoms + 4 * rows_y + 32, width), bf16)
    corner_a, corner_b = pl.pallas_call(
        functools.partial(corner_kernel, atoms), out_shape=(corner, corner), in_specs=[vmem] * 3, out_specs=(vmem, vmem),
        compiler_params=pltpu.CompilerParams(vmem_limit_bytes=2**21),
    )(tail, col_a, col_b)
    corner_b = pair_exchange(corner_b, "gx", 1)
    corner_a = pair_exchange(corner_a, "gx", 0)

    def side(lx, other, ghost, info, row, corner, sums):
        return pl.pallas_call(
            functools.partial(side_kernel, sizes, lx, other, ghost),
            out_shape=(
                jax.ShapeDtypeStruct((3, cols, atoms), f32),
                jax.ShapeDtypeStruct((3, 4, atoms), f32),
                jax.ShapeDtypeStruct((3, rows_y, atoms), f32),
                jax.ShapeDtypeStruct((rows, width), bf16),
                jax.ShapeDtypeStruct((rows_y, atoms), f32),
            ),
            in_specs=[smem, smem, vmem, vmem] + [hbm] * 7 + [vmem] * 2,
            out_specs=(vmem,) * 5,
            scratch_shapes=[
                ext, tab, upright, pltpu.VMEM((rows, width), bf16), pltpu.VMEM((rows_y, atoms, 5 * atoms), bf16),
                pltpu.VMEM((rows_y, atoms, 5 * atoms), f32), own_sums, pushed,
                pltpu.VMEM((4 * rows_y + 64, width), bf16),
                pltpu.VMEM((rows, width), f32), pltpu.VMEM(w_one.shape, bf16), pltpu.VMEM(w_two.shape, bf16), sems,
            ],
            compiler_params=params,
        )(info, links, positions, occupied, row, corner, col_a, col_b, sums, w_one, w_two, bias, out)

    pushed_a, edges_a, own_a, grad_a, energy_a = side(1, 2, 0, info, row_a, corner_a, sums_a)
    from_a = pair_exchange(pushed_a, "gx", 0)
    pushed_b, edges_b, own_b, grad_b, energy_b = side(2, 1, 3, info, row_b, corner_b, sums_b)
    from_b = pair_exchange(pushed_b, "gx", 1)
    inner_shape = jax.ShapeDtypeStruct((3, 2, rows_y, atoms), f32)
    edge_shape = jax.ShapeDtypeStruct((3, 4, atoms), f32)

    def inner(lx, gradients, own, *before):
        return pl.pallas_call(
            functools.partial(last_kernel, sizes, lx),
            out_shape=(inner_shape, edge_shape) if lx == 1 else inner_shape,
            in_specs=[smem, smem, vmem, vmem, hbm] + [vmem] * (2 + len(before)),
            out_specs=(vmem, vmem) if lx == 1 else vmem,
            scratch_shapes=[
                ext, tab, upright, pltpu.VMEM((rows_y, atoms, 6 * atoms), f32), own_sums, pushed, sems,
            ],
            compiler_params=params,
        )(info, links, positions, occupied, lines_of, gradients, own, *before)

    grid, edges = inner(1, grad_a, own_a, edges_a, edges_b)
    forces = inner(2, grad_b, own_b, grid, from_a, from_b)
    near_rows = jnp.stack([from_a, from_b], axis=1)
    first = edges[:, 0:2] + near_rows[:, :, 0]
    last = edges[:, 2:4] + near_rows[:, :, cols - 1]
    side_a = pair_exchange(jnp.where(odd_y == 1, first, last), "gy", 0)
    side_b = pair_exchange(jnp.where(odd_y == 1, last, first), "gy", 1)
    side_a, side_b = (jnp.where(odd_x == 1, side, side[:, ::-1]) for side in (side_a, side_b))
    forces = forces.at[:, :, 0].add(jnp.where(odd_y == 1, side_a, side_b))
    forces = forces.at[:, :, rows_y - 1].add(jnp.where(odd_y == 1, side_b, side_a))
    energy = jnp.where(odd_x == 1, jnp.stack([energy_a, energy_b]), jnp.stack([energy_b, energy_a]))
    return forces, energy


def solution(mesh):
    in_specs = (
        P(None, "gx", "gy", None),
        P("gx", "gy", None, None),
        P("gx", "gy"),
        P("gx", "gy", None),
        P(),
        P(),
        P(),
        P(),
    )
    out_specs = (P(None, "gx", "gy", None), P("gx", "gy", None))
    return jax.shard_map(body, mesh=mesh, in_specs=in_specs, out_specs=out_specs, check_vma=False)
```

time: 156 us -> 48.2 us (0.31)
  matrix products: 56.7 us -> 0 us
  other arithmetic: 32.5 us -> 1.7 us
  local copies, waits for them, and re-layouts: 30.2 us -> 4.97 us
  Pallas kernels: 0 us -> 25.1 us
  waiting for transfers between devices: 15.9 us -> 0.03 us
  starting transfers between devices: 17.9 us -> 15 us
    dot_general x21 -> x0, matrix products: 56.7 us -> none  [the longest x9 27.3 us: body(): jnp.einsum('bif,bjf->bij', gradients, remote_embed, preferred_element_typ...]
    pallas_call x0 -> x6, Pallas kernels: none -> 25.1 us  [the longest x2 13.3 us: side(): pl.pallas_call(functools.partial(side_kernel, sizes, lx, other, ghost), o...]
    gather x18 -> x0, local copies, waits for them, and re-layouts: 21.1 us -> none  [the longest x9 15.6 us: gather_bin(): return (remote[:3], remote[3], flat_embed[linked], shift_x, shift_y, linked)]
    ppermute x12 -> x10, waiting for transfers between devices: 15.9 us -> 0.03 us  [pair_exchange(): return lax.ppermute(value, axis, pairs)]
    add x20 -> x2, other arithmetic: 13.4 us -> 0.01 us  [the longest x1 0.01 us: body(): forces.at[:, :, rows_y - 1].add(jnp.where(odd_y == 1, side_b, side_a))]
    scatter-add x12 -> x0, other arithmetic: 11.2 us -> none  [the longest x9 10.1 us: body(): ghost_force = ghost_force.at[:, linked].add(pushed)]
    slice x15 -> x0, local copies, waits for them, and re-layouts: 6.45 us -> none  [the longest x9 5.02 us: pair_weights(): remote_pos[0][:, None, :]]
    ppermute x12 -> x10, starting transfers between devices: 17.9 us -> 15 us  [pair_exchange(): return lax.ppermute(value, axis, pairs)]
  transfers between devices with their start and end apart: 12 -> 10, of which waited for: 7 -> 0; matrix products, arithmetic and copies ran while one was open for 20% -> 4% of each run, Pallas kernels for 0% -> 52%
where the time goes in v2:
time: 48.2 us; the launch traced here: 47.9 us
  Pallas kernels  25.1 us (52%)
  starting transfers between devices  15 us (31%)
  local copies, waits for them, and re-layouts  4.97 us (10%)
  other arithmetic  1.7 us (4%)
  between operations  1.02 us (2%)
    ppermute x10, starting transfers between devices, pair_exchange(): return lax.ppermute(value, axis, pairs)  15 us
    pallas_call x2, Pallas kernels, side(): pl.pallas_call(functools.partial(side_kernel, sizes, lx, other, ghost), o...  13.3 us
    pallas_call x2, Pallas kernels, inner(): pl.pallas_call(functools.partial(last_kernel, sizes, lx), out_shape=(inne...  8.19 us
    pallas_call x1, Pallas kernels, body(): pl.pallas_call(functools.partial(first_kernel, sizes), out_shape=(sums, s...  3.64 us
    unnamed x21, local copies, waits for them, and re-layouts  2.12 us
    dynamic_slice x1, local copies, waits for them, and re-layouts, body(): lax.dynamic_slice_in_dim(again, 1 - odd_x, 1, 0)  1.08 us
  transfers between devices with their start and end apart: 10, of which 0 were waited for; matrix products, arithmetic and copies ran while one was open for 4% of the time, Pallas kernels for 52%

profile of v2, /device:TPU:0, one launch (start us, length us, event | category | flops | bytes accessed | tf_op | source)
XLA Modules:
  0.0 47.9 jit_solution(10912485277213031799)
XLA Ops:
  0.6 0.0 copy-start.1
  0.6 0.0 copy-start
  0.7 0.8 %fusion.2 = f32[1,2,8,128]{3,2,1,0:T(8,128)S(1)} fusion(s32[2,8]{1,0:T(2,128)} %param.14), kind=kLoop, calls=%fused_computation.17 | loop fusion | flops 4096 | bytes 8256 | tf_op jit(solution)/shard_map/convert_element_type | solution.py:345
  1.5 0.0 copy-done.1
  1.6 1.1 %constant_dynamic-slice_fusion.2 = bf16[1,8,128,256]{3,2,1,0:T(8,128)(2,1)S(1)} fusion(bf16[2,8,128,256]{3,2,1,0:T(8,128)(2,1)} %param.13, s32[]{:T(128)S(6)} %select_n.87), kind=kLoop, calls=%fused_computation.33 | loop fusion | bytes 1048580 | tf_op jit(solution)/shard_map/dynamic_slice | solution.py:350
  2.7 0.5 %collective-permute-start.1 = (bf16[1,8,128,256]{3,2,1,0:T(8,128)(2,1)S(1)}, bf16[1,8,128,256]{3,2,1,0:T(8,128)(2,1)S(1)}, u32[]{:S(2)}, u32[]{:S(2)}) collective-permute-start(bf16[1,8,128,256]{3,2,1,0:T(8,128)(2,1)S(1)} %constant_dynamic-slice_fusion.2), channel_id=1, source_target_pairs={{0,4},{4,0},{8,12},{12,8},{16,20},{20,16},{24,28},{28,24},{1,5},{5... | collective-permute-start | bytes 1572872 | tf_op jit(solution)/shard_map/ppermute | solution.py:26
  3.2 0.0 copy-done
  3.2 0.8 %constant_dynamic-slice_fusion.3 = bf16[1,8,128,256]{3,2,1,0:T(8,128)(2,1)} fusion(bf16[2,8,128,256]{3,2,1,0:T(8,128)(2,1)S(1)} %copy-done, s32[]{:T(128)S(6)} %select_n.84), kind=kLoop, calls=%fused_computation.34 | loop fusion | bytes 1048580 | tf_op jit(solution)/shard_map/dynamic_slice | solution.py:344
  4.0 4.7 %collective-permute-start = (bf16[1,8,128,256]{3,2,1,0:T(8,128)(2,1)}, bf16[1,8,128,256]{3,2,1,0:T(8,128)(2,1)S(1)}, u32[]{:S(2)}, u32[]{:S(2)}) collective-permute-start(bf16[1,8,128,256]{3,2,1,0:T(8,128)(2,1)} %constant_dynamic-slice_fusion.3), channel_id=1, source_target_pairs={{4,8},{8,4},{12,16},{16,12},{20,24},{24,20},{28,0},{0,28},{5,9},{9... | collective-permute-start | bytes 1572872 | tf_op jit(solution)/shard_map/ppermute | solution.py:26
  8.9 0.0 collective-permute-done.1
  8.9 1.6 %collective-permute-start.2 = (bf16[272,256]{1,0:T(8,128)(2,1)S(1)}, bf16[272,256]{1,0:T(8,128)(2,1)S(1)}, u32[]{:S(2)}, u32[]{:S(2)}) collective-permute-start(bf16[272,256]{1,0:T(8,128)(2,1)S(1)} %pad_maximum_fusion), channel_id=1, source_target_pairs={{0,1},{1,0},{2,3},{3,2},{4,5},{5,4},{6,7},{7,6},{8,9},{9,8},{10,11... | collective-permute-start | bytes 417800 | tf_op jit(solution)/shard_map/ppermute | solution.py:26
  10.5 1.6 %collective-permute-start.3 = (bf16[272,256]{1,0:T(8,128)(2,1)S(1)}, bf16[272,256]{1,0:T(8,128)(2,1)S(1)}, u32[]{:S(2)}, u32[]{:S(2)}) collective-permute-start(bf16[272,256]{1,0:T(8,128)(2,1)S(1)} %pad_maximum_fusion.1), channel_id=1, source_target_pairs={{1,2},{2,1},{3,0},{0,3},{5,6},{6,5},{7,4},{4,7},{9,10},{10,9},{11,... | collective-permute-start | bytes 417800 | tf_op jit(solution)/shard_map/ppermute | solution.py:26
  12.1 0.0 copy-done.9
  12.1 0.1 fusion.1.occupied
  12.1 0.7 %copy-done.8 = s32[2,8,9]{2,1,0:T(8,128)S(1)} copy-done((s32[2,8,9]{2,1,0:T(8,128)S(1)}, s32[2,8,9]{2,1,0:T(8,128)}, u32[]{:S(2)}) %copy-start.8) | copy-done | bytes 600
  12.8 0.1 reshape.116.links
  12.9 0.1 pad_add_fusion.info
  13.0 3.6 %shard_map.95 = (f32[1024,256]{1,0:T(8,128)S(1)}, f32[1024,256]{1,0:T(8,128)S(1)}, bf16[64,256]{1,0:T(8,128)(2,1)S(1)}) custom-call(s32[2]{0:T(128)S(1)} %pad_add_fusion.info, s32[144]{0:T(256)S(1)} %reshape.116.links, f32[3,2,8,128]{3,2,1,0:T(8,128)S(1)} %copy-done.1, f32[2,8,128]{2,1,0:T(8,128)S(1)} %fusion.1.occupied, bf16[2,1024,256]{2,1,0:T(8,128)(2,1)S(1)} %bitcast.44, ...), custom_call_target="tpu_custom_call" | custom-call | tf_op jit(solution)/shard_map/pallas_call | solution.py:380
  16.6 0.0 collective-permute-done.2.col_a
  16.7 0.0 collective-permute-done.3.col_b
  16.7 0.0 copy-start.2
  16.7 0.0 copy-start.3
  16.7 0.0 copy-start.5
  16.7 0.1 collective-permute-start.5
  16.8 2.8 %collective-permute-start.4 = (bf16[320,256]{1,0:T(8,128)(2,1)S(1)}, bf16[320,256]{1,0:T(8,128)(2,1)S(1)}, u32[]{:S(2)}, u32[]{:S(2)}) collective-permute-start(bf16[320,256]{1,0:T(8,128)(2,1)S(1)} %get-tuple-element.51), channel_id=1, source_target_pairs={{4,8},{8,4},{12,16},{16,12},{20,24},{24,20},{28,0},{0,28},{5,9},{9... | collective-permute-start | bytes 491528 | tf_op jit(solution)/shard_map/ppermute | solution.py:26
  19.7 0.0 collective-permute-done.5.corner
  19.7 0.0 copy-done.2
  19.7 0.7 %copy-done.4 = f32[256]{0:T(256)S(1)} copy-done((f32[256]{0:T(256)S(1)}, f32[256]{0:T(256)}, u32[]{:S(2)}) %copy-start.4) | copy-done | bytes 1048
  20.3 6.6 %shard_map.98 = (f32[3,10,128]{2,1,0:T(8,128)S(1)}, f32[3,4,128]{2,1,0:T(4,128)S(1)}, f32[3,8,128]{2,1,0:T(8,128)S(1)}, bf16[1024,256]{1,0:T(8,128)(2,1)S(1)}, f32[8,128]{1,0:T(8,128)S(1)}) custom-call(s32[2]{0:T(128)S(1)} %pad_add_fusion.info, s32[144]{0:T(256)S(1)} %reshape.116.links, f32[3,2,8,128]{3,2,1,0:T(8,128)S(1)} %copy-done.1, ...), custom_call_target="tpu_custom_call" | custom-call | tf_op jit(solution)/shard_map/pallas_call | solution.py:399
  27.0 0.1 collective-permute-start.6
  27.1 0.0 collective-permute-done
  27.1 0.0 collective-permute-done.4.corner
  27.1 6.6 %shard_map.97 = (f32[3,10,128]{2,1,0:T(8,128)S(1)}, f32[3,4,128]{2,1,0:T(4,128)S(1)}, f32[3,8,128]{2,1,0:T(8,128)S(1)}, bf16[1024,256]{1,0:T(8,128)(2,1)S(1)}, f32[8,128]{1,0:T(8,128)S(1)}) custom-call(s32[2]{0:T(128)S(1)} %pad_add_fusion.info, s32[144]{0:T(256)S(1)} %reshape.116.links, f32[3,2,8,128]{3,2,1,0:T(8,128)S(1)} %copy-done.1, ...), custom_call_target="tpu_custom_call" | custom-call | tf_op jit(solution)/shard_map/pallas_call | solution.py:399
  33.7 1.4 %collective-permute-start.7 = (f32[3,10,128]{2,1,0:T(8,128)S(1)}, f32[3,10,128]{2,1,0:T(8,128)S(1)}, u32[]{:S(2)}, u32[]{:S(2)}) collective-permute-start(f32[3,10,128]{2,1,0:T(8,128)S(1)} %get-tuple-element.64), channel_id=1, source_target_pairs={{4,8},{8,4},{12,16},{16,12},{20,24},{24,20},{28,0},{0,28},{5,9},{9... | collective-permute-start | bytes 46088 | tf_op jit(solution)/shard_map/ppermute | solution.py:26
  35.2 3.9 %shard_map.99 = (f32[3,2,8,128]{3,2,1,0:T(8,128)S(1)}, f32[3,4,128]{2,1,0:T(4,128)S(1)}) custom-call(s32[2]{0:T(128)S(1)} %pad_add_fusion.info, s32[144]{0:T(256)S(1)} %reshape.116.links, f32[3,2,8,128]{3,2,1,0:T(8,128)S(1)} %copy-done.1, f32[2,8,128]{2,1,0:T(8,128)S(1)} %fusion.1.occupied, bf16[2,1024,256]{2,1,0:T(8,128)(2,1)S(1)} %bitcast.45, ...), custom_call_target="tpu_custom_call" | custom-call | tf_op jit(solution)/shard_map/pallas_call | solution.py:427
  39.1 0.0 collective-permute-done.6.refs_1_
  39.1 0.0 collective-permute-done.7.refs_2_
  39.1 1.6 %collective-permute-start.8 = (f32[3,2,128]{2,1,0:T(2,128)S(1)}, f32[3,2,128]{2,1,0:T(2,128)S(1)}, u32[]{:S(2)}, u32[]{:S(2)}) collective-permute-start(f32[3,2,128]{2,1,0:T(2,128)S(1)} %get-tuple-element.81), channel_id=1, source_target_pairs={{0,1},{1,0},{2,3},{3,2},{4,5},{5,4},{6,7},{7,6},{8,9},{9,8},{10,11... | collective-permute-start | bytes 9224 | tf_op jit(solution)/shard_map/ppermute | solution.py:26
  40.7 0.7 %collective-permute-start.9 = (f32[3,2,128]{2,1,0:T(2,128)S(1)}, f32[3,2,128]{2,1,0:T(2,128)S(1)}, u32[]{:S(2)}, u32[]{:S(2)}) collective-permute-start(f32[3,2,128]{2,1,0:T(2,128)S(1)} %get-tuple-element.80), channel_id=1, source_target_pairs={{1,2},{2,1},{3,0},{0,3},{5,6},{6,5},{7,4},{4,7},{9,10},{10,9},{11,... | collective-permute-start | bytes 9224 | tf_op jit(solution)/shard_map/ppermute | solution.py:26
  41.4 0.6 %maximum_select_fusion = f32[2,8,128]{2,1,0:T(8,128)} fusion(f32[1,8,128]{2,1,0:T(8,128)S(1)} %bitcast.57, f32[1,8,128]{2,1,0:T(8,128)S(1)} %bitcast.56, pred[]{:T(512)S(6)} %eq.7), kind=kLoop, calls=%fused_computation.13 | loop fusion | flops 6144 | bytes 16385 | tf_op jit(solution)/shard_map/jit(_where)/select_n | solution.py:448
  42.0 4.3 %shard_map.100 = f32[3,2,8,128]{3,2,1,0:T(8,128)} custom-call(s32[2]{0:T(128)S(1)} %pad_add_fusion.info, s32[144]{0:T(256)S(1)} %reshape.116.links, f32[3,2,8,128]{3,2,1,0:T(8,128)S(1)} %copy-done.1, f32[2,8,128]{2,1,0:T(8,128)S(1)} %fusion.1.occupied, bf16[2,1024,256]{2,1,0:T(8,128)(2,1)S(1)} %bitcast.46, ...), custom_call_target="tpu_custom_call" | custom-call | tf_op jit(solution)/shard_map/pallas_call | solution.py:427
  46.3 0.0 collective-permute-done.8
  46.4 0.0 copy-start.6
  46.4 0.0 collective-permute-done.9
  46.4 0.6 %slice-done = f32[3,2,1,128]{3,2,1,0:T(1,128)S(1)} async-done(((f32[3,2,8,128]{3,2,1,0:T(8,128)}), f32[3,2,1,128]{3,2,1,0:T(1,128)S(1)}, s32[]{:S(2)}) %slice-start) | async-done | bytes 3096 | tf_op jit(solution)/shard_map/slice.52
  47.0 0.1 copy-done.6
  47.3 0.0 copy-start.7
  47.3 0.6 %copy-done.7 = f32[3,2,8,128]{3,2,1,0:T(8,128)} copy-done((f32[3,2,8,128]{3,2,1,0:T(8,128)}, f32[3,2,8,128]{3,2,1,0:T(8,128)S(1)}, u32[]{:S(2)}) %copy-start.7) | copy-done | bytes 24600
  (30 shorter events, 0.4 us)
Async XLA Ops:
  0.6 0.9 %copy-start.1 = (f32[3,2,8,128]{3,2,1,0:T(8,128)S(1)}, f32[3,2,8,128]{3,2,1,0:T(8,128)}, u32[]{:S(2)}) copy-start(f32[3,2,8,128]{3,2,1,0:T(8,128)} %positions.9) | copy-start | bytes 73732
  0.6 2.5 %copy-start = (bf16[2,8,128,256]{3,2,1,0:T(8,128)(2,1)S(1)}, bf16[2,8,128,256]{3,2,1,0:T(8,128)(2,1)}, u32[]{:S(2)}) copy-start(bf16[2,8,128,256]{3,2,1,0:T(8,128)(2,1)} %param.13) | copy-start | bytes 3145732
  2.7 6.2 %collective-permute-start.1 = (bf16[1,8,128,256]{3,2,1,0:T(8,128)(2,1)S(1)}, bf16[1,8,128,256]{3,2,1,0:T(8,128)(2,1)S(1)}, u32[]{:S(2)}, u32[]{:S(2)}) collective-permute-start(bf16[1,8,128,256]{3,2,1,0:T(8,128)(2,1)S(1)} %constant_dynamic-slice_fusion.2), channel_id=1, source_target_pairs={{0,4},{4,0},{8,12},{12,8},{16,20},{20,16},{24,28},{28,24},{1,5},{5... | collective-permute-start | bytes 1572872 | tf_op jit(solution)/shard_map/ppermute | solution.py:26
  4.0 23.1 %collective-permute-start = (bf16[1,8,128,256]{3,2,1,0:T(8,128)(2,1)}, bf16[1,8,128,256]{3,2,1,0:T(8,128)(2,1)S(1)}, u32[]{:S(2)}, u32[]{:S(2)}) collective-permute-start(bf16[1,8,128,256]{3,2,1,0:T(8,128)(2,1)} %constant_dynamic-slice_fusion.3), channel_id=1, source_target_pairs={{4,8},{8,4},{12,16},{16,12},{20,24},{24,20},{28,0},{0,28},{5,9},{9... | collective-permute-start | bytes 1572872 | tf_op jit(solution)/shard_map/ppermute | solution.py:26
  8.9 7.7 %collective-permute-start.2 = (bf16[272,256]{1,0:T(8,128)(2,1)S(1)}, bf16[272,256]{1,0:T(8,128)(2,1)S(1)}, u32[]{:S(2)}, u32[]{:S(2)}) collective-permute-start(bf16[272,256]{1,0:T(8,128)(2,1)S(1)} %pad_maximum_fusion), channel_id=1, source_target_pairs={{0,1},{1,0},{2,3},{3,2},{4,5},{5,4},{6,7},{7,6},{8,9},{9,8},{10,11... | collective-permute-start | bytes 417800 | tf_op jit(solution)/shard_map/ppermute | solution.py:26
  10.5 1.6 %copy-start.9 = (s32[2,8]{1,0:T(2,128)S(1)}, s32[2,8]{1,0:T(2,128)}, u32[]{:S(2)}) copy-start(s32[2,8]{1,0:T(2,128)} %param.14) | copy-start | bytes 196
  10.5 6.2 %collective-permute-start.3 = (bf16[272,256]{1,0:T(8,128)(2,1)S(1)}, bf16[272,256]{1,0:T(8,128)(2,1)S(1)}, u32[]{:S(2)}, u32[]{:S(2)}) collective-permute-start(bf16[272,256]{1,0:T(8,128)(2,1)S(1)} %pad_maximum_fusion.1), channel_id=1, source_target_pairs={{1,2},{2,1},{3,0},{0,3},{5,6},{6,5},{7,4},{4,7},{9,10},{10,9},{11,... | collective-permute-start | bytes 417800 | tf_op jit(solution)/shard_map/ppermute | solution.py:26
  12.1 0.7 %copy-start.8 = (s32[2,8,9]{2,1,0:T(8,128)S(1)}, s32[2,8,9]{2,1,0:T(8,128)}, u32[]{:S(2)}) copy-start(s32[2,8,9]{2,1,0:T(8,128)} %param.15) | copy-start | bytes 1732
  16.7 3.0 %copy-start.2 = (bf16[256,256]{1,0:T(8,128)(2,1)S(1)}, bf16[256,256]{1,0:T(8,128)(2,1)}, u32[]{:S(2)}) copy-start(bf16[256,256]{1,0:T(8,128)(2,1)} %w_one_in.3) | copy-start | bytes 393220
  16.7 3.0 %copy-start.3 = (bf16[256,256]{1,0:T(8,128)(2,1)S(1)}, bf16[256,256]{1,0:T(8,128)(2,1)}, u32[]{:S(2)}) copy-start(bf16[256,256]{1,0:T(8,128)(2,1)} %w_two_in.3) | copy-start | bytes 393220
  16.7 3.0 %copy-start.5 = (f32[256]{0:T(256)S(1)}, f32[256]{0:T(256)}, u32[]{:S(2)}) copy-start(f32[256]{0:T(256)} %param.19) | copy-start | bytes 3076
  16.7 2.9 %collective-permute-start.5 = (bf16[320,256]{1,0:T(8,128)(2,1)S(1)}, bf16[320,256]{1,0:T(8,128)(2,1)S(1)}, u32[]{:S(2)}, u32[]{:S(2)}) collective-permute-start(bf16[320,256]{1,0:T(8,128)(2,1)S(1)} %get-tuple-element.56), channel_id=1, source_target_pairs={{0,4},{4,0},{8,12},{12,8},{16,20},{20,16},{24,28},{28,24},{1,5},{5... | collective-permute-start | bytes 491528 | tf_op jit(solution)/shard_map/ppermute | solution.py:26
  16.8 10.3 %collective-permute-start.4 = (bf16[320,256]{1,0:T(8,128)(2,1)S(1)}, bf16[320,256]{1,0:T(8,128)(2,1)S(1)}, u32[]{:S(2)}, u32[]{:S(2)}) collective-permute-start(bf16[320,256]{1,0:T(8,128)(2,1)S(1)} %get-tuple-element.51), channel_id=1, source_target_pairs={{4,8},{8,4},{12,16},{16,12},{20,24},{24,20},{28,0},{0,28},{5,9},{9... | collective-permute-start | bytes 491528 | tf_op jit(solution)/shard_map/ppermute | solution.py:26
  19.7 0.7 %copy-start.4 = (f32[256]{0:T(256)S(1)}, f32[256]{0:T(256)}, u32[]{:S(2)}) copy-start(f32[256]{0:T(256)} %param.17) | copy-start | bytes 3076
  27.0 12.1 %collective-permute-start.6 = (f32[3,10,128]{2,1,0:T(8,128)S(1)}, f32[3,10,128]{2,1,0:T(8,128)S(1)}, u32[]{:S(2)}, u32[]{:S(2)}) collective-permute-start(f32[3,10,128]{2,1,0:T(8,128)S(1)} %get-tuple-element.63), channel_id=1, source_target_pairs={{0,4},{4,0},{8,12},{12,8},{16,20},{20,16},{24,28},{28,24},{1,5},{5... | collective-permute-start | bytes 46088 | tf_op jit(solution)/shard_map/ppermute | solution.py:26
  33.7 5.3 %collective-permute-start.7 = (f32[3,10,128]{2,1,0:T(8,128)S(1)}, f32[3,10,128]{2,1,0:T(8,128)S(1)}, u32[]{:S(2)}, u32[]{:S(2)}) collective-permute-start(f32[3,10,128]{2,1,0:T(8,128)S(1)} %get-tuple-element.64), channel_id=1, source_target_pairs={{4,8},{8,4},{12,16},{16,12},{20,24},{24,20},{28,0},{0,28},{5,9},{9... | collective-permute-start | bytes 46088 | tf_op jit(solution)/shard_map/ppermute | solution.py:26
  39.1 7.2 %collective-permute-start.8 = (f32[3,2,128]{2,1,0:T(2,128)S(1)}, f32[3,2,128]{2,1,0:T(2,128)S(1)}, u32[]{:S(2)}, u32[]{:S(2)}) collective-permute-start(f32[3,2,128]{2,1,0:T(2,128)S(1)} %get-tuple-element.81), channel_id=1, source_target_pairs={{0,1},{1,0},{2,3},{3,2},{4,5},{5,4},{6,7},{7,6},{8,9},{9,8},{10,11... | collective-permute-start | bytes 9224 | tf_op jit(solution)/shard_map/ppermute | solution.py:26
  40.7 5.7 %collective-permute-start.9 = (f32[3,2,128]{2,1,0:T(2,128)S(1)}, f32[3,2,128]{2,1,0:T(2,128)S(1)}, u32[]{:S(2)}, u32[]{:S(2)}) collective-permute-start(f32[3,2,128]{2,1,0:T(2,128)S(1)} %get-tuple-element.80), channel_id=1, source_target_pairs={{1,2},{2,1},{3,0},{0,3},{5,6},{6,5},{7,4},{4,7},{9,10},{10,9},{11,... | collective-permute-start | bytes 9224 | tf_op jit(solution)/shard_map/ppermute | solution.py:26
  46.3 0.7 %slice-start = ((f32[3,2,8,128]{3,2,1,0:T(8,128)}), f32[3,2,1,128]{3,2,1,0:T(1,128)S(1)}, s32[]{:S(2)}) async-start(f32[3,2,8,128]{3,2,1,0:T(8,128)} %shard_map.100), calls=%async_computation | async-start | bytes 6144 | tf_op jit(solution)/shard_map/slice.52
  46.4 0.8 %copy-start.6 = (f32[3,2,8,128]{3,2,1,0:T(8,128)S(1)}, f32[3,2,8,128]{3,2,1,0:T(8,128)}, u32[]{:S(2)}) copy-start(f32[3,2,8,128]{3,2,1,0:T(8,128)} %shard_map.100) | copy-start | bytes 73732
  47.3 0.6 %copy-start.7 = (f32[3,2,8,128]{3,2,1,0:T(8,128)}, f32[3,2,8,128]{3,2,1,0:T(8,128)S(1)}, u32[]{:S(2)}) copy-start(f32[3,2,8,128]{3,2,1,0:T(8,128)S(1)} %scatter-add.9) | copy-start | bytes 73732

commit v3 on v2

--- a/solution.py
+++ b/solution.py
@@ -15,6 +15,7 @@
 bf16 = jnp.bfloat16
 across = (((1,), (1,)), ((), ()))
 lead = 7
+bins = 8
 lines = 32
 
 
@@ -43,15 +44,15 @@
 
 
 class Block:
-    def __init__(self, sizes, info, links, ext, tab, sems):
+    def __init__(self, sizes, info, links, tab, near, sems=None):
         self.rows_y, self.atoms, self.width = sizes
         self.cols = self.rows_y + 2
         self.odd_x, self.odd_y = info[0], info[1]
         self.sign = jnp.where(self.odd_x == 1, 1.0, -1.0).astype(f32)
         self.side_a = jnp.where(self.odd_y == 1, 0, self.cols - 1)
         self.side_b = self.cols - 1 - self.side_a
-        self.links, self.ext, self.tab, self.sems = links, ext, tab, sems
-        self.copies = []
+        self.links, self.tab, self.near, self.sems = links, tab, near, sems
+        self.copies, self.written = [], set()
 
     def home(self, lx):
         return 1 - self.odd_x if lx == 1 else self.odd_x
@@ -64,26 +65,6 @@
     def wait(self, start=0, end=None):
         for copy in self.copies[start:end]:
             copy.wait()
-
-    def bins_at(self, slot, count):
-        at = pl.multiple_of(slot * self.atoms, self.atoms)
-        return self.ext.at[pl.ds(at, count * self.atoms)]
-
-    def fetch_row(self, lx, src):
-        self.fetch(src, self.bins_at(lx * self.cols + 1, self.rows_y))
-
-    def fetch_side(self, lx, side, src):
-        self.fetch(src, self.bins_at(lx * self.cols + side, 1))
-
-    def fetch_own(self, embed):
-        for lx in (1, 2):
-            self.fetch_row(lx, embed.at[self.home(lx)])
-
-    def fetch_cols(self, col_a, col_b):
-        for lx in (1, 2):
-            rows = pl.ds((lx - 1) * self.atoms, self.atoms)
-            self.fetch_side(lx, self.side_a, col_a.at[rows])
-            self.fetch_side(lx, self.side_b, col_b.at[rows])
 
     def store(self, lx, rows, y, value):
         there = value[3] > 0.5
@@ -129,15 +110,12 @@
     def rows_of(self, lx, y, to, ky):
         kx = to - lx + 1
         list_x = jnp.where(self.odd_x == 1, kx, 2 - kx)
-        link = self.links[(self.home(lx) * self.rows_y + y) * 9 + list_x * 3 + ky]
+        link = self.links[self.home(lx), y, list_x * 3 + ky]
         at = pl.ds(lead + y + ky, 1)
         z = jnp.where(link < 4 * self.cols, self.tab[2, to, at], -far)
         return self.tab[0, to, at], self.tab[1, to, at], z
 
-    def near(self, to, y, ky, count):
-        return self.bins_at(to * self.cols + y + ky, count)[...]
-
-    def describe(self, group, lx, y, targets):
+    def weigh(self, group, lx, y, targets):
         atoms = self.atoms
         for start in range(0, atoms, lines):
             some = slice(start, start + lines)
@@ -150,21 +128,27 @@
                     weight = jnp.exp2(-(dx * dx + dy * dy + dz * dz))
                     group[some, at : at + atoms] = weight.astype(bf16)
                     at += atoms
+
+    def describe(self, group, lx, y, targets):
+        atoms = self.atoms
         total, at = None, 0
         for to, ky, count in targets:
             part = group[:, at : at + count * atoms]
-            part = jnp.dot(part, self.near(to, y, ky, count), preferred_element_type=f32)
+            part = jnp.dot(part, self.near(self, to, y, ky, count), preferred_element_type=f32)
             total = part if total is None else total + part
             at += count * atoms
         return total
 
-    def push(self, dots, sums, pushed, lx, y, grad, targets):
+    def project(self, dots, y, grad, targets):
         atoms, at = self.atoms, 0
         for to, ky, count in targets:
             dots[:, at : at + count * atoms] = lax.dot_general(
-                grad, self.near(to, y, ky, count), across, preferred_element_type=f32
+                grad, self.near(self, to, y, ky, count), across, preferred_element_type=f32
             )
             at += count * atoms
+
+    def push(self, dots, group, sums, pushed, lx, y, targets):
+        atoms = self.atoms
         for start in range(0, atoms, lines):
             some = slice(start, start + lines)
             own = [None] * 3
@@ -174,13 +158,21 @@
                 for ky in range(first, first + count):
                     row = self.rows_of(lx, y, to, ky)
                     delta = [row[c] - mine[c] for c in range(3)]
-                    square = delta[0] * delta[0] + delta[1] * delta[1] + delta[2] * delta[2]
-                    strength = dots[some, at : at + atoms] * jnp.exp2(-square)
+                    if group is None:
+                        square = delta[0] * delta[0] + delta[1] * delta[1] + delta[2] * delta[2]
+                        weight = jnp.exp2(-square)
+                    else:
+                        weight = group[some, at : at + atoms].astype(f32)
+                    strength = dots[some, at : at + atoms] * weight
                     at += atoms
                     for c in range(3):
                         moved = strength * delta[c]
                         own[c] = moved if own[c] is None else own[c] + moved
-                        pushed[c, to, y + ky] += jnp.sum(moved.reshape(lines // 8, 8, atoms), axis=0)
+                        total = jnp.sum(moved.reshape(lines // 8, 8, atoms), axis=0)
+                        if (c, to, y + ky) in self.written:
+                            total = total + pushed[c, to, y + ky]
+                        self.written.add((c, to, y + ky))
+                        pushed[c, to, y + ky] = total
             for c in range(3):
                 sums[c, y * atoms + start : y * atoms + start + lines] = own[c]
 
@@ -189,11 +181,11 @@
         return tuple((to, first, last + 1 - first) for to in rows)
 
     def outside(self, y, lx, other, ghost):
-        targets = ((ghost, 0, 3),)
-        for edge, ky in ((0, 0), (self.rows_y - 1, 2)):
-            if y == edge:
-                targets = targets + ((lx, ky, 1), (other, ky, 1))
-        return targets
+        if y == 0:
+            return ((ghost, 0, 1), (ghost, 1, 2), (lx, 0, 1), (other, 0, 1))
+        if y == self.rows_y - 1:
+            return ((ghost, 0, 2), (ghost, 2, 1), (lx, 2, 1), (other, 2, 1))
+        return ((ghost, 0, 3),)
 
     def gathered(self, sums, c):
         total = row_sums(sums[c])
@@ -204,16 +196,25 @@
         return unit * self.sign if c == 0 else unit
 
 
-def first_kernel(sizes, info, links, positions, occupied, embed, tail, sums_a, sums_b, tail_out, ext, tab, upright, group, sems):
-    block = Block(sizes, info, links, ext, tab, sems)
+def own_near(embed):
+    def near(block, to, y, ky, count):
+        first = (y + ky - 1) * block.atoms
+        return embed[block.home(to), first : first + count * block.atoms]
+
+    return near
+
+
+def first_kernel(
+    sizes, info, links, positions, occupied, embed, tail, sums_a, sums_b, tail_out, group, tab, upright
+):
+    block = Block(sizes, info, links, tab, own_near(embed))
     rows_y, atoms = block.rows_y, block.atoms
-    block.fetch_own(embed)
     block.place_own(positions, occupied)
     block.spread(upright)
     tail_out[...] = tail[...]
-    block.wait()
     for lx, out in ((1, sums_a), (2, sums_b)):
         for y in range(rows_y):
+            block.weigh(group.at[lx - 1, y], lx, y, block.inside(y, (1, 2)))
             total = block.describe(group.at[lx - 1, y], lx, y, block.inside(y, (1, 2)))
             out[y * atoms : (y + 1) * atoms] = total
 
@@ -231,45 +232,45 @@
 
 
 def side_kernel(
-    sizes, lx, other, ghost, info, links, positions, occupied, row, corner, col_a, col_b, sums_in,
-    w_one_in, w_two_in, bias_one, w_out, pushed_out, edges_out, own_out, gradients, energy_out,
-    ext, tab, upright, features, group, dots, own_sums, pushed, tails, sums, w_one, w_two, sems
+    sizes, lx, other, ghost, info, links, positions, occupied, row_in, corner, col_a, col_b, sums,
+    w_one_in, w_two_in, bias_in, out_in, pushed_out, edges_out, own_out, gradients, energy_out,
+    row, tab, upright, features, group, dots, own_sums, pushed, w_one, w_two, bias_one, w_out, sems
 ):
-    block = Block(sizes, info, links, ext, tab, sems)
+    def near(block, to, y, ky, count):
+        atoms, odd, slot = block.atoms, block.odd_y == 1, y + ky
+        left = slot == 0
+        if to == ghost and (left or slot == block.cols - 1):
+            first = jnp.where(odd, 0 if left else atoms, atoms if left else 0)
+            return corner[pl.ds(pl.multiple_of(first, atoms), atoms)]
+        if to == ghost:
+            return row[(slot - 1) * atoms : (slot - 1 + count) * atoms]
+        rows = slice((to - 1) * atoms, to * atoms)
+        return jnp.where(odd == left, col_a[rows], col_b[rows])
+
+    block = Block(sizes, info, links, tab, near, sems)
     rows_y, atoms, cols = block.rows_y, block.atoms, block.cols
-    block.fetch_row(ghost, row)
-    block.fetch_cols(col_a, col_b)
-    block.fetch_side(ghost, block.side_a, corner.at[pl.ds(0, atoms)])
-    block.fetch_side(ghost, block.side_b, corner.at[pl.ds(atoms, atoms)])
-    tail = 4 * rows_y
-    block.fetch(corner.at[pl.ds(2 * atoms, tail + 32)], tails.at[pl.ds(0, tail + 32)])
-    block.fetch(col_a.at[pl.ds(2 * atoms, 16)], tails.at[pl.ds(tail + 32, 16)])
-    block.fetch(col_b.at[pl.ds(2 * atoms, 16)], tails.at[pl.ds(tail + 48, 16)])
-    held = len(block.copies)
-    for src, dst in ((sums_in, sums), (w_one_in, w_one), (w_two_in, w_two)):
+    for src, dst in ((row_in, row), (w_one_in, w_one), (w_two_in, w_two), (bias_in, bias_one), (out_in, w_out)):
         block.fetch(src, dst)
     block.place_own(positions, occupied)
-    pushed[...] = jnp.zeros_like(pushed)
-    block.wait(0, held)
-    value = block.unpacked(tails[pl.ds(0, tail)])
+    at = 2 * atoms
+    value = block.unpacked(corner[at : at + 4 * rows_y])
     block.place_row(ghost, [value[rows_y * c : rows_y * (c + 1)] for c in range(4)])
+    at += 4 * rows_y
     for n, side in enumerate((block.side_a, block.side_b)):
-        value = block.unpacked(tails[pl.ds(tail + 16 * n, 16)])
+        value = block.unpacked(corner[at + 16 * n : at + 16 * (n + 1)])
         block.place_side(ghost, side, [value[4 * c + lx - 1 : 4 * c + lx] for c in range(4)])
-    block.place_cols(tails[pl.ds(tail + 32, 16)], tails[pl.ds(tail + 48, 16)])
+    block.place_cols(col_a[2 * atoms :], col_b[2 * atoms :])
     block.spread(upright)
 
-    block.wait(held)
+    targets = [block.outside(y, lx, other, ghost) for y in range(rows_y)]
     for y in range(rows_y):
-        targets = block.outside(y, lx, other, ghost)
-        rows = slice(y * atoms, (y + 1) * atoms)
-        features[rows] = (sums[rows] + block.describe(group.at[y], lx, y, targets)).astype(bf16)
-
-    bins = 4
-
-    @pl.loop(0, rows_y // bins)
-    def _(chunk):
-        rows = pl.ds(pl.multiple_of(chunk * bins * atoms, bins * atoms), bins * atoms)
+        block.weigh(group.at[y], lx, y, targets[y])
+    block.wait()
+    for first in range(0, rows_y, bins):
+        for y in range(first, first + bins):
+            rows = slice(y * atoms, (y + 1) * atoms)
+            features[rows] = (sums[rows] + block.describe(group.at[y], lx, y, targets[y])).astype(bf16)
+        rows = slice(first * atoms, (first + bins) * atoms)
         inner = jnp.dot(features[rows], w_one[...], preferred_element_type=f32)
         act_one = jnp.tanh(inner + bias_one[...])
         act_two = jnp.tanh(jnp.dot(act_one.astype(bf16), w_two[...], preferred_element_type=f32))
@@ -280,16 +281,16 @@
             half = half + scaled[:, start : start + 128]
         energy = row_sums(half)
         for b in range(bins):
-            at = pl.ds(chunk * bins + b, 1)
+            at = pl.ds(first + b, 1)
             energy_out[at] = energy[:, b * atoms : (b + 1) * atoms] * occupied[block.home(lx), at]
         back_two = (out - scaled * act_two).astype(bf16)
         back_one = lax.dot_general(back_two, w_two[...], across, preferred_element_type=f32)
         back_one = (back_one * (1.0 - act_one * act_one)).astype(bf16)
         gradients[rows] = lax.dot_general(back_one, w_one[...], across, preferred_element_type=f32).astype(bf16)
-
-    for y in range(rows_y):
-        grad = gradients[y * atoms : (y + 1) * atoms]
-        block.push(dots.at[y], own_sums, pushed, lx, y, grad, block.outside(y, lx, other, ghost))
+        for y in range(first, first + bins):
+            grad = gradients[y * atoms : (y + 1) * atoms]
+            block.project(dots.at[y], y, grad, targets[y])
+            block.push(dots.at[y], group.at[y], own_sums, pushed, lx, y, targets[y])
     for c in range(3):
         for y, total in enumerate(block.gathered(own_sums, c)):
             own_out[c, y : y + 1] = total * -block.unit(c)
@@ -303,32 +304,33 @@
 
 
 def last_kernel(sizes, lx, info, links, positions, occupied, embed, gradients, own_in, *refs):
-    *refs, ext, tab, upright, dots, own_sums, pushed, sems = refs
-    *before, grid_out, edges_out = refs if lx == 1 else refs + [None]
-    block = Block(sizes, info, links, ext, tab, sems)
+    *refs, tab, upright, dots, own_sums, pushed = refs
+    *before, grid_out, other_out = refs
+    edges_out = energy_out = other_out
+    block = Block(sizes, info, links, tab, own_near(embed))
     rows_y, atoms = block.rows_y, block.atoms
-    block.fetch_own(embed)
     block.place_own(positions, occupied)
     block.spread(upright)
-    pushed[...] = jnp.zeros_like(pushed)
-    block.wait()
     for y in range(rows_y):
-        grad = gradients[y * atoms : (y + 1) * atoms]
-        block.push(dots.at[y], own_sums, pushed, lx, y, grad, block.inside(y, (1, 2)))
+        block.project(dots.at[y], y, gradients[y * atoms : (y + 1) * atoms], block.inside(y, (1, 2)))
+        block.push(dots.at[y], None, own_sums, pushed, lx, y, block.inside(y, (1, 2)))
     for c in range(3):
         for y, total in enumerate(block.gathered(own_sums, c)):
             pushed[c, lx, y + 1, 0:1] -= total
         for to in (1, 2):
             total = jnp.sum(pushed[c, to, 1 : rows_y + 1], axis=1) * block.unit(c)
             total = total + own_in[c] if to == lx else total
-            if len(before) == 3:
-                grid, from_a, from_b = before
+            if lx == 2:
+                grid, from_a, from_b = before[:3]
                 ghost = from_a if to == 1 else from_b
                 grid_out[c, block.home(to)] = total + grid[c, to - 1] + ghost[c, pl.ds(1, rows_y)]
             else:
                 grid_out[c, to - 1] = total
-    if len(before) == 2:
+    if lx == 1:
         edges_out[...] = before[0][...] + before[1][...]
+    else:
+        for to in (1, 2):
+            energy_out[block.home(to)] = before[2 + to][...]
 
 
 def body(positions, embed, counts, neighbours, w_one, bias_one, w_two, w_out):
@@ -341,7 +343,8 @@
     odd_x = lax.axis_index("gx") % 2
     odd_y = lax.axis_index("gy") % 2
     lines_of = embed.reshape(2, rows, width)
-    row_b = pair_exchange(lax.dynamic_slice_in_dim(embed, odd_x, 1, 0), "gx", 1)
+    next_b, positions = lax.optimization_barrier((lax.dynamic_slice_in_dim(embed, odd_x, 1, 0), positions))
+    row_b = pair_exchange(next_b, "gx", 1)
     occupied = (jnp.arange(atoms, dtype=jnp.int32) < counts[:, :, None]).astype(f32)
     coords = packed(jnp.concatenate([positions, occupied[None]], axis=0))
     order = jnp.where(odd_x == 1, coords, coords[:, ::-1])
@@ -361,7 +364,7 @@
     col_b = pair_exchange(col_message(odd_y * (rows_y - 1)), "gy", 1)
     col_a = pair_exchange(col_message((1 - odd_y) * (rows_y - 1)), "gy", 0)
 
-    links = neighbours.reshape(-1)
+    links = neighbours
     info = jnp.stack([odd_x, odd_y]).astype(jnp.int32)
     bias, out = bias_one.reshape(1, hidden), w_out.reshape(1, hidden)
     vmem = pl.BlockSpec(memory_space=pltpu.VMEM)
@@ -369,7 +372,6 @@
     hbm = pl.BlockSpec(memory_space=pl.ANY)
     sizes = (rows_y, atoms, width)
     params = pltpu.CompilerParams(vmem_limit_bytes=13 * 2**20)
-    ext = pltpu.VMEM((4 * cols * atoms, width), bf16)
     tab = pltpu.VMEM((4, 4, 24, atoms), f32)
     upright = pltpu.VMEM((atoms, atoms), f32)
     own_sums = pltpu.VMEM((3, rows, atoms), f32)
@@ -380,9 +382,9 @@
     sums_a, sums_b, tail = pl.pallas_call(
         functools.partial(first_kernel, sizes),
         out_shape=(sums, sums, jax.ShapeDtypeStruct(tail.shape, bf16)),
-        in_specs=[smem, smem, vmem, vmem, hbm, vmem],
+        in_specs=[smem, smem, vmem, vmem, vmem, vmem],
         out_specs=(vmem, vmem, vmem),
-        scratch_shapes=[ext, tab, upright, pltpu.VMEM((2, rows_y, atoms, 6 * atoms), bf16), sems],
+        scratch_shapes=[pltpu.VMEM((2, rows_y, atoms, 6 * atoms), bf16), tab, upright],
         compiler_params=params,
     )(info, links, positions, occupied, later, tail)
 
@@ -405,13 +407,13 @@
                 jax.ShapeDtypeStruct((rows, width), bf16),
                 jax.ShapeDtypeStruct((rows_y, atoms), f32),
             ),
-            in_specs=[smem, smem, vmem, vmem] + [hbm] * 7 + [vmem] * 2,
+            in_specs=[smem, smem, vmem, vmem, hbm] + [vmem] * 4 + [hbm] * 4,
             out_specs=(vmem,) * 5,
             scratch_shapes=[
-                ext, tab, upright, pltpu.VMEM((rows, width), bf16), pltpu.VMEM((rows_y, atoms, 5 * atoms), bf16),
+                pltpu.VMEM((rows, width), bf16), tab, upright, pltpu.VMEM((rows, width), bf16), pltpu.VMEM((rows_y, atoms, 5 * atoms), bf16),
                 pltpu.VMEM((rows_y, atoms, 5 * atoms), f32), own_sums, pushed,
-                pltpu.VMEM((4 * rows_y + 64, width), bf16),
-                pltpu.VMEM((rows, width), f32), pltpu.VMEM(w_one.shape, bf16), pltpu.VMEM(w_two.shape, bf16), sems,
+                pltpu.VMEM(w_one.shape, bf16), pltpu.VMEM(w_two.shape, bf16),
+                pltpu.VMEM(bias.shape, f32), pltpu.VMEM(out.shape, f32), sems,
             ],
             compiler_params=params,
         )(info, links, positions, occupied, row, corner, col_a, col_b, sums, w_one, w_two, bias, out)
@@ -421,31 +423,32 @@
     pushed_b, edges_b, own_b, grad_b, energy_b = side(2, 1, 3, info, row_b, corner_b, sums_b)
     from_b = pair_exchange(pushed_b, "gx", 1)
     inner_shape = jax.ShapeDtypeStruct((3, 2, rows_y, atoms), f32)
+    energy_shape = jax.ShapeDtypeStruct((2, rows_y, atoms), f32)
     edge_shape = jax.ShapeDtypeStruct((3, 4, atoms), f32)
 
     def inner(lx, gradients, own, *before):
         return pl.pallas_call(
             functools.partial(last_kernel, sizes, lx),
-            out_shape=(inner_shape, edge_shape) if lx == 1 else inner_shape,
-            in_specs=[smem, smem, vmem, vmem, hbm] + [vmem] * (2 + len(before)),
-            out_specs=(vmem, vmem) if lx == 1 else vmem,
+            out_shape=(inner_shape, edge_shape if lx == 1 else energy_shape),
+            in_specs=[smem, smem, vmem, vmem, vmem, vmem] + [vmem] * (1 + len(before)),
+            out_specs=(vmem, vmem),
             scratch_shapes=[
-                ext, tab, upright, pltpu.VMEM((rows_y, atoms, 6 * atoms), f32), own_sums, pushed, sems,
+                tab, upright, pltpu.VMEM((rows_y, atoms, 6 * atoms), f32), own_sums, pushed,
             ],
             compiler_params=params,
         )(info, links, positions, occupied, lines_of, gradients, own, *before)
 
     grid, edges = inner(1, grad_a, own_a, edges_a, edges_b)
-    forces = inner(2, grad_b, own_b, grid, from_a, from_b)
+    forces, energy = inner(2, grad_b, own_b, grid, from_a, from_b, energy_a, energy_b)
     near_rows = jnp.stack([from_a, from_b], axis=1)
     first = edges[:, 0:2] + near_rows[:, :, 0]
     last = edges[:, 2:4] + near_rows[:, :, cols - 1]
     side_a = pair_exchange(jnp.where(odd_y == 1, first, last), "gy", 0)
     side_b = pair_exchange(jnp.where(odd_y == 1, last, first), "gy", 1)
     side_a, side_b = (jnp.where(odd_x == 1, side, side[:, ::-1]) for side in (side_a, side_b))
-    forces = forces.at[:, :, 0].add(jnp.where(odd_y == 1, side_a, side_b))
-    forces = forces.at[:, :, rows_y - 1].add(jnp.where(odd_y == 1, side_b, side_a))
-    energy = jnp.where(odd_x == 1, jnp.stack([energy_a, energy_b]), jnp.stack([energy_b, energy_a]))
+    left, right = jnp.where(odd_y == 1, side_a, side_b), jnp.where(odd_y == 1, side_b, side_a)
+    at_y = jnp.arange(rows_y, dtype=jnp.int32)[:, None]
+    forces = forces + jnp.where(at_y == 0, left[:, :, None], 0.0) + jnp.where(at_y == rows_y - 1, right[:, :, None], 0.0)
     return forces, energy
 
 

time: 48.2 us -> 42.5 us (0.88)
  Pallas kernels: 25.1 us -> 21.6 us
  local copies, waits for them, and re-layouts: 4.97 us -> 2.68 us
  other arithmetic: 1.7 us -> 1.01 us
  starting transfers between devices: 15 us -> 15.6 us
    pallas_call x2, Pallas kernels: 13.3 us -> 10.4 us  [side(): pl.pallas_call(functools.partial(side_kernel, sizes, lx, other, ghost), o...]
    dynamic_slice x1, local copies, waits for them, and re-layouts: 1.08 us -> 0.03 us  [body(): lax.dynamic_slice_in_dim(again, 1 - odd_x, 1, 0)]
    convert_element_type x2, other arithmetic: 0.91 us -> 0.14 us  [body(): (jnp.arange(atoms, dtype=jnp.int32) < counts[:, :, None]).astype(f32)]
    unnamed x21 -> x17, local copies, waits for them, and re-layouts: 2.12 us -> 1.35 us
    add x2 -> x1, other arithmetic: 0.01 us -> 0.68 us  [body(): forces + jnp.where(at_y == 0, left[:, :, None], 0.0)]
    another operation x2 -> x0, local copies, waits for them, and re-layouts: 0.63 us -> none
    ppermute x10, starting transfers between devices: 15 us -> 15.6 us  [pair_exchange(): return lax.ppermute(value, axis, pairs)]
    select_n x2 -> x1, other arithmetic: 0.61 us -> 0.01 us  [body(): jnp.where(odd_y == 1, side_a, side_b)]
  transfers between devices with their start and end apart: 10 -> 10, of which waited for: 0 -> 2; matrix products, arithmetic and copies ran while one was open for 4% -> 1% of each run, Pallas kernels for 52% -> 51%
where the time goes in v3:
time: 42.5 us; the launch traced here: 42.3 us
  Pallas kernels  21.6 us (51%)
  starting transfers between devices  15.6 us (37%)
  local copies, waits for them, and re-layouts  2.68 us (6%)
  other arithmetic  1.01 us (2%)
  between operations  0.91 us (2%)
  waiting for transfers between devices  0.45 us (1%)
    ppermute x10, starting transfers between devices, pair_exchange(): return lax.ppermute(value, axis, pairs)  15.6 us
    pallas_call x2, Pallas kernels, side(): pl.pallas_call(functools.partial(side_kernel, sizes, lx, other, ghost), o...  10.4 us
    pallas_call x2, Pallas kernels, inner(): pl.pallas_call(functools.partial(last_kernel, sizes, lx), out_shape=(inne...  7.61 us
    pallas_call x1, Pallas kernels, body(): pl.pallas_call(functools.partial(first_kernel, sizes), out_shape=(sums, s...  3.55 us
    unnamed x17, local copies, waits for them, and re-layouts  1.35 us
    dynamic_slice x1, local copies, waits for them, and re-layouts, body(): lax.dynamic_slice_in_dim(embed, odd_x, 1, 0)  1.16 us
  transfers between devices with their start and end apart: 10, of which 2 were waited for; matrix products, arithmetic and copies ran while one was open for 1% of the time, Pallas kernels for 51%

profile of v3, /device:TPU:0, one launch (start us, length us, event | category | flops | bytes accessed | tf_op | source)
XLA Modules:
  0.0 42.3 jit_solution(18303832179345532055)
XLA Ops:
  0.6 0.0 copy-start
  0.7 0.0 copy-start.7
  0.7 0.0 copy-start.1
  0.7 1.2 %constant_dynamic-slice_fusion.3 = bf16[1,8,128,256]{3,2,1,0:T(8,128)(2,1)S(1)} fusion(bf16[2,8,128,256]{3,2,1,0:T(8,128)(2,1)} %param.9, s32[]{:T(128)S(6)} %select_n.83), kind=kLoop, calls=%fused_computation.33 | loop fusion | bytes 1048580 | tf_op jit(solution)/shard_map/dynamic_slice | solution.py:346
  1.8 0.0 copy-done.7
  1.8 0.1 fusion.2
  1.9 0.0 copy-done.1
  2.0 0.0 copy-done
  2.1 0.5 %collective-permute-start.1 = (bf16[1,8,128,256]{3,2,1,0:T(8,128)(2,1)S(1)}, bf16[1,8,128,256]{3,2,1,0:T(8,128)(2,1)S(1)}, u32[]{:S(2)}, u32[]{:S(2)}) collective-permute-start(bf16[1,8,128,256]{3,2,1,0:T(8,128)(2,1)S(1)} %constant_dynamic-slice_fusion.2), channel_id=1, source_target_pairs={{0,4},{4,0},{8,12},{12,8},{16,20},{20,16},{24,28},{28,24},{1,5},{5... | collective-permute-start | bytes 1572872 | tf_op jit(solution)/shard_map/ppermute | solution.py:27
  2.6 4.7 %collective-permute-start = (bf16[1,8,128,256]{3,2,1,0:T(8,128)(2,1)S(1)}, bf16[1,8,128,256]{3,2,1,0:T(8,128)(2,1)S(1)}, u32[]{:S(2)}, u32[]{:S(2)}) collective-permute-start(bf16[1,8,128,256]{3,2,1,0:T(8,128)(2,1)S(1)} %constant_dynamic-slice_fusion.3), channel_id=1, source_target_pairs={{4,8},{8,4},{12,16},{16,12},{20,24},{24,20},{28,0},{0,28},{5,9},{9... | collective-permute-start | bytes 1572872 | tf_op jit(solution)/shard_map/ppermute | solution.py:27
  7.4 0.0 collective-permute-done.1
  7.5 2.5 %collective-permute-start.3 = (bf16[272,256]{1,0:T(8,128)(2,1)S(1)}, bf16[272,256]{1,0:T(8,128)(2,1)S(1)}, u32[]{:S(2)}, u32[]{:S(2)}) collective-permute-start(bf16[272,256]{1,0:T(8,128)(2,1)S(1)} %pad_maximum_fusion.1), channel_id=1, source_target_pairs={{1,2},{2,1},{3,0},{0,3},{5,6},{6,5},{7,4},{4,7},{9,10},{10,9},{11,... | collective-permute-start | bytes 417800 | tf_op jit(solution)/shard_map/ppermute | solution.py:27
  10.0 0.6 %collective-permute-start.2 = (bf16[272,256]{1,0:T(8,128)(2,1)S(1)}, bf16[272,256]{1,0:T(8,128)(2,1)S(1)}, u32[]{:S(2)}, u32[]{:S(2)}) collective-permute-start(bf16[272,256]{1,0:T(8,128)(2,1)S(1)} %pad_maximum_fusion), channel_id=1, source_target_pairs={{0,1},{1,0},{2,3},{3,2},{4,5},{5,4},{6,7},{7,6},{8,9},{9,8},{10,11... | collective-permute-start | bytes 417800 | tf_op jit(solution)/shard_map/ppermute | solution.py:27
  10.6 0.1 fusion.1.occupied
  10.7 0.0 copy-start.4
  10.7 0.1 pad_add_fusion.info
  10.8 0.6 %copy-done.4 = s32[2,8,9]{2,1,0:T(8,128)S(1)} copy-done((s32[2,8,9]{2,1,0:T(8,128)S(1)}, s32[2,8,9]{2,1,0:T(8,128)}, u32[]{:S(2)}) %copy-start.4) | copy-done | bytes 600
  11.4 3.5 %shard_map.95 = (f32[1024,256]{1,0:T(8,128)S(1)}, f32[1024,256]{1,0:T(8,128)S(1)}, bf16[64,256]{1,0:T(8,128)(2,1)S(1)}) custom-call(s32[2]{0:T(128)S(1)} %pad_add_fusion.info, s32[2,8,9]{2,1,0:T(8,128)S(1)} %copy-done.4, f32[3,2,8,128]{3,2,1,0:T(8,128)S(1)} %copy-done.1, f32[2,8,128]{2,1,0:T(8,128)S(1)} %fusion.1.occupied, ...), custom_call_target="tpu_custom_call" | custom-call | tf_op jit(solution)/shard_map/pallas_call | solution.py:382
  15.0 0.0 collective-permute-done.3.col_b
  15.0 0.3 collective-permute-done.2.col_a
  15.3 0.0 copy-start.2
  15.3 0.0 copy-start.3
  15.3 0.0 copy-start.6
  15.3 0.1 collective-permute-start.5
  15.4 3.7 %collective-permute-start.4 = (bf16[320,256]{1,0:T(8,128)(2,1)S(1)}, bf16[320,256]{1,0:T(8,128)(2,1)S(1)}, u32[]{:S(2)}, u32[]{:S(2)}) collective-permute-start(bf16[320,256]{1,0:T(8,128)(2,1)S(1)} %get-tuple-element.33), channel_id=1, source_target_pairs={{4,8},{8,4},{12,16},{16,12},{20,24},{24,20},{28,0},{0,28},{5,9},{9... | collective-permute-start | bytes 491528 | tf_op jit(solution)/shard_map/ppermute | solution.py:27
  19.1 0.0 collective-permute-done.5.corner
  19.1 0.0 copy-start.5
  19.1 0.0 copy-done.2
  19.1 0.0 copy-done.3
  19.1 0.0 copy-done.6
  19.1 0.7 %copy-done.5 = f32[256]{0:T(256)S(1)} copy-done((f32[256]{0:T(256)S(1)}, f32[256]{0:T(256)}, u32[]{:S(2)}) %copy-start.5) | copy-done | bytes 1048
  19.8 5.1 %shard_map.98 = (f32[3,10,128]{2,1,0:T(8,128)S(1)}, f32[3,4,128]{2,1,0:T(4,128)S(1)}, f32[3,8,128]{2,1,0:T(8,128)S(1)}, bf16[1024,256]{1,0:T(8,128)(2,1)S(1)}, f32[8,128]{1,0:T(8,128)S(1)}) custom-call(s32[2]{0:T(128)S(1)} %pad_add_fusion.info, s32[2,8,9]{2,1,0:T(8,128)S(1)} %copy-done.4, f32[3,2,8,128]{3,2,1,0:T(8,128)S(1)} %copy-done.1, ...), custom_call_target="tpu_custom_call" | custom-call | tf_op jit(solution)/shard_map/pallas_call | solution.py:401
  24.9 0.1 collective-permute-start.6
  25.0 0.0 collective-permute-done
  25.0 0.0 collective-permute-done.4.corner
  25.0 5.3 %shard_map.97 = (f32[3,10,128]{2,1,0:T(8,128)S(1)}, f32[3,4,128]{2,1,0:T(4,128)S(1)}, f32[3,8,128]{2,1,0:T(8,128)S(1)}, bf16[1024,256]{1,0:T(8,128)(2,1)S(1)}, f32[8,128]{1,0:T(8,128)S(1)}) custom-call(s32[2]{0:T(128)S(1)} %pad_add_fusion.info, s32[2,8,9]{2,1,0:T(8,128)S(1)} %copy-done.4, f32[3,2,8,128]{3,2,1,0:T(8,128)S(1)} %copy-done.1, ...), custom_call_target="tpu_custom_call" | custom-call | tf_op jit(solution)/shard_map/pallas_call | solution.py:401
  30.3 1.4 %collective-permute-start.7 = (f32[3,10,128]{2,1,0:T(8,128)S(1)}, f32[3,10,128]{2,1,0:T(8,128)S(1)}, u32[]{:S(2)}, u32[]{:S(2)}) collective-permute-start(f32[3,10,128]{2,1,0:T(8,128)S(1)} %get-tuple-element.46), channel_id=1, source_target_pairs={{4,8},{8,4},{12,16},{16,12},{20,24},{24,20},{28,0},{0,28},{5,9},{9... | collective-permute-start | bytes 46088 | tf_op jit(solution)/shard_map/ppermute | solution.py:27
  31.7 3.6 %shard_map.99 = (f32[3,2,8,128]{3,2,1,0:T(8,128)S(1)}, f32[3,4,128]{2,1,0:T(4,128)S(1)}) custom-call(s32[2]{0:T(128)S(1)} %pad_add_fusion.info, s32[2,8,9]{2,1,0:T(8,128)S(1)} %copy-done.4, f32[3,2,8,128]{3,2,1,0:T(8,128)S(1)} %copy-done.1, f32[2,8,128]{2,1,0:T(8,128)S(1)} %fusion.1.occupied, bf16[2,1024,256]{2,1,0:T(8,128)(2,1)S(1)} %bitcast.38, ...), custom_call_target="tpu_custom_call" | custom-call | tf_op jit(solution)/shard_map/pallas_call | solution.py:430
  35.3 0.0 collective-permute-done.6.refs_1_
  35.3 0.1 collective-permute-done.7.refs_2_
  35.4 1.6 %collective-permute-start.8 = (f32[3,2,128]{2,1,0:T(2,128)S(1)}, f32[3,2,128]{2,1,0:T(2,128)S(1)}, u32[]{:S(2)}, u32[]{:S(2)}) collective-permute-start(f32[3,2,128]{2,1,0:T(2,128)S(1)} %get-tuple-element.63), channel_id=1, source_target_pairs={{0,1},{1,0},{2,3},{3,2},{4,5},{5,4},{6,7},{7,6},{8,9},{9,8},{10,11... | collective-permute-start | bytes 9224 | tf_op jit(solution)/shard_map/ppermute | solution.py:27
  37.0 0.5 %collective-permute-start.9 = (f32[3,2,128]{2,1,0:T(2,128)S(1)}, f32[3,2,128]{2,1,0:T(2,128)S(1)}, u32[]{:S(2)}, u32[]{:S(2)}) collective-permute-start(f32[3,2,128]{2,1,0:T(2,128)S(1)} %get-tuple-element.62), channel_id=1, source_target_pairs={{1,2},{2,1},{3,0},{0,3},{5,6},{6,5},{7,4},{4,7},{9,10},{10,9},{11,... | collective-permute-start | bytes 9224 | tf_op jit(solution)/shard_map/ppermute | solution.py:27
  37.5 4.0 %shard_map.100 = (f32[3,2,8,128]{3,2,1,0:T(8,128)S(1)}, f32[2,8,128]{2,1,0:T(8,128)}) custom-call(s32[2]{0:T(128)S(1)} %pad_add_fusion.info, s32[2,8,9]{2,1,0:T(8,128)S(1)} %copy-done.4, f32[3,2,8,128]{3,2,1,0:T(8,128)S(1)} %copy-done.1, f32[2,8,128]{2,1,0:T(8,128)S(1)} %fusion.1.occupied, bf16[2,1024,256]{2,1,0:T(8,128)(2,1)S(1)} %bitcast.39, ...), custom_call_target="tpu_custom_call" | custom-call | tf_op jit(solution)/shard_map/pallas_call | solution.py:430
  41.5 0.0 collective-permute-done.8
  41.5 0.0 collective-permute-done.9
  41.6 0.7 %select_add_fusion = f32[3,2,8,128]{3,2,1,0:T(8,128)} fusion(f32[3,2,8,128]{3,2,1,0:T(8,128)S(1)} %get-tuple-element.49, f32[3,2,128]{2,1,0:T(2,128)S(1)} %get-tuple-element.61, f32[3,2,128]{2,1,0:T(2,128)S(1)} %get-tuple-element.60, pred[8]{0:T(512)(128)(4,1)S(1)} %get-tuple-element.66, pred[8]{0:T(512)(128)(4,1)S(1)} %get-tuple-element.67), kind=kLoop, calls=%fused_computation.11 | loop fusion | flops 24576 | bytes 55312 | tf_op jit(solution)/shard_map/add | solution.py:451
  (22 shorter events, 0.3 us)
Async XLA Ops:
  0.6 1.4 %copy-start = (bf16[2,8,128,256]{3,2,1,0:T(8,128)(2,1)S(1)}, bf16[2,8,128,256]{3,2,1,0:T(8,128)(2,1)}, u32[]{:S(2)}) copy-start(bf16[2,8,128,256]{3,2,1,0:T(8,128)(2,1)} %param.9) | copy-start | bytes 3145732
  0.7 1.2 %copy-start.7 = (s32[2,8]{1,0:T(2,128)S(1)}, s32[2,8]{1,0:T(2,128)}, u32[]{:S(2)}) copy-start(s32[2,8]{1,0:T(2,128)} %param.10) | copy-start | bytes 196
  0.7 1.3 %copy-start.1 = (f32[3,2,8,128]{3,2,1,0:T(8,128)S(1)}, f32[3,2,8,128]{3,2,1,0:T(8,128)}, u32[]{:S(2)}) copy-start(f32[3,2,8,128]{3,2,1,0:T(8,128)} %positions.4) | copy-start | bytes 73732
  2.1 5.4 %collective-permute-start.1 = (bf16[1,8,128,256]{3,2,1,0:T(8,128)(2,1)S(1)}, bf16[1,8,128,256]{3,2,1,0:T(8,128)(2,1)S(1)}, u32[]{:S(2)}, u32[]{:S(2)}) collective-permute-start(bf16[1,8,128,256]{3,2,1,0:T(8,128)(2,1)S(1)} %constant_dynamic-slice_fusion.2), channel_id=1, source_target_pairs={{0,4},{4,0},{8,12},{12,8},{16,20},{20,16},{24,28},{28,24},{1,5},{5... | collective-permute-start | bytes 1572872 | tf_op jit(solution)/shard_map/ppermute | solution.py:27
  2.6 22.4 %collective-permute-start = (bf16[1,8,128,256]{3,2,1,0:T(8,128)(2,1)S(1)}, bf16[1,8,128,256]{3,2,1,0:T(8,128)(2,1)S(1)}, u32[]{:S(2)}, u32[]{:S(2)}) collective-permute-start(bf16[1,8,128,256]{3,2,1,0:T(8,128)(2,1)S(1)} %constant_dynamic-slice_fusion.3), channel_id=1, source_target_pairs={{4,8},{8,4},{12,16},{16,12},{20,24},{24,20},{28,0},{0,28},{5,9},{9... | collective-permute-start | bytes 1572872 | tf_op jit(solution)/shard_map/ppermute | solution.py:27
  7.5 7.4 %collective-permute-start.3 = (bf16[272,256]{1,0:T(8,128)(2,1)S(1)}, bf16[272,256]{1,0:T(8,128)(2,1)S(1)}, u32[]{:S(2)}, u32[]{:S(2)}) collective-permute-start(bf16[272,256]{1,0:T(8,128)(2,1)S(1)} %pad_maximum_fusion.1), channel_id=1, source_target_pairs={{1,2},{2,1},{3,0},{0,3},{5,6},{6,5},{7,4},{4,7},{9,10},{10,9},{11,... | collective-permute-start | bytes 417800 | tf_op jit(solution)/shard_map/ppermute | solution.py:27
  10.0 5.2 %collective-permute-start.2 = (bf16[272,256]{1,0:T(8,128)(2,1)S(1)}, bf16[272,256]{1,0:T(8,128)(2,1)S(1)}, u32[]{:S(2)}, u32[]{:S(2)}) collective-permute-start(bf16[272,256]{1,0:T(8,128)(2,1)S(1)} %pad_maximum_fusion), channel_id=1, source_target_pairs={{0,1},{1,0},{2,3},{3,2},{4,5},{5,4},{6,7},{7,6},{8,9},{9,8},{10,11... | collective-permute-start | bytes 417800 | tf_op jit(solution)/shard_map/ppermute | solution.py:27
  10.7 0.7 %copy-start.4 = (s32[2,8,9]{2,1,0:T(8,128)S(1)}, s32[2,8,9]{2,1,0:T(8,128)}, u32[]{:S(2)}) copy-start(s32[2,8,9]{2,1,0:T(8,128)} %links.9) | copy-start | bytes 1732
  15.3 3.8 %copy-start.2 = (bf16[256,256]{1,0:T(8,128)(2,1)S(1)}, bf16[256,256]{1,0:T(8,128)(2,1)}, u32[]{:S(2)}) copy-start(bf16[256,256]{1,0:T(8,128)(2,1)} %w_one_in.3) | copy-start | bytes 393220
  15.3 3.8 %copy-start.3 = (bf16[256,256]{1,0:T(8,128)(2,1)S(1)}, bf16[256,256]{1,0:T(8,128)(2,1)}, u32[]{:S(2)}) copy-start(bf16[256,256]{1,0:T(8,128)(2,1)} %w_two_in.3) | copy-start | bytes 393220
  15.3 3.8 %copy-start.6 = (f32[256]{0:T(256)S(1)}, f32[256]{0:T(256)}, u32[]{:S(2)}) copy-start(f32[256]{0:T(256)} %param.15) | copy-start | bytes 3076
  15.3 3.8 %collective-permute-start.5 = (bf16[320,256]{1,0:T(8,128)(2,1)S(1)}, bf16[320,256]{1,0:T(8,128)(2,1)S(1)}, u32[]{:S(2)}, u32[]{:S(2)}) collective-permute-start(bf16[320,256]{1,0:T(8,128)(2,1)S(1)} %get-tuple-element.38), channel_id=1, source_target_pairs={{0,4},{4,0},{8,12},{12,8},{16,20},{20,16},{24,28},{28,24},{1,5},{5... | collective-permute-start | bytes 491528 | tf_op jit(solution)/shard_map/ppermute | solution.py:27
  15.4 9.6 %collective-permute-start.4 = (bf16[320,256]{1,0:T(8,128)(2,1)S(1)}, bf16[320,256]{1,0:T(8,128)(2,1)S(1)}, u32[]{:S(2)}, u32[]{:S(2)}) collective-permute-start(bf16[320,256]{1,0:T(8,128)(2,1)S(1)} %get-tuple-element.33), channel_id=1, source_target_pairs={{4,8},{8,4},{12,16},{16,12},{20,24},{24,20},{28,0},{0,28},{5,9},{9... | collective-permute-start | bytes 491528 | tf_op jit(solution)/shard_map/ppermute | solution.py:27
  19.1 0.7 %copy-start.5 = (f32[256]{0:T(256)S(1)}, f32[256]{0:T(256)}, u32[]{:S(2)}) copy-start(f32[256]{0:T(256)} %param.13) | copy-start | bytes 3076
  24.9 10.4 %collective-permute-start.6 = (f32[3,10,128]{2,1,0:T(8,128)S(1)}, f32[3,10,128]{2,1,0:T(8,128)S(1)}, u32[]{:S(2)}, u32[]{:S(2)}) collective-permute-start(f32[3,10,128]{2,1,0:T(8,128)S(1)} %get-tuple-element.45), channel_id=1, source_target_pairs={{0,4},{4,0},{8,12},{12,8},{16,20},{20,16},{24,28},{28,24},{1,5},{5... | collective-permute-start | bytes 46088 | tf_op jit(solution)/shard_map/ppermute | solution.py:27
  30.3 5.1 %collective-permute-start.7 = (f32[3,10,128]{2,1,0:T(8,128)S(1)}, f32[3,10,128]{2,1,0:T(8,128)S(1)}, u32[]{:S(2)}, u32[]{:S(2)}) collective-permute-start(f32[3,10,128]{2,1,0:T(8,128)S(1)} %get-tuple-element.46), channel_id=1, source_target_pairs={{4,8},{8,4},{12,16},{16,12},{20,24},{24,20},{28,0},{0,28},{5,9},{9... | collective-permute-start | bytes 46088 | tf_op jit(solution)/shard_map/ppermute | solution.py:27
  35.4 6.1 %collective-permute-start.8 = (f32[3,2,128]{2,1,0:T(2,128)S(1)}, f32[3,2,128]{2,1,0:T(2,128)S(1)}, u32[]{:S(2)}, u32[]{:S(2)}) collective-permute-start(f32[3,2,128]{2,1,0:T(2,128)S(1)} %get-tuple-element.63), channel_id=1, source_target_pairs={{0,1},{1,0},{2,3},{3,2},{4,5},{5,4},{6,7},{7,6},{8,9},{9,8},{10,11... | collective-permute-start | bytes 9224 | tf_op jit(solution)/shard_map/ppermute | solution.py:27
  37.0 4.6 %collective-permute-start.9 = (f32[3,2,128]{2,1,0:T(2,128)S(1)}, f32[3,2,128]{2,1,0:T(2,128)S(1)}, u32[]{:S(2)}, u32[]{:S(2)}) collective-permute-start(f32[3,2,128]{2,1,0:T(2,128)S(1)} %get-tuple-element.62), channel_id=1, source_target_pairs={{1,2},{2,1},{3,0},{0,3},{5,6},{6,5},{7,4},{4,7},{9,10},{10,9},{11,... | collective-permute-start | bytes 9224 | tf_op jit(solution)/shard_map/ppermute | solution.py:27

commit v4 on v3

--- a/solution.py
+++ b/solution.py
@@ -107,12 +107,16 @@
         columns = [first + c * self.rows_y for c in range(3)]
         return [jnp.broadcast_to(self.upright[some, c : c + 1], (lines, self.atoms)) for c in columns]
 
-    def rows_of(self, lx, y, to, ky):
+    def present(self, lx, y, to, ky):
         kx = to - lx + 1
         list_x = jnp.where(self.odd_x == 1, kx, 2 - kx)
-        link = self.links[self.home(lx), y, list_x * 3 + ky]
+        return self.links[self.home(lx), y, list_x * 3 + ky] < 4 * self.cols
+
+    def rows_of(self, lx, y, to, ky, mirrored=False):
         at = pl.ds(lead + y + ky, 1)
-        z = jnp.where(link < 4 * self.cols, self.tab[2, to, at], -far)
+        z = self.tab[2, to, at]
+        if not mirrored:
+            z = jnp.where(self.present(lx, y, to, ky), z, -far)
         return self.tab[0, to, at], self.tab[1, to, at], z
 
     def weigh(self, group, lx, y, targets):
@@ -147,7 +151,21 @@
             )
             at += count * atoms
 
-    def push(self, dots, group, sums, pushed, lx, y, targets):
+    def project_mirrored(self, dots, first, lx, y, target, mine, yours):
+        atoms, (to, ky, count) = self.atoms, target
+        parts = []
+        for k in range(ky, ky + count):
+            bins = slice((y + k - 1) * atoms, (y + k) * atoms)
+            near, grad = self.near(self, to, y, k, 1), yours[bins]
+            near = jnp.where(self.present(lx, y, to, k), near, jnp.zeros_like(near))
+            grad = jnp.where(self.present(to, y + k - 1, lx, 2 - k), grad, jnp.zeros_like(grad))
+            parts.append(jnp.concatenate([near, grad], axis=1))
+        both = jnp.concatenate([mine[y * atoms : (y + 1) * atoms], self.near(self, lx, y, 1, 1)], axis=1)
+        dots[:, first : first + count * atoms] = lax.dot_general(
+            both, jnp.concatenate(parts, axis=0), across, preferred_element_type=f32
+        )
+
+    def push(self, dots, group, sums, pushed, lx, y, targets, mirrored=None):
         atoms = self.atoms
         for start in range(0, atoms, lines):
             some = slice(start, start + lines)
@@ -156,7 +174,7 @@
             at = 0
             for to, first, count in targets:
                 for ky in range(first, first + count):
-                    row = self.rows_of(lx, y, to, ky)
+                    row = self.rows_of(lx, y, to, ky, to == mirrored)
                     delta = [row[c] - mine[c] for c in range(3)]
                     if group is None:
                         square = delta[0] * delta[0] + delta[1] * delta[1] + delta[2] * delta[2]
@@ -205,13 +223,14 @@
 
 
 def first_kernel(
-    sizes, info, links, positions, occupied, embed, tail, sums_a, sums_b, tail_out, group, tab, upright
+    sizes, info, links, positions, occupied, embed, tail, bias, out, sums_a, sums_b, tail_out, vectors, group, tab, upright
 ):
     block = Block(sizes, info, links, tab, own_near(embed))
     rows_y, atoms = block.rows_y, block.atoms
     block.place_own(positions, occupied)
     block.spread(upright)
     tail_out[...] = tail[...]
+    vectors[0:1], vectors[1:2] = bias[...], out[...]
     for lx, out in ((1, sums_a), (2, sums_b)):
         for y in range(rows_y):
             block.weigh(group.at[lx - 1, y], lx, y, block.inside(y, (1, 2)))
@@ -233,8 +252,8 @@
 
 def side_kernel(
     sizes, lx, other, ghost, info, links, positions, occupied, row_in, corner, col_a, col_b, sums,
-    w_one_in, w_two_in, bias_in, out_in, pushed_out, edges_out, own_out, gradients, energy_out,
-    row, tab, upright, features, group, dots, own_sums, pushed, w_one, w_two, bias_one, w_out, sems
+    w_one_in, w_two_in, vectors, pushed_out, edges_out, own_out, gradients, energy_out,
+    row, tab, upright, features, group, dots, own_sums, pushed, w_one, w_two, sems
 ):
     def near(block, to, y, ky, count):
         atoms, odd, slot = block.atoms, block.odd_y == 1, y + ky
@@ -249,7 +268,7 @@
 
     block = Block(sizes, info, links, tab, near, sems)
     rows_y, atoms, cols = block.rows_y, block.atoms, block.cols
-    for src, dst in ((row_in, row), (w_one_in, w_one), (w_two_in, w_two), (bias_in, bias_one), (out_in, w_out)):
+    for src, dst in ((row_in, row), (w_one_in, w_one), (w_two_in, w_two)):
         block.fetch(src, dst)
     block.place_own(positions, occupied)
     at = 2 * atoms
@@ -272,9 +291,9 @@
             features[rows] = (sums[rows] + block.describe(group.at[y], lx, y, targets[y])).astype(bf16)
         rows = slice(first * atoms, (first + bins) * atoms)
         inner = jnp.dot(features[rows], w_one[...], preferred_element_type=f32)
-        act_one = jnp.tanh(inner + bias_one[...])
+        act_one = jnp.tanh(inner + vectors[0:1])
         act_two = jnp.tanh(jnp.dot(act_one.astype(bf16), w_two[...], preferred_element_type=f32))
-        out = w_out[...]
+        out = vectors[1:2]
         scaled = act_two * out
         half = scaled[:, :128]
         for start in range(128, scaled.shape[1], 128):
@@ -312,13 +331,19 @@
     block.place_own(positions, occupied)
     block.spread(upright)
     for y in range(rows_y):
-        block.project(dots.at[y], y, gradients[y * atoms : (y + 1) * atoms], block.inside(y, (1, 2)))
-        block.push(dots.at[y], None, own_sums, pushed, lx, y, block.inside(y, (1, 2)))
+        targets = block.inside(y, (lx,))
+        block.project(dots.at[y], y, gradients[y * atoms : (y + 1) * atoms], targets)
+        if lx == 1:
+            targets = targets + block.inside(y, (2,))
+            block.project_mirrored(dots.at[y], targets[0][2] * atoms, lx, y, targets[1], gradients, before[2])
+        block.push(dots.at[y], None, own_sums, pushed, lx, y, targets, 2 if lx == 1 else None)
     for c in range(3):
         for y, total in enumerate(block.gathered(own_sums, c)):
             pushed[c, lx, y + 1, 0:1] -= total
         for to in (1, 2):
-            total = jnp.sum(pushed[c, to, 1 : rows_y + 1], axis=1) * block.unit(c)
+            total = jnp.zeros((rows_y, atoms), f32)
+            if to >= lx:
+                total = jnp.sum(pushed[c, to, 1 : rows_y + 1], axis=1) * block.unit(c)
             total = total + own_in[c] if to == lx else total
             if lx == 2:
                 grid, from_a, from_b = before[:3]
@@ -379,14 +404,15 @@
     sems = pltpu.SemaphoreType.DMA((16,))
     sums = jax.ShapeDtypeStruct((rows, width), f32)
     tail = order.transpose(1, 0, 2, 3).reshape(8 * rows_y, width)
-    sums_a, sums_b, tail = pl.pallas_call(
+    vectors = jax.ShapeDtypeStruct((2, hidden), f32)
+    sums_a, sums_b, tail, vectors = pl.pallas_call(
         functools.partial(first_kernel, sizes),
-        out_shape=(sums, sums, jax.ShapeDtypeStruct(tail.shape, bf16)),
-        in_specs=[smem, smem, vmem, vmem, vmem, vmem],
-        out_specs=(vmem, vmem, vmem),
+        out_shape=(sums, sums, jax.ShapeDtypeStruct(tail.shape, bf16), vectors),
+        in_specs=[smem, smem] + [vmem] * 6,
+        out_specs=(vmem,) * 4,
         scratch_shapes=[pltpu.VMEM((2, rows_y, atoms, 6 * atoms), bf16), tab, upright],
         compiler_params=params,
-    )(info, links, positions, occupied, later, tail)
+    )(info, links, positions, occupied, later, tail, bias, out)
 
 
     corner = jax.ShapeDtypeStruct((2 * atoms + 4 * rows_y + 32, width), bf16)
@@ -407,16 +433,15 @@
                 jax.ShapeDtypeStruct((rows, width), bf16),
                 jax.ShapeDtypeStruct((rows_y, atoms), f32),
             ),
-            in_specs=[smem, smem, vmem, vmem, hbm] + [vmem] * 4 + [hbm] * 4,
+            in_specs=[smem, smem, vmem, vmem, hbm] + [vmem] * 4 + [hbm] * 2 + [vmem],
             out_specs=(vmem,) * 5,
             scratch_shapes=[
                 pltpu.VMEM((rows, width), bf16), tab, upright, pltpu.VMEM((rows, width), bf16), pltpu.VMEM((rows_y, atoms, 5 * atoms), bf16),
                 pltpu.VMEM((rows_y, atoms, 5 * atoms), f32), own_sums, pushed,
-                pltpu.VMEM(w_one.shape, bf16), pltpu.VMEM(w_two.shape, bf16),
-                pltpu.VMEM(bias.shape, f32), pltpu.VMEM(out.shape, f32), sems,
+                pltpu.VMEM(w_one.shape, bf16), pltpu.VMEM(w_two.shape, bf16), sems,
             ],
             compiler_params=params,
-        )(info, links, positions, occupied, row, corner, col_a, col_b, sums, w_one, w_two, bias, out)
+        )(info, links, positions, occupied, row, corner, col_a, col_b, sums, w_one, w_two, vectors)
 
     pushed_a, edges_a, own_a, grad_a, energy_a = side(1, 2, 0, info, row_a, corner_a, sums_a)
     from_a = pair_exchange(pushed_a, "gx", 0)
@@ -438,7 +463,7 @@
             compiler_params=params,
         )(info, links, positions, occupied, lines_of, gradients, own, *before)
 
-    grid, edges = inner(1, grad_a, own_a, edges_a, edges_b)
+    grid, edges = inner(1, grad_a, own_a, edges_a, edges_b, grad_b)
     forces, energy = inner(2, grad_b, own_b, grid, from_a, from_b, energy_a, energy_b)
     near_rows = jnp.stack([from_a, from_b], axis=1)
     first = edges[:, 0:2] + near_rows[:, :, 0]

time: 42.5 us -> 41.7 us (0.981)
  Pallas kernels: 21.6 us -> 20.6 us
  waiting for transfers between devices: 0.45 us -> 1.34 us
  local copies, waits for them, and re-layouts: 2.68 us -> 2.09 us
    pallas_call x2, Pallas kernels: 7.61 us -> 6.66 us  [inner(): pl.pallas_call(functools.partial(last_kernel, sizes, lx), out_shape=(inne...]
    ppermute x10, waiting for transfers between devices: 0.45 us -> 1.34 us  [pair_exchange(): return lax.ppermute(value, axis, pairs)]
    unnamed x17, local copies, waits for them, and re-layouts: 1.35 us -> 0.76 us
  transfers between devices with their start and end apart: 10 -> 10, of which waited for: 2 -> 2; matrix products, arithmetic and copies ran while one was open for 1% -> 1% of each run, Pallas kernels for 51% -> 49%
where the time goes in v4:
time: 41.7 us; the launch traced here: 41.6 us
  Pallas kernels  20.6 us (49%)
  starting transfers between devices  15.6 us (37%)
  local copies, waits for them, and re-layouts  2.09 us (5%)
  waiting for transfers between devices  1.34 us (3%)
  other arithmetic  1.01 us (2%)
  between operations  0.93 us (2%)
    ppermute x10, starting transfers between devices, pair_exchange(): return lax.ppermute(value, axis, pairs)  15.6 us
    pallas_call x2, Pallas kernels, side(): pl.pallas_call(functools.partial(side_kernel, sizes, lx, other, ghost), o...  10.3 us
    pallas_call x2, Pallas kernels, inner(): pl.pallas_call(functools.partial(last_kernel, sizes, lx), out_shape=(inne...  6.66 us
    pallas_call x1, Pallas kernels, body(): pl.pallas_call(functools.partial(first_kernel, sizes), out_shape=(sums, s...  3.54 us
    ppermute x10, waiting for transfers between devices, pair_exchange(): return lax.ppermute(value, axis, pairs)  1.34 us
    dynamic_slice x1, local copies, waits for them, and re-layouts, body(): lax.dynamic_slice_in_dim(embed, odd_x, 1, 0)  1.16 us
  transfers between devices with their start and end apart: 10, of which 2 were waited for; matrix products, arithmetic and copies ran while one was open for 1% of the time, Pallas kernels for 49%

profile of v4, /device:TPU:0, one launch (start us, length us, event | category | flops | bytes accessed | tf_op | source)
XLA Modules:
  0.0 41.6 jit_solution(17726567896199902162)
XLA Ops:
  0.6 0.0 copy-start
  0.7 0.0 copy-start.7
  0.7 0.0 copy-start.1
  0.7 1.2 %constant_dynamic-slice_fusion.3 = bf16[1,8,128,256]{3,2,1,0:T(8,128)(2,1)S(1)} fusion(bf16[2,8,128,256]{3,2,1,0:T(8,128)(2,1)} %param.9, s32[]{:T(128)S(6)} %select_n.83), kind=kLoop, calls=%fused_computation.33 | loop fusion | bytes 1048580 | tf_op jit(solution)/shard_map/dynamic_slice | solution.py:371
  1.8 0.0 copy-done.7
  1.8 0.1 fusion.2
  1.9 0.0 copy-done.1
  2.0 0.0 copy-done
  2.1 0.5 %collective-permute-start.1 = (bf16[1,8,128,256]{3,2,1,0:T(8,128)(2,1)S(1)}, bf16[1,8,128,256]{3,2,1,0:T(8,128)(2,1)S(1)}, u32[]{:S(2)}, u32[]{:S(2)}) collective-permute-start(bf16[1,8,128,256]{3,2,1,0:T(8,128)(2,1)S(1)} %constant_dynamic-slice_fusion.2), channel_id=1, source_target_pairs={{0,4},{4,0},{8,12},{12,8},{16,20},{20,16},{24,28},{28,24},{1,5},{5... | collective-permute-start | bytes 1572872 | tf_op jit(solution)/shard_map/ppermute | solution.py:27
  2.6 4.7 %collective-permute-start = (bf16[1,8,128,256]{3,2,1,0:T(8,128)(2,1)S(1)}, bf16[1,8,128,256]{3,2,1,0:T(8,128)(2,1)S(1)}, u32[]{:S(2)}, u32[]{:S(2)}) collective-permute-start(bf16[1,8,128,256]{3,2,1,0:T(8,128)(2,1)S(1)} %constant_dynamic-slice_fusion.3), channel_id=1, source_target_pairs={{4,8},{8,4},{12,16},{16,12},{20,24},{24,20},{28,0},{0,28},{5,9},{9... | collective-permute-start | bytes 1572872 | tf_op jit(solution)/shard_map/ppermute | solution.py:27
  7.4 0.0 collective-permute-done.1
  7.5 2.5 %collective-permute-start.3 = (bf16[272,256]{1,0:T(8,128)(2,1)S(1)}, bf16[272,256]{1,0:T(8,128)(2,1)S(1)}, u32[]{:S(2)}, u32[]{:S(2)}) collective-permute-start(bf16[272,256]{1,0:T(8,128)(2,1)S(1)} %pad_maximum_fusion.1), channel_id=1, source_target_pairs={{1,2},{2,1},{3,0},{0,3},{5,6},{6,5},{7,4},{4,7},{9,10},{10,9},{11,... | collective-permute-start | bytes 417800 | tf_op jit(solution)/shard_map/ppermute | solution.py:27
  10.0 0.6 %collective-permute-start.2 = (bf16[272,256]{1,0:T(8,128)(2,1)S(1)}, bf16[272,256]{1,0:T(8,128)(2,1)S(1)}, u32[]{:S(2)}, u32[]{:S(2)}) collective-permute-start(bf16[272,256]{1,0:T(8,128)(2,1)S(1)} %pad_maximum_fusion), channel_id=1, source_target_pairs={{0,1},{1,0},{2,3},{3,2},{4,5},{5,4},{6,7},{7,6},{8,9},{9,8},{10,11... | collective-permute-start | bytes 417800 | tf_op jit(solution)/shard_map/ppermute | solution.py:27
  10.6 0.1 fusion.1.occupied
  10.7 0.0 copy-start.6
  10.7 0.0 copy-start.4
  10.7 0.1 pad_add_fusion.info
  10.8 0.0 copy-start.5
  10.8 0.6 %copy-done.6 = f32[256]{0:T(256)S(1)} copy-done((f32[256]{0:T(256)S(1)}, f32[256]{0:T(256)}, u32[]{:S(2)}) %copy-start.6) | copy-done | bytes 1048
  11.4 0.0 copy-done.4
  11.4 0.1 copy-done.5
  11.5 3.5 %shard_map.95 = (f32[1024,256]{1,0:T(8,128)S(1)}, f32[1024,256]{1,0:T(8,128)S(1)}, bf16[64,256]{1,0:T(8,128)(2,1)S(1)}, f32[2,256]{1,0:T(2,128)S(1)}) custom-call(s32[2]{0:T(128)S(1)} %pad_add_fusion.info, s32[2,8,9]{2,1,0:T(8,128)S(1)} %copy-done.4, f32[3,2,8,128]{3,2,1,0:T(8,128)S(1)} %copy-done.1, f32[2,8,128]{2,1,0:T(8,128)S(1)} %fusion.1.occupied, ...), custom_call_target="tpu_custom_call" | custom-call | tf_op jit(solution)/shard_map/pallas_call | solution.py:408
  15.0 0.0 collective-permute-done.3.col_b
  15.0 0.2 collective-permute-done.2.col_a
  15.3 0.0 copy-start.2
  15.3 0.0 copy-start.3
  15.3 0.1 collective-permute-start.5
  15.4 3.7 %collective-permute-start.4 = (bf16[320,256]{1,0:T(8,128)(2,1)S(1)}, bf16[320,256]{1,0:T(8,128)(2,1)S(1)}, u32[]{:S(2)}, u32[]{:S(2)}) collective-permute-start(bf16[320,256]{1,0:T(8,128)(2,1)S(1)} %get-tuple-element.34), channel_id=1, source_target_pairs={{4,8},{8,4},{12,16},{16,12},{20,24},{24,20},{28,0},{0,28},{5,9},{9... | collective-permute-start | bytes 491528 | tf_op jit(solution)/shard_map/ppermute | solution.py:27
  19.1 0.0 collective-permute-done.5.corner
  19.1 0.0 copy-done.2
  19.1 0.0 copy-done.3
  19.1 5.1 %shard_map.98 = (f32[3,10,128]{2,1,0:T(8,128)S(1)}, f32[3,4,128]{2,1,0:T(4,128)S(1)}, f32[3,8,128]{2,1,0:T(8,128)S(1)}, bf16[1024,256]{1,0:T(8,128)(2,1)S(1)}, f32[8,128]{1,0:T(8,128)S(1)}) custom-call(s32[2]{0:T(128)S(1)} %pad_add_fusion.info, s32[2,8,9]{2,1,0:T(8,128)S(1)} %copy-done.4, f32[3,2,8,128]{3,2,1,0:T(8,128)S(1)} %copy-done.1, ...), custom_call_target="tpu_custom_call" | custom-call | tf_op jit(solution)/shard_map/pallas_call | solution.py:427
  24.2 0.1 collective-permute-start.6
  24.3 0.0 collective-permute-done
  24.3 0.0 collective-permute-done.4.corner
  24.3 5.2 %shard_map.97 = (f32[3,10,128]{2,1,0:T(8,128)S(1)}, f32[3,4,128]{2,1,0:T(4,128)S(1)}, f32[3,8,128]{2,1,0:T(8,128)S(1)}, bf16[1024,256]{1,0:T(8,128)(2,1)S(1)}, f32[8,128]{1,0:T(8,128)S(1)}) custom-call(s32[2]{0:T(128)S(1)} %pad_add_fusion.info, s32[2,8,9]{2,1,0:T(8,128)S(1)} %copy-done.4, f32[3,2,8,128]{3,2,1,0:T(8,128)S(1)} %copy-done.1, ...), custom_call_target="tpu_custom_call" | custom-call | tf_op jit(solution)/shard_map/pallas_call | solution.py:427
  29.6 1.4 %collective-permute-start.7 = (f32[3,10,128]{2,1,0:T(8,128)S(1)}, f32[3,10,128]{2,1,0:T(8,128)S(1)}, u32[]{:S(2)}, u32[]{:S(2)}) collective-permute-start(f32[3,10,128]{2,1,0:T(8,128)S(1)} %get-tuple-element.48), channel_id=1, source_target_pairs={{4,8},{8,4},{12,16},{16,12},{20,24},{24,20},{28,0},{0,28},{5,9},{9... | collective-permute-start | bytes 46088 | tf_op jit(solution)/shard_map/ppermute | solution.py:27
  31.0 3.8 %shard_map.99 = (f32[3,2,8,128]{3,2,1,0:T(8,128)S(1)}, f32[3,4,128]{2,1,0:T(4,128)S(1)}) custom-call(s32[2]{0:T(128)S(1)} %pad_add_fusion.info, s32[2,8,9]{2,1,0:T(8,128)S(1)} %copy-done.4, f32[3,2,8,128]{3,2,1,0:T(8,128)S(1)} %copy-done.1, f32[2,8,128]{2,1,0:T(8,128)S(1)} %fusion.1.occupied, bf16[2,1024,256]{2,1,0:T(8,128)(2,1)S(1)} %bitcast.38, ...), custom_call_target="tpu_custom_call" | custom-call | tf_op jit(solution)/shard_map/pallas_call | solution.py:455
  34.7 0.0 collective-permute-done.6.refs_1_
  34.7 0.0 collective-permute-done.7.refs_2_
  34.8 1.6 %collective-permute-start.8 = (f32[3,2,128]{2,1,0:T(2,128)S(1)}, f32[3,2,128]{2,1,0:T(2,128)S(1)}, u32[]{:S(2)}, u32[]{:S(2)}) collective-permute-start(f32[3,2,128]{2,1,0:T(2,128)S(1)} %get-tuple-element.65), channel_id=1, source_target_pairs={{0,1},{1,0},{2,3},{3,2},{4,5},{5,4},{6,7},{7,6},{8,9},{9,8},{10,11... | collective-permute-start | bytes 9224 | tf_op jit(solution)/shard_map/ppermute | solution.py:27
  36.3 0.5 %collective-permute-start.9 = (f32[3,2,128]{2,1,0:T(2,128)S(1)}, f32[3,2,128]{2,1,0:T(2,128)S(1)}, u32[]{:S(2)}, u32[]{:S(2)}) collective-permute-start(f32[3,2,128]{2,1,0:T(2,128)S(1)} %get-tuple-element.64), channel_id=1, source_target_pairs={{1,2},{2,1},{3,0},{0,3},{5,6},{6,5},{7,4},{4,7},{9,10},{10,9},{11,... | collective-permute-start | bytes 9224 | tf_op jit(solution)/shard_map/ppermute | solution.py:27
  36.8 2.9 %shard_map.100 = (f32[3,2,8,128]{3,2,1,0:T(8,128)S(1)}, f32[2,8,128]{2,1,0:T(8,128)}) custom-call(s32[2]{0:T(128)S(1)} %pad_add_fusion.info, s32[2,8,9]{2,1,0:T(8,128)S(1)} %copy-done.4, f32[3,2,8,128]{3,2,1,0:T(8,128)S(1)} %copy-done.1, f32[2,8,128]{2,1,0:T(8,128)S(1)} %fusion.1.occupied, bf16[2,1024,256]{2,1,0:T(8,128)(2,1)S(1)} %bitcast.39, ...), custom_call_target="tpu_custom_call" | custom-call | tf_op jit(solution)/shard_map/pallas_call | solution.py:455
  39.7 0.0 collective-permute-done.8
  39.7 1.1 %collective-permute-done.9 = f32[3,2,128]{2,1,0:T(2,128)S(1)} collective-permute-done((f32[3,2,128]{2,1,0:T(2,128)S(1)}, f32[3,2,128]{2,1,0:T(2,128)S(1)}, u32[]{:S(2)}, u32[]{:S(2)}) %collective-permute-start.9) | collective-permute-done | bytes 3104 | tf_op jit(solution)/shard_map/ppermute | solution.py:27
  40.9 0.7 %select_add_fusion = f32[3,2,8,128]{3,2,1,0:T(8,128)} fusion(f32[3,2,8,128]{3,2,1,0:T(8,128)S(1)} %get-tuple-element.51, f32[3,2,128]{2,1,0:T(2,128)S(1)} %get-tuple-element.63, f32[3,2,128]{2,1,0:T(2,128)S(1)} %get-tuple-element.62, pred[8]{0:T(512)(128)(4,1)S(1)} %get-tuple-element.68, pred[8]{0:T(512)(128)(4,1)S(1)} %get-tuple-element.69), kind=kLoop, calls=%fused_computation.11 | loop fusion | flops 24576 | bytes 55312 | tf_op jit(solution)/shard_map/add | solution.py:476
  (22 shorter events, 0.3 us)
Async XLA Ops:
  0.6 1.4 %copy-start = (bf16[2,8,128,256]{3,2,1,0:T(8,128)(2,1)S(1)}, bf16[2,8,128,256]{3,2,1,0:T(8,128)(2,1)}, u32[]{:S(2)}) copy-start(bf16[2,8,128,256]{3,2,1,0:T(8,128)(2,1)} %param.9) | copy-start | bytes 3145732
  0.7 1.2 %copy-start.7 = (s32[2,8]{1,0:T(2,128)S(1)}, s32[2,8]{1,0:T(2,128)}, u32[]{:S(2)}) copy-start(s32[2,8]{1,0:T(2,128)} %param.10) | copy-start | bytes 196
  0.7 1.3 %copy-start.1 = (f32[3,2,8,128]{3,2,1,0:T(8,128)S(1)}, f32[3,2,8,128]{3,2,1,0:T(8,128)}, u32[]{:S(2)}) copy-start(f32[3,2,8,128]{3,2,1,0:T(8,128)} %positions.4) | copy-start | bytes 73732
  2.1 5.4 %collective-permute-start.1 = (bf16[1,8,128,256]{3,2,1,0:T(8,128)(2,1)S(1)}, bf16[1,8,128,256]{3,2,1,0:T(8,128)(2,1)S(1)}, u32[]{:S(2)}, u32[]{:S(2)}) collective-permute-start(bf16[1,8,128,256]{3,2,1,0:T(8,128)(2,1)S(1)} %constant_dynamic-slice_fusion.2), channel_id=1, source_target_pairs={{0,4},{4,0},{8,12},{12,8},{16,20},{20,16},{24,28},{28,24},{1,5},{5... | collective-permute-start | bytes 1572872 | tf_op jit(solution)/shard_map/ppermute | solution.py:27
  2.6 21.7 %collective-permute-start = (bf16[1,8,128,256]{3,2,1,0:T(8,128)(2,1)S(1)}, bf16[1,8,128,256]{3,2,1,0:T(8,128)(2,1)S(1)}, u32[]{:S(2)}, u32[]{:S(2)}) collective-permute-start(bf16[1,8,128,256]{3,2,1,0:T(8,128)(2,1)S(1)} %constant_dynamic-slice_fusion.3), channel_id=1, source_target_pairs={{4,8},{8,4},{12,16},{16,12},{20,24},{24,20},{28,0},{0,28},{5,9},{9... | collective-permute-start | bytes 1572872 | tf_op jit(solution)/shard_map/ppermute | solution.py:27
  7.5 7.5 %collective-permute-start.3 = (bf16[272,256]{1,0:T(8,128)(2,1)S(1)}, bf16[272,256]{1,0:T(8,128)(2,1)S(1)}, u32[]{:S(2)}, u32[]{:S(2)}) collective-permute-start(bf16[272,256]{1,0:T(8,128)(2,1)S(1)} %pad_maximum_fusion.1), channel_id=1, source_target_pairs={{1,2},{2,1},{3,0},{0,3},{5,6},{6,5},{7,4},{4,7},{9,10},{10,9},{11,... | collective-permute-start | bytes 417800 | tf_op jit(solution)/shard_map/ppermute | solution.py:27
  10.0 5.2 %collective-permute-start.2 = (bf16[272,256]{1,0:T(8,128)(2,1)S(1)}, bf16[272,256]{1,0:T(8,128)(2,1)S(1)}, u32[]{:S(2)}, u32[]{:S(2)}) collective-permute-start(bf16[272,256]{1,0:T(8,128)(2,1)S(1)} %pad_maximum_fusion), channel_id=1, source_target_pairs={{0,1},{1,0},{2,3},{3,2},{4,5},{5,4},{6,7},{7,6},{8,9},{9,8},{10,11... | collective-permute-start | bytes 417800 | tf_op jit(solution)/shard_map/ppermute | solution.py:27
  10.7 0.7 %copy-start.6 = (f32[256]{0:T(256)S(1)}, f32[256]{0:T(256)}, u32[]{:S(2)}) copy-start(f32[256]{0:T(256)} %param.15) | copy-start | bytes 3076
  10.7 0.7 %copy-start.4 = (s32[2,8,9]{2,1,0:T(8,128)S(1)}, s32[2,8,9]{2,1,0:T(8,128)}, u32[]{:S(2)}) copy-start(s32[2,8,9]{2,1,0:T(8,128)} %links.9) | copy-start | bytes 1732
  10.8 0.7 %copy-start.5 = (f32[256]{0:T(256)S(1)}, f32[256]{0:T(256)}, u32[]{:S(2)}) copy-start(f32[256]{0:T(256)} %param.13) | copy-start | bytes 3076
  15.3 3.8 %copy-start.2 = (bf16[256,256]{1,0:T(8,128)(2,1)S(1)}, bf16[256,256]{1,0:T(8,128)(2,1)}, u32[]{:S(2)}) copy-start(bf16[256,256]{1,0:T(8,128)(2,1)} %w_one_in.3) | copy-start | bytes 393220
  15.3 3.8 %copy-start.3 = (bf16[256,256]{1,0:T(8,128)(2,1)S(1)}, bf16[256,256]{1,0:T(8,128)(2,1)}, u32[]{:S(2)}) copy-start(bf16[256,256]{1,0:T(8,128)(2,1)} %w_two_in.3) | copy-start | bytes 393220
  15.3 3.8 %collective-permute-start.5 = (bf16[320,256]{1,0:T(8,128)(2,1)S(1)}, bf16[320,256]{1,0:T(8,128)(2,1)S(1)}, u32[]{:S(2)}, u32[]{:S(2)}) collective-permute-start(bf16[320,256]{1,0:T(8,128)(2,1)S(1)} %get-tuple-element.40), channel_id=1, source_target_pairs={{0,4},{4,0},{8,12},{12,8},{16,20},{20,16},{24,28},{28,24},{1,5},{5... | collective-permute-start | bytes 491528 | tf_op jit(solution)/shard_map/ppermute | solution.py:27
  15.4 8.9 %collective-permute-start.4 = (bf16[320,256]{1,0:T(8,128)(2,1)S(1)}, bf16[320,256]{1,0:T(8,128)(2,1)S(1)}, u32[]{:S(2)}, u32[]{:S(2)}) collective-permute-start(bf16[320,256]{1,0:T(8,128)(2,1)S(1)} %get-tuple-element.34), channel_id=1, source_target_pairs={{4,8},{8,4},{12,16},{16,12},{20,24},{24,20},{28,0},{0,28},{5,9},{9... | collective-permute-start | bytes 491528 | tf_op jit(solution)/shard_map/ppermute | solution.py:27
  24.2 10.5 %collective-permute-start.6 = (f32[3,10,128]{2,1,0:T(8,128)S(1)}, f32[3,10,128]{2,1,0:T(8,128)S(1)}, u32[]{:S(2)}, u32[]{:S(2)}) collective-permute-start(f32[3,10,128]{2,1,0:T(8,128)S(1)} %get-tuple-element.47), channel_id=1, source_target_pairs={{0,4},{4,0},{8,12},{12,8},{16,20},{20,16},{24,28},{28,24},{1,5},{5... | collective-permute-start | bytes 46088 | tf_op jit(solution)/shard_map/ppermute | solution.py:27
  29.6 5.2 %collective-permute-start.7 = (f32[3,10,128]{2,1,0:T(8,128)S(1)}, f32[3,10,128]{2,1,0:T(8,128)S(1)}, u32[]{:S(2)}, u32[]{:S(2)}) collective-permute-start(f32[3,10,128]{2,1,0:T(8,128)S(1)} %get-tuple-element.48), channel_id=1, source_target_pairs={{4,8},{8,4},{12,16},{16,12},{20,24},{24,20},{28,0},{0,28},{5,9},{9... | collective-permute-start | bytes 46088 | tf_op jit(solution)/shard_map/ppermute | solution.py:27
  34.8 4.9 %collective-permute-start.8 = (f32[3,2,128]{2,1,0:T(2,128)S(1)}, f32[3,2,128]{2,1,0:T(2,128)S(1)}, u32[]{:S(2)}, u32[]{:S(2)}) collective-permute-start(f32[3,2,128]{2,1,0:T(2,128)S(1)} %get-tuple-element.65), channel_id=1, source_target_pairs={{0,1},{1,0},{2,3},{3,2},{4,5},{5,4},{6,7},{7,6},{8,9},{9,8},{10,11... | collective-permute-start | bytes 9224 | tf_op jit(solution)/shard_map/ppermute | solution.py:27
  36.3 4.5 %collective-permute-start.9 = (f32[3,2,128]{2,1,0:T(2,128)S(1)}, f32[3,2,128]{2,1,0:T(2,128)S(1)}, u32[]{:S(2)}, u32[]{:S(2)}) collective-permute-start(f32[3,2,128]{2,1,0:T(2,128)S(1)} %get-tuple-element.64), channel_id=1, source_target_pairs={{1,2},{2,1},{3,0},{0,3},{5,6},{6,5},{7,4},{4,7},{9,10},{10,9},{11,... | collective-permute-start | bytes 9224 | tf_op jit(solution)/shard_map/ppermute | solution.py:27

commit v5 on v4

--- a/solution.py
+++ b/solution.py
@@ -192,7 +192,7 @@
                         self.written.add((c, to, y + ky))
                         pushed[c, to, y + ky] = total
             for c in range(3):
-                sums[c, y * atoms + start : y * atoms + start + lines] = own[c]
+                sums[c, y * atoms + start : y * atoms + start + lines] = own[c].astype(bf16)
 
     def inside(self, y, rows):
         first, last = (1 if y == 0 else 0), (1 if y == self.rows_y - 1 else 2)
@@ -206,7 +206,8 @@
         return ((ghost, 0, 3),)
 
     def gathered(self, sums, c):
-        total = row_sums(sums[c])
+        ones = jnp.ones((8, self.atoms), bf16)
+        total = lax.dot_general(ones, sums[c], across, preferred_element_type=f32)[0:1]
         return [total[:, y * self.atoms : (y + 1) * self.atoms] for y in range(self.rows_y)]
 
     def unit(self, c):
@@ -282,11 +283,10 @@
     block.spread(upright)
 
     targets = [block.outside(y, lx, other, ghost) for y in range(rows_y)]
-    for y in range(rows_y):
-        block.weigh(group.at[y], lx, y, targets[y])
     block.wait()
     for first in range(0, rows_y, bins):
         for y in range(first, first + bins):
+            block.weigh(group.at[y], lx, y, targets[y])
             rows = slice(y * atoms, (y + 1) * atoms)
             features[rows] = (sums[rows] + block.describe(group.at[y], lx, y, targets[y])).astype(bf16)
         rows = slice(first * atoms, (first + bins) * atoms)
@@ -399,7 +399,7 @@
     params = pltpu.CompilerParams(vmem_limit_bytes=13 * 2**20)
     tab = pltpu.VMEM((4, 4, 24, atoms), f32)
     upright = pltpu.VMEM((atoms, atoms), f32)
-    own_sums = pltpu.VMEM((3, rows, atoms), f32)
+    own_sums = pltpu.VMEM((3, rows, atoms), bf16)
     pushed = pltpu.VMEM((3, 4, cols, 8, atoms), f32)
     sems = pltpu.SemaphoreType.DMA((16,))
     sums = jax.ShapeDtypeStruct((rows, width), f32)

time: 41.7 us -> 40.9 us (0.981)
  Pallas kernels: 20.6 us -> 19.3 us
    pallas_call x2, Pallas kernels: 10.3 us -> 9.55 us  [side(): pl.pallas_call(functools.partial(side_kernel, sizes, lx, other, ghost), o...]
    pallas_call x2, Pallas kernels: 6.66 us -> 6.13 us  [inner(): pl.pallas_call(functools.partial(last_kernel, sizes, lx), out_shape=(inne...]
  transfers between devices with their start and end apart: 10 -> 10, of which waited for: 2 -> 3; matrix products, arithmetic and copies ran while one was open for 1% -> 1% of each run, Pallas kernels for 49% -> 47%
where the time goes in v5:
time: 40.9 us; the launch traced here: 40.7 us
  Pallas kernels  19.3 us (47%)
  starting transfers between devices  15.8 us (39%)
  local copies, waits for them, and re-layouts  2.09 us (5%)
  waiting for transfers between devices  1.61 us (4%)
  other arithmetic  1.01 us (2%)
  between operations  0.91 us (2%)
    ppermute x10, starting transfers between devices, pair_exchange(): return lax.ppermute(value, axis, pairs)  15.8 us
    pallas_call x2, Pallas kernels, side(): pl.pallas_call(functools.partial(side_kernel, sizes, lx, other, ghost), o...  9.55 us
    pallas_call x2, Pallas kernels, inner(): pl.pallas_call(functools.partial(last_kernel, sizes, lx), out_shape=(inne...  6.13 us
    pallas_call x1, Pallas kernels, body(): pl.pallas_call(functools.partial(first_kernel, sizes), out_shape=(sums, s...  3.54 us
    ppermute x10, waiting for transfers between devices, pair_exchange(): return lax.ppermute(value, axis, pairs)  1.61 us
    dynamic_slice x1, local copies, waits for them, and re-layouts, body(): lax.dynamic_slice_in_dim(embed, odd_x, 1, 0)  1.16 us
  transfers between devices with their start and end apart: 10, of which 3 were waited for; matrix products, arithmetic and copies ran while one was open for 1% of the time, Pallas kernels for 47%

profile of v5, /device:TPU:0, one launch (start us, length us, event | category | flops | bytes accessed | tf_op | source)
XLA Modules:
  0.0 40.7 jit_solution(15032509063492198825)
XLA Ops:
  0.6 0.0 copy-start
  0.7 0.0 copy-start.7
  0.7 0.0 copy-start.1
  0.7 1.2 %constant_dynamic-slice_fusion.3 = bf16[1,8,128,256]{3,2,1,0:T(8,128)(2,1)S(1)} fusion(bf16[2,8,128,256]{3,2,1,0:T(8,128)(2,1)} %param.9, s32[]{:T(128)S(6)} %select_n.83), kind=kLoop, calls=%fused_computation.33 | loop fusion | bytes 1048580 | tf_op jit(solution)/shard_map/dynamic_slice | solution.py:371
  1.8 0.0 copy-done.7
  1.8 0.1 fusion.2
  1.9 0.0 copy-done.1
  2.0 0.0 copy-done
  2.1 0.5 %collective-permute-start.1 = (bf16[1,8,128,256]{3,2,1,0:T(8,128)(2,1)S(1)}, bf16[1,8,128,256]{3,2,1,0:T(8,128)(2,1)S(1)}, u32[]{:S(2)}, u32[]{:S(2)}) collective-permute-start(bf16[1,8,128,256]{3,2,1,0:T(8,128)(2,1)S(1)} %constant_dynamic-slice_fusion.2), channel_id=1, source_target_pairs={{0,4},{4,0},{8,12},{12,8},{16,20},{20,16},{24,28},{28,24},{1,5},{5... | collective-permute-start | bytes 1572872 | tf_op jit(solution)/shard_map/ppermute | solution.py:27
  2.6 4.7 %collective-permute-start = (bf16[1,8,128,256]{3,2,1,0:T(8,128)(2,1)S(1)}, bf16[1,8,128,256]{3,2,1,0:T(8,128)(2,1)S(1)}, u32[]{:S(2)}, u32[]{:S(2)}) collective-permute-start(bf16[1,8,128,256]{3,2,1,0:T(8,128)(2,1)S(1)} %constant_dynamic-slice_fusion.3), channel_id=1, source_target_pairs={{4,8},{8,4},{12,16},{16,12},{20,24},{24,20},{28,0},{0,28},{5,9},{9... | collective-permute-start | bytes 1572872 | tf_op jit(solution)/shard_map/ppermute | solution.py:27
  7.4 0.0 collective-permute-done.1
  7.5 2.5 %collective-permute-start.3 = (bf16[272,256]{1,0:T(8,128)(2,1)S(1)}, bf16[272,256]{1,0:T(8,128)(2,1)S(1)}, u32[]{:S(2)}, u32[]{:S(2)}) collective-permute-start(bf16[272,256]{1,0:T(8,128)(2,1)S(1)} %pad_maximum_fusion.1), channel_id=1, source_target_pairs={{1,2},{2,1},{3,0},{0,3},{5,6},{6,5},{7,4},{4,7},{9,10},{10,9},{11,... | collective-permute-start | bytes 417800 | tf_op jit(solution)/shard_map/ppermute | solution.py:27
  10.0 0.6 %collective-permute-start.2 = (bf16[272,256]{1,0:T(8,128)(2,1)S(1)}, bf16[272,256]{1,0:T(8,128)(2,1)S(1)}, u32[]{:S(2)}, u32[]{:S(2)}) collective-permute-start(bf16[272,256]{1,0:T(8,128)(2,1)S(1)} %pad_maximum_fusion), channel_id=1, source_target_pairs={{0,1},{1,0},{2,3},{3,2},{4,5},{5,4},{6,7},{7,6},{8,9},{9,8},{10,11... | collective-permute-start | bytes 417800 | tf_op jit(solution)/shard_map/ppermute | solution.py:27
  10.6 0.1 fusion.1.occupied
  10.7 0.0 copy-start.6
  10.7 0.0 copy-start.4
  10.7 0.1 pad_add_fusion.info
  10.8 0.0 copy-start.5
  10.8 0.6 %copy-done.6 = f32[256]{0:T(256)S(1)} copy-done((f32[256]{0:T(256)S(1)}, f32[256]{0:T(256)}, u32[]{:S(2)}) %copy-start.6) | copy-done | bytes 1048
  11.4 0.0 copy-done.4
  11.4 0.1 copy-done.5
  11.5 3.5 %shard_map.95 = (f32[1024,256]{1,0:T(8,128)S(1)}, f32[1024,256]{1,0:T(8,128)S(1)}, bf16[64,256]{1,0:T(8,128)(2,1)S(1)}, f32[2,256]{1,0:T(2,128)S(1)}) custom-call(s32[2]{0:T(128)S(1)} %pad_add_fusion.info, s32[2,8,9]{2,1,0:T(8,128)S(1)} %copy-done.4, f32[3,2,8,128]{3,2,1,0:T(8,128)S(1)} %copy-done.1, f32[2,8,128]{2,1,0:T(8,128)S(1)} %fusion.1.occupied, ...), custom_call_target="tpu_custom_call" | custom-call | tf_op jit(solution)/shard_map/pallas_call | solution.py:408
  15.0 0.0 collective-permute-done.3.col_b
  15.0 0.2 collective-permute-done.2.col_a
  15.3 0.0 copy-start.2
  15.3 0.0 copy-start.3
  15.3 0.1 collective-permute-start.5
  15.4 3.7 %collective-permute-start.4 = (bf16[320,256]{1,0:T(8,128)(2,1)S(1)}, bf16[320,256]{1,0:T(8,128)(2,1)S(1)}, u32[]{:S(2)}, u32[]{:S(2)}) collective-permute-start(bf16[320,256]{1,0:T(8,128)(2,1)S(1)} %get-tuple-element.34), channel_id=1, source_target_pairs={{4,8},{8,4},{12,16},{16,12},{20,24},{24,20},{28,0},{0,28},{5,9},{9... | collective-permute-start | bytes 491528 | tf_op jit(solution)/shard_map/ppermute | solution.py:27
  19.1 0.0 collective-permute-done.5.corner
  19.1 0.0 copy-done.2
  19.1 0.0 copy-done.3
  19.1 4.9 %shard_map.98 = (f32[3,10,128]{2,1,0:T(8,128)S(1)}, f32[3,4,128]{2,1,0:T(4,128)S(1)}, f32[3,8,128]{2,1,0:T(8,128)S(1)}, bf16[1024,256]{1,0:T(8,128)(2,1)S(1)}, f32[8,128]{1,0:T(8,128)S(1)}) custom-call(s32[2]{0:T(128)S(1)} %pad_add_fusion.info, s32[2,8,9]{2,1,0:T(8,128)S(1)} %copy-done.4, f32[3,2,8,128]{3,2,1,0:T(8,128)S(1)} %copy-done.1, ...), custom_call_target="tpu_custom_call" | custom-call | tf_op jit(solution)/shard_map/pallas_call | solution.py:427
  24.0 0.1 collective-permute-start.6
  24.1 0.0 collective-permute-done
  24.1 0.0 collective-permute-done.4.corner
  24.1 4.7 %shard_map.97 = (f32[3,10,128]{2,1,0:T(8,128)S(1)}, f32[3,4,128]{2,1,0:T(4,128)S(1)}, f32[3,8,128]{2,1,0:T(8,128)S(1)}, bf16[1024,256]{1,0:T(8,128)(2,1)S(1)}, f32[8,128]{1,0:T(8,128)S(1)}) custom-call(s32[2]{0:T(128)S(1)} %pad_add_fusion.info, s32[2,8,9]{2,1,0:T(8,128)S(1)} %copy-done.4, f32[3,2,8,128]{3,2,1,0:T(8,128)S(1)} %copy-done.1, ...), custom_call_target="tpu_custom_call" | custom-call | tf_op jit(solution)/shard_map/pallas_call | solution.py:427
  28.8 1.6 %collective-permute-start.7 = (f32[3,10,128]{2,1,0:T(8,128)S(1)}, f32[3,10,128]{2,1,0:T(8,128)S(1)}, u32[]{:S(2)}, u32[]{:S(2)}) collective-permute-start(f32[3,10,128]{2,1,0:T(8,128)S(1)} %get-tuple-element.48), channel_id=1, source_target_pairs={{4,8},{8,4},{12,16},{16,12},{20,24},{24,20},{28,0},{0,28},{5,9},{9... | collective-permute-start | bytes 46088 | tf_op jit(solution)/shard_map/ppermute | solution.py:27
  30.3 3.4 %shard_map.99 = (f32[3,2,8,128]{3,2,1,0:T(8,128)S(1)}, f32[3,4,128]{2,1,0:T(4,128)S(1)}) custom-call(s32[2]{0:T(128)S(1)} %pad_add_fusion.info, s32[2,8,9]{2,1,0:T(8,128)S(1)} %copy-done.4, f32[3,2,8,128]{3,2,1,0:T(8,128)S(1)} %copy-done.1, f32[2,8,128]{2,1,0:T(8,128)S(1)} %fusion.1.occupied, bf16[2,1024,256]{2,1,0:T(8,128)(2,1)S(1)} %bitcast.38, ...), custom_call_target="tpu_custom_call" | custom-call | tf_op jit(solution)/shard_map/pallas_call | solution.py:455
  33.7 0.0 collective-permute-done.6.refs_1_
  33.7 0.1 collective-permute-done.7.refs_2_
  33.9 1.6 %collective-permute-start.8 = (f32[3,2,128]{2,1,0:T(2,128)S(1)}, f32[3,2,128]{2,1,0:T(2,128)S(1)}, u32[]{:S(2)}, u32[]{:S(2)}) collective-permute-start(f32[3,2,128]{2,1,0:T(2,128)S(1)} %get-tuple-element.65), channel_id=1, source_target_pairs={{0,1},{1,0},{2,3},{3,2},{4,5},{5,4},{6,7},{7,6},{8,9},{9,8},{10,11... | collective-permute-start | bytes 9224 | tf_op jit(solution)/shard_map/ppermute | solution.py:27
  35.5 0.5 %collective-permute-start.9 = (f32[3,2,128]{2,1,0:T(2,128)S(1)}, f32[3,2,128]{2,1,0:T(2,128)S(1)}, u32[]{:S(2)}, u32[]{:S(2)}) collective-permute-start(f32[3,2,128]{2,1,0:T(2,128)S(1)} %get-tuple-element.64), channel_id=1, source_target_pairs={{1,2},{2,1},{3,0},{0,3},{5,6},{6,5},{7,4},{4,7},{9,10},{10,9},{11,... | collective-permute-start | bytes 9224 | tf_op jit(solution)/shard_map/ppermute | solution.py:27
  35.9 2.8 %shard_map.100 = (f32[3,2,8,128]{3,2,1,0:T(8,128)S(1)}, f32[2,8,128]{2,1,0:T(8,128)}) custom-call(s32[2]{0:T(128)S(1)} %pad_add_fusion.info, s32[2,8,9]{2,1,0:T(8,128)S(1)} %copy-done.4, f32[3,2,8,128]{3,2,1,0:T(8,128)S(1)} %copy-done.1, f32[2,8,128]{2,1,0:T(8,128)S(1)} %fusion.1.occupied, bf16[2,1024,256]{2,1,0:T(8,128)(2,1)S(1)} %bitcast.39, ...), custom_call_target="tpu_custom_call" | custom-call | tf_op jit(solution)/shard_map/pallas_call | solution.py:455
  38.7 0.0 collective-permute-done.8
  38.7 1.2 %collective-permute-done.9 = f32[3,2,128]{2,1,0:T(2,128)S(1)} collective-permute-done((f32[3,2,128]{2,1,0:T(2,128)S(1)}, f32[3,2,128]{2,1,0:T(2,128)S(1)}, u32[]{:S(2)}, u32[]{:S(2)}) %collective-permute-start.9) | collective-permute-done | bytes 3104 | tf_op jit(solution)/shard_map/ppermute | solution.py:27
  40.0 0.7 %select_add_fusion = f32[3,2,8,128]{3,2,1,0:T(8,128)} fusion(f32[3,2,8,128]{3,2,1,0:T(8,128)S(1)} %get-tuple-element.51, f32[3,2,128]{2,1,0:T(2,128)S(1)} %get-tuple-element.63, f32[3,2,128]{2,1,0:T(2,128)S(1)} %get-tuple-element.62, pred[8]{0:T(512)(128)(4,1)S(1)} %get-tuple-element.68, pred[8]{0:T(512)(128)(4,1)S(1)} %get-tuple-element.69), kind=kLoop, calls=%fused_computation.11 | loop fusion | flops 24576 | bytes 55312 | tf_op jit(solution)/shard_map/add | solution.py:476
  (22 shorter events, 0.3 us)
Async XLA Ops:
  0.6 1.4 %copy-start = (bf16[2,8,128,256]{3,2,1,0:T(8,128)(2,1)S(1)}, bf16[2,8,128,256]{3,2,1,0:T(8,128)(2,1)}, u32[]{:S(2)}) copy-start(bf16[2,8,128,256]{3,2,1,0:T(8,128)(2,1)} %param.9) | copy-start | bytes 3145732
  0.7 1.2 %copy-start.7 = (s32[2,8]{1,0:T(2,128)S(1)}, s32[2,8]{1,0:T(2,128)}, u32[]{:S(2)}) copy-start(s32[2,8]{1,0:T(2,128)} %param.10) | copy-start | bytes 196
  0.7 1.3 %copy-start.1 = (f32[3,2,8,128]{3,2,1,0:T(8,128)S(1)}, f32[3,2,8,128]{3,2,1,0:T(8,128)}, u32[]{:S(2)}) copy-start(f32[3,2,8,128]{3,2,1,0:T(8,128)} %positions.4) | copy-start | bytes 73732
  2.1 5.4 %collective-permute-start.1 = (bf16[1,8,128,256]{3,2,1,0:T(8,128)(2,1)S(1)}, bf16[1,8,128,256]{3,2,1,0:T(8,128)(2,1)S(1)}, u32[]{:S(2)}, u32[]{:S(2)}) collective-permute-start(bf16[1,8,128,256]{3,2,1,0:T(8,128)(2,1)S(1)} %constant_dynamic-slice_fusion.2), channel_id=1, source_target_pairs={{0,4},{4,0},{8,12},{12,8},{16,20},{20,16},{24,28},{28,24},{1,5},{5... | collective-permute-start | bytes 1572872 | tf_op jit(solution)/shard_map/ppermute | solution.py:27
  2.6 21.5 %collective-permute-start = (bf16[1,8,128,256]{3,2,1,0:T(8,128)(2,1)S(1)}, bf16[1,8,128,256]{3,2,1,0:T(8,128)(2,1)S(1)}, u32[]{:S(2)}, u32[]{:S(2)}) collective-permute-start(bf16[1,8,128,256]{3,2,1,0:T(8,128)(2,1)S(1)} %constant_dynamic-slice_fusion.3), channel_id=1, source_target_pairs={{4,8},{8,4},{12,16},{16,12},{20,24},{24,20},{28,0},{0,28},{5,9},{9... | collective-permute-start | bytes 1572872 | tf_op jit(solution)/shard_map/ppermute | solution.py:27
  7.5 7.5 %collective-permute-start.3 = (bf16[272,256]{1,0:T(8,128)(2,1)S(1)}, bf16[272,256]{1,0:T(8,128)(2,1)S(1)}, u32[]{:S(2)}, u32[]{:S(2)}) collective-permute-start(bf16[272,256]{1,0:T(8,128)(2,1)S(1)} %pad_maximum_fusion.1), channel_id=1, source_target_pairs={{1,2},{2,1},{3,0},{0,3},{5,6},{6,5},{7,4},{4,7},{9,10},{10,9},{11,... | collective-permute-start | bytes 417800 | tf_op jit(solution)/shard_map/ppermute | solution.py:27
  10.0 5.2 %collective-permute-start.2 = (bf16[272,256]{1,0:T(8,128)(2,1)S(1)}, bf16[272,256]{1,0:T(8,128)(2,1)S(1)}, u32[]{:S(2)}, u32[]{:S(2)}) collective-permute-start(bf16[272,256]{1,0:T(8,128)(2,1)S(1)} %pad_maximum_fusion), channel_id=1, source_target_pairs={{0,1},{1,0},{2,3},{3,2},{4,5},{5,4},{6,7},{7,6},{8,9},{9,8},{10,11... | collective-permute-start | bytes 417800 | tf_op jit(solution)/shard_map/ppermute | solution.py:27
  10.7 0.7 %copy-start.6 = (f32[256]{0:T(256)S(1)}, f32[256]{0:T(256)}, u32[]{:S(2)}) copy-start(f32[256]{0:T(256)} %param.15) | copy-start | bytes 3076
  10.7 0.7 %copy-start.4 = (s32[2,8,9]{2,1,0:T(8,128)S(1)}, s32[2,8,9]{2,1,0:T(8,128)}, u32[]{:S(2)}) copy-start(s32[2,8,9]{2,1,0:T(8,128)} %links.9) | copy-start | bytes 1732
  10.8 0.7 %copy-start.5 = (f32[256]{0:T(256)S(1)}, f32[256]{0:T(256)}, u32[]{:S(2)}) copy-start(f32[256]{0:T(256)} %param.13) | copy-start | bytes 3076
  15.3 3.8 %copy-start.2 = (bf16[256,256]{1,0:T(8,128)(2,1)S(1)}, bf16[256,256]{1,0:T(8,128)(2,1)}, u32[]{:S(2)}) copy-start(bf16[256,256]{1,0:T(8,128)(2,1)} %w_one_in.3) | copy-start | bytes 393220
  15.3 3.8 %copy-start.3 = (bf16[256,256]{1,0:T(8,128)(2,1)S(1)}, bf16[256,256]{1,0:T(8,128)(2,1)}, u32[]{:S(2)}) copy-start(bf16[256,256]{1,0:T(8,128)(2,1)} %w_two_in.3) | copy-start | bytes 393220
  15.3 3.8 %collective-permute-start.5 = (bf16[320,256]{1,0:T(8,128)(2,1)S(1)}, bf16[320,256]{1,0:T(8,128)(2,1)S(1)}, u32[]{:S(2)}, u32[]{:S(2)}) collective-permute-start(bf16[320,256]{1,0:T(8,128)(2,1)S(1)} %get-tuple-element.40), channel_id=1, source_target_pairs={{0,4},{4,0},{8,12},{12,8},{16,20},{20,16},{24,28},{28,24},{1,5},{5... | collective-permute-start | bytes 491528 | tf_op jit(solution)/shard_map/ppermute | solution.py:27
  15.4 8.7 %collective-permute-start.4 = (bf16[320,256]{1,0:T(8,128)(2,1)S(1)}, bf16[320,256]{1,0:T(8,128)(2,1)S(1)}, u32[]{:S(2)}, u32[]{:S(2)}) collective-permute-start(bf16[320,256]{1,0:T(8,128)(2,1)S(1)} %get-tuple-element.34), channel_id=1, source_target_pairs={{4,8},{8,4},{12,16},{16,12},{20,24},{24,20},{28,0},{0,28},{5,9},{9... | collective-permute-start | bytes 491528 | tf_op jit(solution)/shard_map/ppermute | solution.py:27
  24.0 9.8 %collective-permute-start.6 = (f32[3,10,128]{2,1,0:T(8,128)S(1)}, f32[3,10,128]{2,1,0:T(8,128)S(1)}, u32[]{:S(2)}, u32[]{:S(2)}) collective-permute-start(f32[3,10,128]{2,1,0:T(8,128)S(1)} %get-tuple-element.47), channel_id=1, source_target_pairs={{0,4},{4,0},{8,12},{12,8},{16,20},{20,16},{24,28},{28,24},{1,5},{5... | collective-permute-start | bytes 46088 | tf_op jit(solution)/shard_map/ppermute | solution.py:27
  28.8 5.1 %collective-permute-start.7 = (f32[3,10,128]{2,1,0:T(8,128)S(1)}, f32[3,10,128]{2,1,0:T(8,128)S(1)}, u32[]{:S(2)}, u32[]{:S(2)}) collective-permute-start(f32[3,10,128]{2,1,0:T(8,128)S(1)} %get-tuple-element.48), channel_id=1, source_target_pairs={{4,8},{8,4},{12,16},{16,12},{20,24},{24,20},{28,0},{0,28},{5,9},{9... | collective-permute-start | bytes 46088 | tf_op jit(solution)/shard_map/ppermute | solution.py:27
  33.9 4.8 %collective-permute-start.8 = (f32[3,2,128]{2,1,0:T(2,128)S(1)}, f32[3,2,128]{2,1,0:T(2,128)S(1)}, u32[]{:S(2)}, u32[]{:S(2)}) collective-permute-start(f32[3,2,128]{2,1,0:T(2,128)S(1)} %get-tuple-element.65), channel_id=1, source_target_pairs={{0,1},{1,0},{2,3},{3,2},{4,5},{5,4},{6,7},{7,6},{8,9},{9,8},{10,11... | collective-permute-start | bytes 9224 | tf_op jit(solution)/shard_map/ppermute | solution.py:27
  35.5 4.5 %collective-permute-start.9 = (f32[3,2,128]{2,1,0:T(2,128)S(1)}, f32[3,2,128]{2,1,0:T(2,128)S(1)}, u32[]{:S(2)}, u32[]{:S(2)}) collective-permute-start(f32[3,2,128]{2,1,0:T(2,128)S(1)} %get-tuple-element.64), channel_id=1, source_target_pairs={{1,2},{2,1},{3,0},{0,3},{5,6},{6,5},{7,4},{4,7},{9,10},{10,9},{11,... | collective-permute-start | bytes 9224 | tf_op jit(solution)/shard_map/ppermute | solution.py:27
